TPU v7x, 256 devices: a whole 4x4x8 slice. The times are simulated.
256 devices in a mesh: gx: 4 (over y), gy: 8 (over z_hi, core), gz: 8 (over z_lo, x).
Axes of the slice: x: 4, y: 4, z: 8 (z_hi: 4, z_lo: 2; z = z_hi * 2 + z_lo), core: 2. Of those that a mesh axis runs over, the one named last changes fastest.
Arguments:
- density: float32 [16, 128, 2048], P('gx', 'gy', 'gz'), may hold values from 2 to 8
- energy: float32 [16, 128, 2048], P('gx', 'gy', 'gz'), may hold values from 0.2 to 1.5
- velocity: float32 [3, 16, 128, 2048], P(None, 'gx', 'gy', 'gz'), may hold values from -3 to 3
- plastic_strain: float32 [16, 128, 2048], P('gx', 'gy', 'gz'), may hold values from 0.01 to 0.5
- damage: float32 [16, 128, 2048], P('gx', 'gy', 'gz'), may hold values from 0 to 0.5
- deviator: float32 [6, 16, 128, 2048], P(None, 'gx', 'gy', 'gz'), may hold values from -1.2 to 1.2
- materials: int32 [16, 128, 2048], P('gx', 'gy', 'gz'), may hold values from 0 to 2
- timestep: float32 [2], replicated, may hold values from 0.05 to 0.3
Outputs:
- density_out: float32 [16, 128, 2048], P('gx', 'gy', 'gz')
- energy_out: float32 [16, 128, 2048], P('gx', 'gy', 'gz')
- velocity_out: float32 [3, 16, 128, 2048], P(None, 'gx', 'gy', 'gz')
- plastic_out: float32 [16, 128, 2048], P('gx', 'gy', 'gz')
- damage_out: float32 [16, 128, 2048], P('gx', 'gy', 'gz')
- deviator_out: float32 [6, 16, 128, 2048], P(None, 'gx', 'gy', 'gz')
All inputs are finite; a program needn't handle non-finite values. Where the computation divides by a largest or mean magnitude, that divisor is 1e-20 or more.
Results may differ from a plain program's by a relative error of at most 0.0003.
Values sent between devices are 32-bit elements; how exact they have to be, the bound alone decides.
No kernel may reach another device: no remote copies, remote signals or barrier semaphores. Data moves between devices by JAX's collectives and lax.ppermute only.
A program may use at most 128 MiB of HBM per device.

v0:
```python
import jax
import jax.numpy as jnp
from jax import lax
from jax.sharding import PartitionSpec as P

STEPS = 2


shear_table = (1.0, 0.5, 0.8)
sound_table = (1.5, 1.2, 1.0)
gruneisen_table = (2.0, 2.1, 1.9)
rest_table = (4.0, 3.0, 5.0)
yield_table = (0.3, 0.2, 0.25)
harden_table = (0.5, 0.3, 0.4)
exponent_table = (0.3, 0.4, 0.35)
rate_table = (0.02, 0.015, 0.01)
cfl_number = 0.2


def with_halo(block, sides, width):
    for axis, dim in sides:
        count = lax.axis_size(axis)
        forward = [(i, i + 1) for i in range(count - 1)]
        backward = [(target, source) for source, target in forward]
        low = lax.ppermute(
            lax.slice_in_dim(block, block.shape[dim] - width, None, axis=dim), axis, forward
        )
        high = lax.ppermute(lax.slice_in_dim(block, 0, width, axis=dim), axis, backward)
        block = jnp.concatenate([low, block, high], axis=dim)
    return block


def lookup(kind_values, values_table):
    result = jnp.zeros(kind_values.shape, jnp.float32)
    for material_no in range(3):
        result = result + jnp.where(kind_values == material_no, values_table[material_no], 0.0)
    return result


def material_params(kind_values):
    return (
        lookup(kind_values, shear_table),
        lookup(kind_values, yield_table),
        lookup(kind_values, harden_table),
        lookup(kind_values, exponent_table),
        lookup(kind_values, rate_table),
    )


def central(padded, direction):
    upper_cut = [slice(1, -1)] * 3
    lower_cut = [slice(1, -1)] * 3
    upper_cut[direction] = slice(2, None)
    lower_cut[direction] = slice(None, -2)
    return 0.5 * (padded[tuple(upper_cut)] - padded[tuple(lower_cut)])


def stress_update(vel_padded, deviator, plastic, damage, pressure, params, time_step):
    shear_mod, yield_base, harden_mod, harden_exp, rate_coef = params
    gradient = [[central(vel_padded[comp_a], comp_b) for comp_b in range(3)] for comp_a in range(3)]
    diverge = gradient[0][0] + gradient[1][1] + gradient[2][2]
    third_div = diverge / 3.0
    strain = [
        gradient[0][0] - third_div,
        gradient[1][1] - third_div,
        gradient[2][2] - third_div,
        0.5 * (gradient[0][1] + gradient[1][0]),
        0.5 * (gradient[1][2] + gradient[2][1]),
        0.5 * (gradient[0][2] + gradient[2][0]),
    ]
    trial_dev = [
        deviator[comp_k] + 2.0 * shear_mod * time_step * strain[comp_k] for comp_k in range(6)
    ]
    trial_sq = (
        trial_dev[0] ** 2
        + trial_dev[1] ** 2
        + trial_dev[2] ** 2
        + 2.0 * (trial_dev[3] ** 2 + trial_dev[4] ** 2 + trial_dev[5] ** 2)
    )
    equivalent = jnp.sqrt(1.5 * trial_sq)
    strain_sq = (
        strain[0] ** 2
        + strain[1] ** 2
        + strain[2] ** 2
        + 2.0 * (strain[3] ** 2 + strain[4] ** 2 + strain[5] ** 2)
    )
    strain_rate = jnp.sqrt(strain_sq * (2.0 / 3.0))
    flow_stress = (
        (yield_base + harden_mod * jnp.exp(harden_exp * jnp.log(plastic)))
        * (1.0 + rate_coef * jnp.log1p(strain_rate))
        * (1.0 - damage)
    )
    bound_stress = jnp.maximum(equivalent, flow_stress)
    factor = flow_stress / bound_stress
    increment = (bound_stress - flow_stress) / (3.0 * shear_mod)
    triaxial = jnp.clip(-pressure / bound_stress, -1.5, 1.5)
    failure = 0.05 + 0.8 * jnp.exp(-1.5 * triaxial)
    new_plastic = plastic + increment
    new_damage = jnp.minimum(damage + increment / failure, 0.9)
    new_dev = [trial_dev[comp_k] * factor for comp_k in range(6)]
    stress = [
        new_dev[0] - pressure,
        new_dev[1] - pressure,
        new_dev[2] - pressure,
        new_dev[3],
        new_dev[4],
        new_dev[5],
    ]
    work_rate = (
        stress[0] * gradient[0][0]
        + stress[1] * gradient[1][1]
        + stress[2] * gradient[2][2]
        + 2.0 * (stress[3] * strain[3] + stress[4] * strain[4] + stress[5] * strain[5])
    )
    return (jnp.stack(stress), jnp.stack(new_dev), new_plastic, new_damage, work_rate)


def finish(stress_padded, density, energy, velocity, work_rate, time_step):
    force_x = (
        central(stress_padded[0], 0) + central(stress_padded[3], 1) + central(stress_padded[5], 2)
    )
    force_y = (
        central(stress_padded[3], 0) + central(stress_padded[1], 1) + central(stress_padded[4], 2)
    )
    force_z = (
        central(stress_padded[5], 0) + central(stress_padded[4], 1) + central(stress_padded[2], 2)
    )
    new_velocity = velocity + time_step * jnp.stack([force_x, force_y, force_z]) / density
    new_energy = energy + time_step * work_rate / density
    return (new_velocity, new_energy)


def sweep(padded, sweep_axis, time_step, lower_wall, upper_wall):
    array_dim = sweep_axis + 1
    length = padded.shape[array_dim] - 4

    def cut_along(source, offset, extent):
        return lax.slice_in_dim(source, offset, offset + extent, axis=array_dim)

    density = padded[0:1]
    conserved = jnp.concatenate([density, density * padded[1:]], axis=0)
    differ = cut_along(conserved, 1, length + 3) - cut_along(conserved, 0, length + 3)
    back_diff = cut_along(differ, 0, length + 2)
    fore_diff = cut_along(differ, 1, length + 2)
    product = back_diff * fore_diff
    positive = product > 0.0
    slopes = jnp.where(
        positive, 2.0 * product / (back_diff + fore_diff + jnp.where(positive, 0.0, 1.0)), 0.0
    )
    vel_row = padded[2 + sweep_axis : 3 + sweep_axis]
    face_speed = 0.5 * (cut_along(vel_row, 1, length + 1) + cut_along(vel_row, 2, length + 1))
    courant = time_step * face_speed
    left_flux = face_speed * (
        cut_along(conserved, 1, length + 1)
        + 0.5 * (1.0 - courant) * cut_along(slopes, 0, length + 1)
    )
    right_flux = face_speed * (
        cut_along(conserved, 2, length + 1)
        - 0.5 * (1.0 + courant) * cut_along(slopes, 1, length + 1)
    )
    face_flux = jnp.where(face_speed > 0.0, left_flux, right_flux)
    dims_shape = [1, 1, 1, 1]
    dims_shape[array_dim] = length + 1
    face_index = jnp.arange(length + 1, dtype=jnp.int32).reshape(dims_shape)
    closed = (face_index == 0) & lower_wall | (face_index == length) & upper_wall
    face_flux = jnp.where(closed, 0.0, face_flux)
    return cut_along(conserved, 2, length) - time_step * (
        cut_along(face_flux, 1, length) - cut_along(face_flux, 0, length)
    )


def to_primitive(updated):
    density = updated[0:1]
    safe_density = jnp.where(True, density, 1.0)
    return jnp.where(True, jnp.concatenate([density, updated[1:] / safe_density], axis=0), 0.0)


def shards(density, energy, velocity, plastic_strain, damage, deviator, materials, timestep):
    place_x = lax.axis_index("gx")
    place_y = lax.axis_index("gy")
    place_z = lax.axis_index("gz")
    groups_x = lax.axis_size("gx")
    groups_y = lax.axis_size("gy")
    groups_z = lax.axis_size("gz")
    kind_float = materials.astype(jnp.float32)
    sound_speed = lookup(kind_float, sound_table)
    gruneisen = lookup(kind_float, gruneisen_table)
    rest_density = lookup(kind_float, rest_table)
    params = material_params(kind_float)
    for step_no in range(STEPS):
        local_speed = jnp.max(jnp.max(jnp.abs(velocity), axis=0) + sound_speed)
        top_speed = lax.pmax(local_speed, ("gx", "gy", "gz"))
        time_step = timestep[step_no] / (1.0 + timestep[step_no] * top_speed / cfl_number)
        pressure = (
            sound_speed * sound_speed * (density - rest_density) + gruneisen * density * energy
        )
        vel_padded = with_halo(velocity, (("gx", 1), ("gy", 2), ("gz", 3)), 1)
        stress, deviator, plastic_strain, damage, work_rate = stress_update(
            vel_padded, deviator, plastic_strain, damage, pressure, params, time_step
        )
        stress_padded = with_halo(stress, (("gx", 1), ("gy", 2), ("gz", 3)), 1)
        velocity, energy = finish(stress_padded, density, energy, velocity, work_rate, time_step)
        primitive = jnp.concatenate(
            [density[None], energy[None], velocity, plastic_strain[None], damage[None], deviator],
            axis=0,
        )
        padded = with_halo(primitive, (("gx", 1),), 2)
        primitive = to_primitive(sweep(padded, 0, time_step, place_x == 0, place_x == groups_x - 1))
        padded = with_halo(primitive, (("gy", 2),), 2)
        primitive = to_primitive(sweep(padded, 1, time_step, place_y == 0, place_y == groups_y - 1))
        padded = with_halo(primitive, (("gz", 3),), 2)
        primitive = to_primitive(sweep(padded, 2, time_step, place_z == 0, place_z == groups_z - 1))
        density = primitive[0]
        energy = primitive[1]
        velocity = primitive[2:5]
        plastic_strain = primitive[5]
        damage = primitive[6]
        deviator = primitive[7:13]
    return (density, energy, velocity, plastic_strain, damage, deviator)


def solution(mesh):
    placed = (
        P("gx", "gy", "gz"),
        P("gx", "gy", "gz"),
        P(None, "gx", "gy", "gz"),
        P("gx", "gy", "gz"),
        P("gx", "gy", "gz"),
        P(None, "gx", "gy", "gz"),
        P("gx", "gy", "gz"),
        P(),
    )
    return jax.shard_map(
        shards,
        mesh=mesh,
        in_specs=placed,
        out_specs=(
            P("gx", "gy", "gz"),
            P("gx", "gy", "gz"),
            P(None, "gx", "gy", "gz"),
            P("gx", "gy", "gz"),
            P("gx", "gy", "gz"),
            P(None, "gx", "gy", "gz"),
        ),
        check_vma=False,
    )
```

profile of v0, /device:TPU:1, one launch (start us, length us, event | category | flops | bytes accessed | tf_op | source)
XLA Modules:
  0.0 383.4 jit_solution(7909201427468726576)
XLA Ops:
  1.5 4.0 %collective-permute-start = (f32[3,1,16,256]{3,2,1,0:T(8,128)S(1)}, f32[3,1,16,256]{3,2,1,0:T(8,128)S(1)}, u32[]{:S(2)}, u32[]{:S(2)}) collective-permute-start(f32[3,1,16,256]{3,2,1,0:T(8,128)S(1)} %get-tuple-element.134), channel_id=1, source_target_pairs={{0,64},{64,128},{128,192},{1,65},{65,129},{129,193},{2,66},{66,130... | collective-permute-start | bytes 147464 | tf_op jit(solution)/shard_map/ppermute | solution.py:25
  10.4 6.9 %collective-permute-start.2 = (f32[3,6,1,256]{3,2,1,0:T(1,128)S(1)}, f32[3,6,1,256]{3,2,1,0:T(1,128)S(1)}, u32[]{:S(2)}, u32[]{:S(2)}) collective-permute-start(f32[3,6,1,256]{3,2,1,0:T(1,128)S(1)} %get-tuple-element.121), channel_id=1, source_target_pairs={{0,8},{8,16},{16,24},{24,32},{32,40},{40,48},{48,56},{1,9},{9,17},... | collective-permute-start | bytes 55304 | tf_op jit(solution)/shard_map/ppermute | solution.py:25
  23.5 3.1 collective-permute-start.4
  28.6 80.6 %pmax.14 = f32[]{:T(128)} all-reduce(f32[]{:T(128)} %get-tuple-element.52), channel_id=1, replica_groups=mesh['gx'=4,'gy'=8,'gz'=8] {'gx','gy','gz'}, use_global_device_ids=true, to_apply=%region_2.3 | all-reduce | flops 1 | bytes 8 | tf_op jit(solution)/shard_map/pmax | solution.py:192
  115.9 3.7 collective-permute-done.7
  119.7 3.8 collective-permute-start.8
  125.4 4.2 %collective-permute-done.9 = f32[6,6,1,256]{3,2,1,0:T(1,128)S(1)} collective-permute-done((f32[6,6,1,256]{3,2,1,0:T(1,128)S(1)}, f32[6,6,1,256]{3,2,1,0:T(1,128)S(1)}, u32[]{:S(2)}, u32[]{:S(2)}) %collective-permute-start.9) | collective-permute-done | bytes 36896 | tf_op jit(solution)/shard_map/ppermute | solution.py:28
  133.7 6.0 %collective-permute-done.10 = f32[6,6,18,1]{3,2,1,0:T(8,128)S(1)} collective-permute-done((f32[6,6,18,1]{3,2,1,0:T(8,128)S(1)}, f32[6,6,18,1]{3,2,1,0:T(8,128)S(1)}, u32[]{:S(2)}, u32[]{:S(2)}) %collective-permute-start.10) | collective-permute-done | bytes 2624 | tf_op jit(solution)/shard_map/ppermute | solution.py:25
  139.8 4.1 %collective-permute-done.11 = f32[6,6,18,1]{3,2,1,0:T(8,128)S(1)} collective-permute-done((f32[6,6,18,1]{3,2,1,0:T(8,128)S(1)}, f32[6,6,18,1]{3,2,1,0:T(8,128)S(1)}, u32[]{:S(2)}, u32[]{:S(2)}) %collective-permute-start.11) | collective-permute-done | bytes 2624 | tf_op jit(solution)/shard_map/ppermute | solution.py:28
  150.2 7.0 %collective-permute-done.12 = f32[13,2,16,256]{3,2,1,0:T(8,128)S(1)} collective-permute-done((f32[13,2,16,256]{3,2,1,0:T(8,128)S(1)}, f32[13,2,16,256]{3,2,1,0:T(8,128)S(1)}, u32[]{:S(2)}, u32[]{:S(2)}) %collective-permute-start.12) | collective-permute-done | bytes 426016 | tf_op jit(solution)/shard_map/ppermute | solution.py:25
  157.3 4.1 %collective-permute-done.13 = f32[13,2,16,256]{3,2,1,0:T(8,128)S(1)} collective-permute-done((f32[13,2,16,256]{3,2,1,0:T(8,128)S(1)}, f32[13,2,16,256]{3,2,1,0:T(8,128)S(1)}, u32[]{:S(2)}, u32[]{:S(2)}) %collective-permute-start.13) | collective-permute-done | bytes 426016 | tf_op jit(solution)/shard_map/ppermute | solution.py:28
  167.4 4.9 %collective-permute-done.15 = f32[13,4,2,256]{3,2,1,0:T(2,128)S(1)} collective-permute-done((f32[13,4,2,256]{3,2,1,0:T(2,128)S(1)}, f32[13,4,2,256]{3,2,1,0:T(2,128)S(1)}, u32[]{:S(2)}, u32[]{:S(2)}) %collective-permute-start.15) | collective-permute-done | bytes 106528 | tf_op jit(solution)/shard_map/ppermute | solution.py:28
  178.8 4.9 %collective-permute-done.16 = f32[13,4,16,2]{3,2,1,0:T(8,128)S(1)} collective-permute-done((f32[13,4,16,2]{3,2,1,0:T(8,128)S(1)}, f32[13,4,16,2]{3,2,1,0:T(8,128)S(1)}, u32[]{:S(2)}, u32[]{:S(2)}) %collective-permute-start.16) | collective-permute-done | bytes 6688 | tf_op jit(solution)/shard_map/ppermute | solution.py:25
  183.7 4.7 %collective-permute-done.17 = f32[13,4,16,2]{3,2,1,0:T(8,128)S(1)} collective-permute-done((f32[13,4,16,2]{3,2,1,0:T(8,128)S(1)}, f32[13,4,16,2]{3,2,1,0:T(8,128)S(1)}, u32[]{:S(2)}, u32[]{:S(2)}) %collective-permute-start.17) | collective-permute-done | bytes 6688 | tf_op jit(solution)/shard_map/ppermute | solution.py:28
  191.8 3.2 collective-permute-start.18
  196.4 3.5 collective-permute-done.19
  199.9 4.1 %collective-permute-start.20 = (f32[3,6,1,256]{3,2,1,0:T(1,128)S(1)}, f32[3,6,1,256]{3,2,1,0:T(1,128)S(1)}, u32[]{:S(2)}, u32[]{:S(2)}) collective-permute-start(f32[3,6,1,256]{3,2,1,0:T(1,128)S(1)} %get-tuple-element.119), channel_id=1, source_target_pairs={{0,8},{8,16},{16,24},{24,32},{32,40},{40,48},{48,56},{1,9},{9,17},... | collective-permute-start | bytes 55304 | tf_op jit(solution)/shard_map/ppermute | solution.py:25
  205.9 4.3 %collective-permute-done.21 = f32[3,6,1,256]{3,2,1,0:T(1,128)S(1)} collective-permute-done((f32[3,6,1,256]{3,2,1,0:T(1,128)S(1)}, f32[3,6,1,256]{3,2,1,0:T(1,128)S(1)}, u32[]{:S(2)}, u32[]{:S(2)}) %collective-permute-start.21) | collective-permute-done | bytes 18464 | tf_op jit(solution)/shard_map/ppermute | solution.py:28
  210.4 6.6 %collective-permute-start.22 = (f32[3,6,18,1]{3,2,1,0:T(8,128)S(1)}, f32[3,6,18,1]{3,2,1,0:T(8,128)}, u32[]{:S(2)}, u32[]{:S(2)}) collective-permute-start(f32[3,6,18,1]{3,2,1,0:T(8,128)S(1)} %get-tuple-element.111), channel_id=1, source_target_pairs={{0,1},{1,2},{2,3},{3,4},{4,5},{5,6},{6,7},{8,9},{9,10},{10,11},{11... | collective-permute-start | bytes 3896 | tf_op jit(solution)/shard_map/ppermute | solution.py:25
  218.9 78.4 %pmax.15 = f32[]{:T(128)} all-reduce(f32[]{:T(128)} %add_reduce_fusion), channel_id=1, replica_groups=mesh['gx'=4,'gy'=8,'gz'=8] {'gx','gy','gz'}, use_global_device_ids=true, to_apply=%region_5.6 | all-reduce | flops 1 | bytes 8 | tf_op jit(solution)/shard_map/pmax | solution.py:192
  305.2 3.7 collective-permute-done.25
  309.0 4.6 %collective-permute-start.26 = (f32[6,6,1,256]{3,2,1,0:T(1,128)S(1)}, f32[6,6,1,256]{3,2,1,0:T(1,128)S(1)}, u32[]{:S(2)}, u32[]{:S(2)}) collective-permute-start(f32[6,6,1,256]{3,2,1,0:T(1,128)S(1)} %get-tuple-element.107), channel_id=1, source_target_pairs={{0,8},{8,16},{16,24},{24,32},{32,40},{40,48},{48,56},{1,9},{9,17},... | collective-permute-start | bytes 110600 | tf_op jit(solution)/shard_map/ppermute | solution.py:25
  315.6 4.2 %collective-permute-done.27 = f32[6,6,1,256]{3,2,1,0:T(1,128)S(1)} collective-permute-done((f32[6,6,1,256]{3,2,1,0:T(1,128)S(1)}, f32[6,6,1,256]{3,2,1,0:T(1,128)S(1)}, u32[]{:S(2)}, u32[]{:S(2)}) %collective-permute-start.27) | collective-permute-done | bytes 36896 | tf_op jit(solution)/shard_map/ppermute | solution.py:28
  322.9 6.0 %collective-permute-done.28 = f32[6,6,18,1]{3,2,1,0:T(8,128)S(1)} collective-permute-done((f32[6,6,18,1]{3,2,1,0:T(8,128)S(1)}, f32[6,6,18,1]{3,2,1,0:T(8,128)S(1)}, u32[]{:S(2)}, u32[]{:S(2)}) %collective-permute-start.28) | collective-permute-done | bytes 2624 | tf_op jit(solution)/shard_map/ppermute | solution.py:25
  328.9 4.1 %collective-permute-done.29 = f32[6,6,18,1]{3,2,1,0:T(8,128)S(1)} collective-permute-done((f32[6,6,18,1]{3,2,1,0:T(8,128)S(1)}, f32[6,6,18,1]{3,2,1,0:T(8,128)S(1)}, u32[]{:S(2)}, u32[]{:S(2)}) %collective-permute-start.29) | collective-permute-done | bytes 2624 | tf_op jit(solution)/shard_map/ppermute | solution.py:28
  334.7 3.7 collective-permute-start.30
  339.7 7.1 %collective-permute-done.30 = f32[13,2,16,256]{3,2,1,0:T(8,128)S(1)} collective-permute-done((f32[13,2,16,256]{3,2,1,0:T(8,128)S(1)}, f32[13,2,16,256]{3,2,1,0:T(8,128)S(1)}, u32[]{:S(2)}, u32[]{:S(2)}) %collective-permute-start.30) | collective-permute-done | bytes 426016 | tf_op jit(solution)/shard_map/ppermute | solution.py:25
  346.7 4.1 %collective-permute-done.31 = f32[13,2,16,256]{3,2,1,0:T(8,128)S(1)} collective-permute-done((f32[13,2,16,256]{3,2,1,0:T(8,128)S(1)}, f32[13,2,16,256]{3,2,1,0:T(8,128)S(1)}, u32[]{:S(2)}, u32[]{:S(2)}) %collective-permute-start.31) | collective-permute-done | bytes 426016 | tf_op jit(solution)/shard_map/ppermute | solution.py:28
  352.5 3.2 collective-permute-start.32
  357.9 4.8 %collective-permute-done.33 = f32[13,4,2,256]{3,2,1,0:T(2,128)S(1)} collective-permute-done((f32[13,4,2,256]{3,2,1,0:T(2,128)S(1)}, f32[13,4,2,256]{3,2,1,0:T(2,128)S(1)}, u32[]{:S(2)}, u32[]{:S(2)}) %collective-permute-start.33) | collective-permute-done | bytes 106528 | tf_op jit(solution)/shard_map/ppermute | solution.py:28
  367.5 4.8 %collective-permute-done.34 = f32[13,4,16,2]{3,2,1,0:T(8,128)S(1)} collective-permute-done((f32[13,4,16,2]{3,2,1,0:T(8,128)S(1)}, f32[13,4,16,2]{3,2,1,0:T(8,128)S(1)}, u32[]{:S(2)}, u32[]{:S(2)}) %collective-permute-start.34) | collective-permute-done | bytes 6688 | tf_op jit(solution)/shard_map/ppermute | solution.py:25
  372.3 5.7 %collective-permute-done.35 = f32[13,4,16,2]{3,2,1,0:T(8,128)S(1)} collective-permute-done((f32[13,4,16,2]{3,2,1,0:T(8,128)S(1)}, f32[13,4,16,2]{3,2,1,0:T(8,128)S(1)}, u32[]{:S(2)}, u32[]{:S(2)}) %collective-permute-start.35) | collective-permute-done | bytes 6688 | tf_op jit(solution)/shard_map/ppermute | solution.py:28
  (193 shorter events, 79.2 us)
Async XLA Ops:
  1.5 5.3 %collective-permute-start = (f32[3,1,16,256]{3,2,1,0:T(8,128)S(1)}, f32[3,1,16,256]{3,2,1,0:T(8,128)S(1)}, u32[]{:S(2)}, u32[]{:S(2)}) collective-permute-start(f32[3,1,16,256]{3,2,1,0:T(8,128)S(1)} %get-tuple-element.134), channel_id=1, source_target_pairs={{0,64},{64,128},{128,192},{1,65},{65,129},{129,193},{2,66},{66,130... | collective-permute-start | bytes 147464 | tf_op jit(solution)/shard_map/ppermute | solution.py:25
  5.5 4.8 %collective-permute-start.1 = (f32[3,1,16,256]{3,2,1,0:T(8,128)S(1)}, f32[3,1,16,256]{3,2,1,0:T(8,128)S(1)}, u32[]{:S(2)}, u32[]{:S(2)}) collective-permute-start(f32[3,1,16,256]{3,2,1,0:T(8,128)S(1)} %get-tuple-element.133), channel_id=1, source_target_pairs={{64,0},{128,64},{192,128},{65,1},{129,65},{193,129},{66,2},{130,66... | collective-permute-start | bytes 147464 | tf_op jit(solution)/shard_map/ppermute | solution.py:28
  10.4 10.1 %collective-permute-start.2 = (f32[3,6,1,256]{3,2,1,0:T(1,128)S(1)}, f32[3,6,1,256]{3,2,1,0:T(1,128)S(1)}, u32[]{:S(2)}, u32[]{:S(2)}) collective-permute-start(f32[3,6,1,256]{3,2,1,0:T(1,128)S(1)} %get-tuple-element.121), channel_id=1, source_target_pairs={{0,8},{8,16},{16,24},{24,32},{32,40},{40,48},{48,56},{1,9},{9,17},... | collective-permute-start | bytes 55304 | tf_op jit(solution)/shard_map/ppermute | solution.py:25
  17.3 6.0 %collective-permute-start.3 = (f32[3,6,1,256]{3,2,1,0:T(1,128)S(1)}, f32[3,6,1,256]{3,2,1,0:T(1,128)S(1)}, u32[]{:S(2)}, u32[]{:S(2)}) collective-permute-start(f32[3,6,1,256]{3,2,1,0:T(1,128)S(1)} %get-tuple-element.122), channel_id=1, source_target_pairs={{8,0},{16,8},{24,16},{32,24},{40,32},{48,40},{56,48},{9,1},{17,9},... | collective-permute-start | bytes 55304 | tf_op jit(solution)/shard_map/ppermute | solution.py:28
  23.5 87.7 %collective-permute-start.4 = (f32[3,6,18,1]{3,2,1,0:T(8,128)S(1)}, f32[3,6,18,1]{3,2,1,0:T(8,128)S(1)}, u32[]{:S(2)}, u32[]{:S(2)}) collective-permute-start(f32[3,6,18,1]{3,2,1,0:T(8,128)S(1)} %get-tuple-element.113), channel_id=1, source_target_pairs={{0,1},{1,2},{2,3},{3,4},{4,5},{5,6},{6,7},{8,9},{9,10},{10,11},{11... | collective-permute-start | bytes 3896 | tf_op jit(solution)/shard_map/ppermute | solution.py:25
  26.6 84.6 %collective-permute-start.5 = (f32[3,6,18,1]{3,2,1,0:T(8,128)S(1)}, f32[3,6,18,1]{3,2,1,0:T(8,128)S(1)}, u32[]{:S(2)}, u32[]{:S(2)}) collective-permute-start(f32[3,6,18,1]{3,2,1,0:T(8,128)S(1)} %get-tuple-element.114), channel_id=1, source_target_pairs={{1,0},{2,1},{3,2},{4,3},{5,4},{6,5},{7,6},{9,8},{10,9},{11,10},{12... | collective-permute-start | bytes 3896 | tf_op jit(solution)/shard_map/ppermute | solution.py:28
  114.2 5.4 %collective-permute-start.7 = (f32[6,1,16,256]{3,2,1,0:T(8,128)S(1)}, f32[6,1,16,256]{3,2,1,0:T(8,128)S(1)}, u32[]{:S(2)}, u32[]{:S(2)}) collective-permute-start(f32[6,1,16,256]{3,2,1,0:T(8,128)S(1)} %get-tuple-element.118), channel_id=1, source_target_pairs={{64,0},{128,64},{192,128},{65,1},{129,65},{193,129},{66,2},{130,66... | collective-permute-start | bytes 294920 | tf_op jit(solution)/shard_map/ppermute | solution.py:28
  119.7 5.7 %collective-permute-start.8 = (f32[6,6,1,256]{3,2,1,0:T(1,128)S(1)}, f32[6,6,1,256]{3,2,1,0:T(1,128)S(1)}, u32[]{:S(2)}, u32[]{:S(2)}) collective-permute-start(f32[6,6,1,256]{3,2,1,0:T(1,128)S(1)} %get-tuple-element.109), channel_id=1, source_target_pairs={{0,8},{8,16},{16,24},{24,32},{32,40},{40,48},{48,56},{1,9},{9,17},... | collective-permute-start | bytes 110600 | tf_op jit(solution)/shard_map/ppermute | solution.py:25
  123.5 6.2 %collective-permute-start.9 = (f32[6,6,1,256]{3,2,1,0:T(1,128)S(1)}, f32[6,6,1,256]{3,2,1,0:T(1,128)S(1)}, u32[]{:S(2)}, u32[]{:S(2)}) collective-permute-start(f32[6,6,1,256]{3,2,1,0:T(1,128)S(1)} %get-tuple-element.110), channel_id=1, source_target_pairs={{8,0},{16,8},{24,16},{32,24},{40,32},{48,40},{56,48},{9,1},{17,9},... | collective-permute-start | bytes 110600 | tf_op jit(solution)/shard_map/ppermute | solution.py:28
  130.0 9.8 %collective-permute-start.10 = (f32[6,6,18,1]{3,2,1,0:T(8,128)S(1)}, f32[6,6,18,1]{3,2,1,0:T(8,128)S(1)}, u32[]{:S(2)}, u32[]{:S(2)}) collective-permute-start(f32[6,6,18,1]{3,2,1,0:T(8,128)S(1)} %get-tuple-element.70), channel_id=1, source_target_pairs={{0,1},{1,2},{2,3},{3,4},{4,5},{5,6},{6,7},{8,9},{9,10},{10,11},{11... | collective-permute-start | bytes 7784 | tf_op jit(solution)/shard_map/ppermute | solution.py:25
  132.4 11.5 %collective-permute-start.11 = (f32[6,6,18,1]{3,2,1,0:T(8,128)S(1)}, f32[6,6,18,1]{3,2,1,0:T(8,128)S(1)}, u32[]{:S(2)}, u32[]{:S(2)}) collective-permute-start(f32[6,6,18,1]{3,2,1,0:T(8,128)S(1)} %get-tuple-element.71), channel_id=1, source_target_pairs={{1,0},{2,1},{3,2},{4,3},{5,4},{6,5},{7,6},{9,8},{10,9},{11,10},{12... | collective-permute-start | bytes 7784 | tf_op jit(solution)/shard_map/ppermute | solution.py:28
  146.1 11.1 %collective-permute-start.12 = (f32[13,2,16,256]{3,2,1,0:T(8,128)S(1)}, f32[13,2,16,256]{3,2,1,0:T(8,128)S(1)}, u32[]{:S(2)}, u32[]{:S(2)}) collective-permute-start(f32[13,2,16,256]{3,2,1,0:T(8,128)S(1)} %get-tuple-element.92), channel_id=1, source_target_pairs={{0,64},{64,128},{128,192},{1,65},{65,129},{129,193},{2,66},{66,130... | collective-permute-start | bytes 1277960 | tf_op jit(solution)/shard_map/ppermute | solution.py:25
  148.9 12.5 %collective-permute-start.13 = (f32[13,2,16,256]{3,2,1,0:T(8,128)S(1)}, f32[13,2,16,256]{3,2,1,0:T(8,128)S(1)}, u32[]{:S(2)}, u32[]{:S(2)}) collective-permute-start(f32[13,2,16,256]{3,2,1,0:T(8,128)S(1)} %get-tuple-element.93), channel_id=1, source_target_pairs={{64,0},{128,64},{192,128},{65,1},{129,65},{193,129},{66,2},{130,66... | collective-permute-start | bytes 1277960 | tf_op jit(solution)/shard_map/ppermute | solution.py:28
  165.4 6.9 %collective-permute-start.15 = (f32[13,4,2,256]{3,2,1,0:T(2,128)S(1)}, f32[13,4,2,256]{3,2,1,0:T(2,128)S(1)}, u32[]{:S(2)}, u32[]{:S(2)}) collective-permute-start(f32[13,4,2,256]{3,2,1,0:T(2,128)S(1)} %get-tuple-element.89), channel_id=1, source_target_pairs={{8,0},{16,8},{24,16},{32,24},{40,32},{48,40},{56,48},{9,1},{17,9},... | collective-permute-start | bytes 319496 | tf_op jit(solution)/shard_map/ppermute | solution.py:28
  174.5 9.2 %collective-permute-start.16 = (f32[13,4,16,2]{3,2,1,0:T(8,128)S(1)}, f32[13,4,16,2]{3,2,1,0:T(8,128)S(1)}, u32[]{:S(2)}, u32[]{:S(2)}) collective-permute-start(f32[13,4,16,2]{3,2,1,0:T(8,128)S(1)} %get-tuple-element.84), channel_id=1, source_target_pairs={{0,1},{1,2},{2,3},{3,4},{4,5},{5,6},{6,7},{8,9},{9,10},{10,11},{11... | collective-permute-start | bytes 19976 | tf_op jit(solution)/shard_map/ppermute | solution.py:25
  177.4 11.1 %collective-permute-start.17 = (f32[13,4,16,2]{3,2,1,0:T(8,128)S(1)}, f32[13,4,16,2]{3,2,1,0:T(8,128)S(1)}, u32[]{:S(2)}, u32[]{:S(2)}) collective-permute-start(f32[13,4,16,2]{3,2,1,0:T(8,128)S(1)} %get-tuple-element.85), channel_id=1, source_target_pairs={{1,0},{2,1},{3,2},{4,3},{5,4},{6,5},{7,6},{9,8},{10,9},{11,10},{12... | collective-permute-start | bytes 19976 | tf_op jit(solution)/shard_map/ppermute | solution.py:28
  195.0 4.8 %collective-permute-start.19 = (f32[3,1,16,256]{3,2,1,0:T(8,128)S(1)}, f32[3,1,16,256]{3,2,1,0:T(8,128)S(1)}, u32[]{:S(2)}, u32[]{:S(2)}) collective-permute-start(f32[3,1,16,256]{3,2,1,0:T(8,128)S(1)} %get-tuple-element.98), channel_id=1, source_target_pairs={{64,0},{128,64},{192,128},{65,1},{129,65},{193,129},{66,2},{130,66... | collective-permute-start | bytes 147464 | tf_op jit(solution)/shard_map/ppermute | solution.py:28
  199.9 6.0 %collective-permute-start.20 = (f32[3,6,1,256]{3,2,1,0:T(1,128)S(1)}, f32[3,6,1,256]{3,2,1,0:T(1,128)S(1)}, u32[]{:S(2)}, u32[]{:S(2)}) collective-permute-start(f32[3,6,1,256]{3,2,1,0:T(1,128)S(1)} %get-tuple-element.119), channel_id=1, source_target_pairs={{0,8},{8,16},{16,24},{24,32},{32,40},{40,48},{48,56},{1,9},{9,17},... | collective-permute-start | bytes 55304 | tf_op jit(solution)/shard_map/ppermute | solution.py:25
  204.0 6.2 %collective-permute-start.21 = (f32[3,6,1,256]{3,2,1,0:T(1,128)S(1)}, f32[3,6,1,256]{3,2,1,0:T(1,128)S(1)}, u32[]{:S(2)}, u32[]{:S(2)}) collective-permute-start(f32[3,6,1,256]{3,2,1,0:T(1,128)S(1)} %get-tuple-element.120), channel_id=1, source_target_pairs={{8,0},{16,8},{24,16},{32,24},{40,32},{48,40},{56,48},{9,1},{17,9},... | collective-permute-start | bytes 55304 | tf_op jit(solution)/shard_map/ppermute | solution.py:28
  210.4 89.0 %collective-permute-start.22 = (f32[3,6,18,1]{3,2,1,0:T(8,128)S(1)}, f32[3,6,18,1]{3,2,1,0:T(8,128)}, u32[]{:S(2)}, u32[]{:S(2)}) collective-permute-start(f32[3,6,18,1]{3,2,1,0:T(8,128)S(1)} %get-tuple-element.111), channel_id=1, source_target_pairs={{0,1},{1,2},{2,3},{3,4},{4,5},{5,6},{6,7},{8,9},{9,10},{10,11},{11... | collective-permute-start | bytes 3896 | tf_op jit(solution)/shard_map/ppermute | solution.py:25
  217.0 82.3 %collective-permute-start.23 = (f32[3,6,18,1]{3,2,1,0:T(8,128)S(1)}, f32[3,6,18,1]{3,2,1,0:T(8,128)}, u32[]{:S(2)}, u32[]{:S(2)}) collective-permute-start(f32[3,6,18,1]{3,2,1,0:T(8,128)S(1)} %get-tuple-element.112), channel_id=1, source_target_pairs={{1,0},{2,1},{3,2},{4,3},{5,4},{6,5},{7,6},{9,8},{10,9},{11,10},{12... | collective-permute-start | bytes 3896 | tf_op jit(solution)/shard_map/ppermute | solution.py:28
  303.6 5.4 %collective-permute-start.25 = (f32[6,1,16,256]{3,2,1,0:T(8,128)S(1)}, f32[6,1,16,256]{3,2,1,0:T(8,128)S(1)}, u32[]{:S(2)}, u32[]{:S(2)}) collective-permute-start(f32[6,1,16,256]{3,2,1,0:T(8,128)S(1)} %get-tuple-element.116), channel_id=1, source_target_pairs={{64,0},{128,64},{192,128},{65,1},{129,65},{193,129},{66,2},{130,66... | collective-permute-start | bytes 294920 | tf_op jit(solution)/shard_map/ppermute | solution.py:28
  309.0 6.6 %collective-permute-start.26 = (f32[6,6,1,256]{3,2,1,0:T(1,128)S(1)}, f32[6,6,1,256]{3,2,1,0:T(1,128)S(1)}, u32[]{:S(2)}, u32[]{:S(2)}) collective-permute-start(f32[6,6,1,256]{3,2,1,0:T(1,128)S(1)} %get-tuple-element.107), channel_id=1, source_target_pairs={{0,8},{8,16},{16,24},{24,32},{32,40},{40,48},{48,56},{1,9},{9,17},... | collective-permute-start | bytes 110600 | tf_op jit(solution)/shard_map/ppermute | solution.py:25
  313.7 6.2 %collective-permute-start.27 = (f32[6,6,1,256]{3,2,1,0:T(1,128)S(1)}, f32[6,6,1,256]{3,2,1,0:T(1,128)S(1)}, u32[]{:S(2)}, u32[]{:S(2)}) collective-permute-start(f32[6,6,1,256]{3,2,1,0:T(1,128)S(1)} %get-tuple-element.108), channel_id=1, source_target_pairs={{8,0},{16,8},{24,16},{32,24},{40,32},{48,40},{56,48},{9,1},{17,9},... | collective-permute-start | bytes 110600 | tf_op jit(solution)/shard_map/ppermute | solution.py:28
  320.2 8.8 %collective-permute-start.28 = (f32[6,6,18,1]{3,2,1,0:T(8,128)S(1)}, f32[6,6,18,1]{3,2,1,0:T(8,128)S(1)}, u32[]{:S(2)}, u32[]{:S(2)}) collective-permute-start(f32[6,6,18,1]{3,2,1,0:T(8,128)S(1)} %get-tuple-element.68), channel_id=1, source_target_pairs={{0,1},{1,2},{2,3},{3,4},{4,5},{5,6},{6,7},{8,9},{9,10},{10,11},{11... | collective-permute-start | bytes 7784 | tf_op jit(solution)/shard_map/ppermute | solution.py:25
  321.6 11.5 %collective-permute-start.29 = (f32[6,6,18,1]{3,2,1,0:T(8,128)S(1)}, f32[6,6,18,1]{3,2,1,0:T(8,128)S(1)}, u32[]{:S(2)}, u32[]{:S(2)}) collective-permute-start(f32[6,6,18,1]{3,2,1,0:T(8,128)S(1)} %get-tuple-element.69), channel_id=1, source_target_pairs={{1,0},{2,1},{3,2},{4,3},{5,4},{6,5},{7,6},{9,8},{10,9},{11,10},{12... | collective-permute-start | bytes 7784 | tf_op jit(solution)/shard_map/ppermute | solution.py:28
  334.7 12.0 %collective-permute-start.30 = (f32[13,2,16,256]{3,2,1,0:T(8,128)S(1)}, f32[13,2,16,256]{3,2,1,0:T(8,128)S(1)}, u32[]{:S(2)}, u32[]{:S(2)}) collective-permute-start(f32[13,2,16,256]{3,2,1,0:T(8,128)S(1)} %get-tuple-element.80), channel_id=1, source_target_pairs={{0,64},{64,128},{128,192},{1,65},{65,129},{129,193},{2,66},{66,130... | collective-permute-start | bytes 1277960 | tf_op jit(solution)/shard_map/ppermute | solution.py:25
  338.4 12.5 %collective-permute-start.31 = (f32[13,2,16,256]{3,2,1,0:T(8,128)S(1)}, f32[13,2,16,256]{3,2,1,0:T(8,128)S(1)}, u32[]{:S(2)}, u32[]{:S(2)}) collective-permute-start(f32[13,2,16,256]{3,2,1,0:T(8,128)S(1)} %get-tuple-element.81), channel_id=1, source_target_pairs={{64,0},{128,64},{192,128},{65,1},{129,65},{193,129},{66,2},{130,66... | collective-permute-start | bytes 1277960 | tf_op jit(solution)/shard_map/ppermute | solution.py:28
  352.5 5.3 %collective-permute-start.32 = (f32[13,4,2,256]{3,2,1,0:T(2,128)S(1)}, f32[13,4,2,256]{3,2,1,0:T(2,128)S(1)}, u32[]{:S(2)}, u32[]{:S(2)}) collective-permute-start(f32[13,4,2,256]{3,2,1,0:T(2,128)S(1)} %get-tuple-element.76), channel_id=1, source_target_pairs={{0,8},{8,16},{16,24},{24,32},{32,40},{40,48},{48,56},{1,9},{9,17},... | collective-permute-start | bytes 319496 | tf_op jit(solution)/shard_map/ppermute | solution.py:25
  355.7 6.9 %collective-permute-start.33 = (f32[13,4,2,256]{3,2,1,0:T(2,128)S(1)}, f32[13,4,2,256]{3,2,1,0:T(2,128)S(1)}, u32[]{:S(2)}, u32[]{:S(2)}) collective-permute-start(f32[13,4,2,256]{3,2,1,0:T(2,128)S(1)} %get-tuple-element.77), channel_id=1, source_target_pairs={{8,0},{16,8},{24,16},{32,24},{40,32},{48,40},{56,48},{9,1},{17,9},... | collective-permute-start | bytes 319496 | tf_op jit(solution)/shard_map/ppermute | solution.py:28
  364.9 7.4 %collective-permute-start.34 = (f32[13,4,16,2]{3,2,1,0:T(8,128)S(1)}, f32[13,4,16,2]{3,2,1,0:T(8,128)S(1)}, u32[]{:S(2)}, u32[]{:S(2)}) collective-permute-start(f32[13,4,16,2]{3,2,1,0:T(8,128)S(1)} %get-tuple-element.72), channel_id=1, source_target_pairs={{0,1},{1,2},{2,3},{3,4},{4,5},{5,6},{6,7},{8,9},{9,10},{10,11},{11... | collective-permute-start | bytes 19976 | tf_op jit(solution)/shard_map/ppermute | solution.py:25
  366.2 11.7 %collective-permute-start.35 = (f32[13,4,16,2]{3,2,1,0:T(8,128)S(1)}, f32[13,4,16,2]{3,2,1,0:T(8,128)S(1)}, u32[]{:S(2)}, u32[]{:S(2)}) collective-permute-start(f32[13,4,16,2]{3,2,1,0:T(8,128)S(1)} %get-tuple-element.73), channel_id=1, source_target_pairs={{1,0},{2,1},{3,2},{4,3},{5,4},{6,5},{7,6},{9,8},{10,9},{11,10},{12... | collective-permute-start | bytes 19976 | tf_op jit(solution)/shard_map/ppermute | solution.py:28
  (12 other events, 50.2 us)
where the time goes:
time: 390 us; the launch traced here: 383 us
  blocking collectives  159 us (41%)
  waiting for transfers between devices  102 us (26%)
  starting transfers between devices  87.2 us (22%)
  other arithmetic  22.8 us (6%)
  local copies, waits for them, and re-layouts  6.56 us (2%)
  between operations  5.8 us (1%)
    pmax x2, blocking collectives, shards(): top_speed = lax.pmax(local_speed, ('gx', 'gy', 'gz'))  159 us
    ppermute x18, waiting for transfers between devices, with_halo(): lax.ppermute(lax.slice_in_dim(block, 0, width, axis=dim), axis, backward)  65.6 us
    ppermute x18, starting transfers between devices, with_halo(): lax.ppermute(lax.slice_in_dim(block, block.shape[dim] - width, None, axis...  59.8 us
    ppermute x18, waiting for transfers between devices, with_halo(): lax.ppermute(lax.slice_in_dim(block, block.shape[dim] - width, None, axis...  36.4 us
    ppermute x18, starting transfers between devices, with_halo(): lax.ppermute(lax.slice_in_dim(block, 0, width, axis=dim), axis, backward)  27.5 us
  transfers between devices with their start and end apart: 36, of which 24 were waited for; matrix products, arithmetic and copies ran while one was open for 1% of the time, Pallas kernels for 0%

commit v1 on v0

v1 whole, which is shorter than its diff:
```python
import jax
import jax.numpy as jnp
from jax import lax
from jax.experimental import pallas as pl
from jax.experimental.pallas import tpu as pltpu
from jax.sharding import PartitionSpec as P


FIELDS = 13
PLANES = 16
ROWS = 24
OWN = 16
LANES = 128
HALF = 64
PAD = 2

shear_table = (1.0, 0.5, 0.8)
sound_table = (1.5, 1.2, 1.0)
gruneisen_table = (2.0, 2.1, 1.9)
rest_table = (4.0, 3.0, 5.0)
yield_table = (0.3, 0.2, 0.25)
harden_table = (0.5, 0.3, 0.4)
exponent_table = (0.3, 0.4, 0.35)
rate_table = (0.02, 0.015, 0.01)
cfl_number = 0.2

ALL_AXES = ("gx", "gy", "gz")
ACROSS = ((0, 3, 5), (3, 1, 4), (5, 4, 2))


def roll(value, shift, axis):
    shift = shift % value.shape[axis]
    return value if shift == 0 else pltpu.roll(value, shift, axis)


def iota(shape, axis):
    return lax.broadcasted_iota(jnp.int32, shape, axis)


def inverse(value):
    guess = pl.reciprocal(value, approx=True)
    return guess * (2.0 - value * guess)


def pick(first, second, table):
    return jnp.where(first, table[0], jnp.where(second, table[1], table[2]))


def stack_rows(even, odd, upper):
    low_rows = iota((8, LANES), 0) < 4
    if upper:
        return jnp.where(low_rows, roll(even[8:], 4, 0), odd[8:])
    return jnp.where(low_rows, even[:8], roll(odd[:8], 4, 0))


def halo_tile(high, low, odd):
    low_rows = iota((8, LANES), 0) < 4
    if odd:
        return jnp.where(low_rows, roll(high, 4, 0), low)
    return jnp.where(low_rows, high, roll(low, 4, 0))


def pack_kernel(place, dens, ener, vel, plas, dama, devi, mat, own, to1, to2, to3, top):
    me = place[0]
    refs = [dens, ener] + [vel.at[i] for i in range(3)] + [plas, dama]
    refs = refs + [devi.at[i] for i in range(6)] + [mat]
    peak = None
    for x in range(4):
        for t in range(2):
            cols = slice(t * LANES, (t + 1) * LANES)
            speed = jnp.maximum(jnp.abs(vel[0, x, :, cols]), jnp.abs(vel[1, x, :, cols]))
            speed = jnp.maximum(speed, jnp.abs(vel[2, x, :, cols]))
            kind = mat[x, :, cols]
            speed = speed + pick(kind == 0, kind == 1, sound_table)
            peak = speed if peak is None else jnp.maximum(peak, speed)
    top[...] = jnp.full(top.shape, jnp.max(peak), jnp.float32)
    left = iota((OWN, LANES), 1) < HALF
    for k, out in enumerate((own, to1, to2, to3)):
        target = me ^ k
        cols = pl.ds(pl.multiple_of((target >> 1) * LANES, LANES), LANES)
        odd = target & 1
        for f in range(FIELDS + 1):
            for j in range(2):
                even_plane = refs[f][2 * j, :, cols].astype(jnp.float32)
                odd_plane = refs[f][2 * j + 1, :, cols].astype(jnp.float32)
                out[f, j] = jnp.where(
                    left,
                    pltpu.roll(even_plane, odd * HALF, 1),
                    pltpu.roll(odd_plane, (1 - odd) * HALF, 1),
                )


def spread_kernel(place, own, from1, from2, from3, state, up, down):
    me = place[0]
    for k, src in enumerate((own, from1, from2, from3)):
        block = me ^ k
        for f in range(FIELDS + 1):
            first, second = src[f, 0], src[f, 1]
            state[f, 4 * block] = first
            state[f, 4 * block + 1] = roll(first, HALF, 1)
            state[f, 4 * block + 2] = second
            state[f, 4 * block + 3] = roll(second, HALF, 1)
            up[f, block] = stack_rows(first, second, True)
            down[f, block] = stack_rows(first, second, False)


def rows_kernel(state, low, high, tiles, z_up, z_down):
    for f in range(FIELDS + 1):
        for block in range(4):
            for j in range(2):
                tile = halo_tile(high[f, block], low[f, block], j == 1)
                tiles[f, 4 * block + 2 * j] = tile
                tiles[f, 4 * block + 2 * j + 1] = roll(tile, HALF, 1)

    def plane(p, carry):
        for rows in (OWN, 8):
            group = iota((rows, LANES), 1) >> 3
            ups = jnp.zeros((rows, LANES), jnp.float32)
            downs = ups
            for f in range(FIELDS + 1):
                value = state[f, p] if rows == OWN else tiles[f, p]
                ups = jnp.where(group == f, roll(value, 8 * f - (HALF - 8), 1), ups)
                downs = jnp.where(group == f, roll(value, 8 * f, 1), downs)
            at = slice(0, OWN) if rows == OWN else slice(OWN, ROWS)
            z_up[p, at] = ups
            z_down[p, at] = downs
        return carry

    lax.fori_loop(0, PLANES, plane, 0)


def set_masks(place, width, inside, face_y, face_z):
    shape = (ROWS, LANES)
    row, lane = iota(shape, 0), iota(shape, 1)
    row_ok = (row < OWN) | ((row < OWN + 4) & (place[1] < place[3])) | ((row >= OWN + 4) & (place[1] > 0))
    lane_ok = (
        (lane < HALF)
        | ((lane < HALF + width) & (place[2] < place[4]))
        | ((lane >= LANES - width) & (place[2] > 0))
    )
    ok = jnp.where(row_ok & lane_ok, 1.0, 0.0)
    inside[...] = ok
    face_y[...] = ok * roll(ok, -1, 0)
    face_z[...] = ok * roll(ok, -1, 1)


def step_size(step_no, timestep, tops):
    top_speed = jnp.max(tops[...], axis=0, keepdims=True)
    asked = timestep[step_no]
    return asked / (1.0 + asked * top_speed / cfl_number)


def central(upper, lower):
    return 0.5 * (upper - lower)


def limited(back, fore):
    product = back * fore
    return jnp.where(product > 0.0, product * inverse(back + fore), 0.0)


def carried(positive, here, there, slope_here, slope_there, courant, weight):
    return courant * (
        jnp.where(positive, here, there) + weight * jnp.where(positive, slope_here, slope_there)
    )


def weigh(courant):
    return jnp.where(courant > 0.0, 1.0, -1.0) - courant


def rolled_sweep(fields, comp, courant_mask, inside, axis, dt):
    velocity = fields[comp]
    courant = dt * 0.5 * (velocity + roll(velocity, -1, axis)) * courant_mask
    positive = courant > 0.0
    weight = weigh(courant)
    density = fields[0]
    result = []
    scale = None
    for f in range(FIELDS):
        q = density if f == 0 else density * fields[f]
        q_next = roll(q, -1, axis)
        fore = q_next - q
        slope = limited(roll(fore, 1, axis), fore)
        flux = carried(positive, q, q_next, slope, roll(slope, -1, axis), courant, weight)
        q = q - (flux - roll(flux, 1, axis))
        if f == 0:
            scale = jnp.where(inside, inverse(q), 0.0)
            result.append(jnp.where(inside, q, 0.0))
        else:
            result.append(q * scale)
    return result


def advance(dt, state, moved, stress, courants, weights, scales, inside, face_y, face_z, out):
    def strain_plane(p, carry):
        at = p + PAD
        ok = inside[...] > 0.0
        vel = [state[2 + i, at] for i in range(3)]
        grad = [
            [
                central(state[2 + i, at + 1], state[2 + i, at - 1]),
                central(roll(vel[i], -1, 0), roll(vel[i], 1, 0)),
                central(roll(vel[i], -1, 1), roll(vel[i], 1, 1)),
            ]
            for i in range(3)
        ]
        third_div = (grad[0][0] + grad[1][1] + grad[2][2]) * (1.0 / 3.0)
        strain = [
            grad[0][0] - third_div,
            grad[1][1] - third_div,
            grad[2][2] - third_div,
            0.5 * (grad[0][1] + grad[1][0]),
            0.5 * (grad[1][2] + grad[2][1]),
            0.5 * (grad[0][2] + grad[2][0]),
        ]
        kind = state[FIELDS, at]
        first, second = kind == 0.0, kind == 1.0
        density, energy = state[0, at], state[1, at]
        plastic, damage = state[5, at], state[6, at]
        pressure = (
            pick(first, second, tuple(c * c for c in sound_table))
            * (density - pick(first, second, rest_table))
            + pick(first, second, gruneisen_table) * density * energy
        )
        shear_dt = pick(first, second, tuple(2.0 * g for g in shear_table)) * dt
        trial = [state[7 + k, at] + shear_dt * strain[k] for k in range(6)]
        trial_sq = (
            trial[0] * trial[0]
            + trial[1] * trial[1]
            + trial[2] * trial[2]
            + 2.0 * (trial[3] * trial[3] + trial[4] * trial[4] + trial[5] * trial[5])
        )
        strain_sq = (
            strain[0] * strain[0]
            + strain[1] * strain[1]
            + strain[2] * strain[2]
            + 2.0 * (strain[3] * strain[3] + strain[4] * strain[4] + strain[5] * strain[5])
        )
        equivalent = jnp.sqrt(1.5 * trial_sq)
        strain_rate = jnp.sqrt(strain_sq * (2.0 / 3.0))
        hardened = pick(first, second, yield_table) + pick(first, second, harden_table) * jnp.exp(
            pick(first, second, exponent_table) * jnp.log(plastic)
        )
        flow = (
            hardened
            * (1.0 + pick(first, second, rate_table) * jnp.log(1.0 + strain_rate))
            * (1.0 - damage)
        )
        bound = jnp.maximum(equivalent, flow)
        per_bound = inverse(bound)
        factor = flow * per_bound
        increment = (bound - flow) * pick(first, second, tuple(1.0 / (3.0 * g) for g in shear_table))
        triaxial = jnp.clip(-pressure * per_bound, -1.5, 1.5)
        failure = 0.05 + 0.8 * jnp.exp(-1.5 * triaxial)
        state[5, at] = jnp.where(ok, plastic + increment, 0.0)
        state[6, at] = jnp.where(ok, jnp.minimum(damage + increment * inverse(failure), 0.9), 0.0)
        dev = [jnp.where(ok, trial[k] * factor, 0.0) for k in range(6)]
        held = jnp.where(ok, pressure, 0.0)
        full = [dev[0] - held, dev[1] - held, dev[2] - held, dev[3], dev[4], dev[5]]
        for k in range(6):
            state[7 + k, at] = dev[k]
            stress[k, p + 1] = full[k]
        work = (
            full[0] * grad[0][0]
            + full[1] * grad[1][1]
            + full[2] * grad[2][2]
            + 2.0 * (full[3] * strain[3] + full[4] * strain[4] + full[5] * strain[5])
        )
        state[1, at] = jnp.where(ok, energy + dt * work * inverse(density), 0.0)
        return carry

    zero = jnp.zeros((ROWS, LANES), jnp.float32)
    for k in range(6):
        stress[k, 0] = zero
        stress[k, PLANES + 1] = zero
    lax.fori_loop(0, PLANES, strain_plane, 0)

    def force_plane(p, carry):
        at = p + PAD
        ok = inside[...] > 0.0
        pushed = jnp.where(ok, dt * inverse(state[0, at]), 0.0)
        here = [stress[k, p + 1] for k in range(6)]
        for i in range(3):
            along_x, along_y, along_z = ACROSS[0][i], ACROSS[1][i], ACROSS[2][i]
            force = (
                central(stress[along_x, p + 2], stress[along_x, p])
                + central(roll(here[along_y], -1, 0), roll(here[along_y], 1, 0))
                + central(roll(here[along_z], -1, 1), roll(here[along_z], 1, 1))
            )
            state[2 + i, at] = state[2 + i, at] + pushed * force
        return carry

    lax.fori_loop(0, PLANES, force_plane, 0)

    for p in range(PLANES - 1):
        courant = dt * 0.5 * (state[2, p + PAD] + state[2, p + PAD + 1])
        courants[p] = courant
        weights[p] = weigh(courant)

    def stream(load, store):
        here = load(0)
        back = here
        ahead = load(1)
        fore = ahead - here
        slope = limited(back, fore)
        last_flux = None
        for p in range(PLANES):
            if p < PLANES - 1:
                further = load(p + 2) if p + 2 < PLANES else None
                next_fore = further - ahead if further is not None else -ahead
                next_slope = limited(fore, next_fore)
                courant = courants[p]
                flux = carried(
                    courant > 0.0, here, ahead, slope, next_slope, courant, weights[p]
                )
                change = flux if last_flux is None else flux - last_flux
            else:
                flux, further, next_fore, next_slope = None, None, None, None
                change = -last_flux
            store(p, here - change)
            last_flux, here, ahead, fore, slope = flux, ahead, further, next_fore, next_slope

    def store_density(p, value):
        ok = inside[...] > 0.0
        moved[0, p] = jnp.where(ok, value, 0.0)
        scales[p] = jnp.where(ok, inverse(value), 0.0)

    stream(lambda p: state[0, p + PAD], store_density)

    def field(f, carry):
        def store(p, value):
            moved[f, p] = value * scales[p]

        stream(lambda p: state[0, p + PAD] * state[f, p + PAD], store)
        return carry

    lax.fori_loop(1, FIELDS, field, 0)

    def plane(p, carry):
        ok = inside[...] > 0.0
        fields = rolled_sweep([moved[f, p] for f in range(FIELDS)], 3, face_y[...], ok, 0, dt)
        fields = [value[:OWN] for value in fields]
        fields = rolled_sweep(fields, 4, face_z[:OWN], ok[:OWN], 1, dt)
        for f in range(FIELDS):
            out[f, p] = fields[f]
        return carry

    lax.fori_loop(0, PLANES, plane, 0)


def clear_ends(state):
    zero = jnp.zeros((ROWS, LANES), jnp.float32)
    for f in range(FIELDS + 1):
        for p in (0, 1, PLANES + PAD, PLANES + PAD + 1):
            state[f, p] = zero


def first_kernel(
    place, timestep, tops, own, tiles, z_low, z_high, out, kinds, up, down, top,
    state, moved, stress, courants, weights, scales, inside, face_y, face_z,
):
    set_masks(place, 8, inside, face_y, face_z)
    clear_ends(state)
    dt = step_size(0, timestep, tops)

    def gather(p, carry):
        ok = inside[...] > 0.0
        lane = iota((ROWS, LANES), 1)
        below, above = z_low[p], z_high[p]
        for f in range(FIELDS + 1):
            value = jnp.concatenate([own[f, p], tiles[f, p]], axis=0)
            side = jnp.where(lane < 96, roll(above, HALF - 8 * f, 1), roll(below, LANES - 8 - 8 * f, 1))
            value = jnp.where(ok, jnp.where(lane < HALF, value, side), 0.0)
            state[f, p + PAD] = value
            if f == FIELDS:
                kinds[p] = value
        return carry

    lax.fori_loop(0, PLANES, gather, 0)
    advance(dt, state, moved, stress, courants, weights, scales, inside, face_y, face_z, out)

    lane = iota((OWN, LANES), 1)
    peak = jnp.zeros((OWN, LANES), jnp.float32)

    def peaks(p, peak):
        speed = jnp.maximum(jnp.abs(out[2, p]), jnp.abs(out[3, p]))
        speed = jnp.maximum(speed, jnp.abs(out[4, p]))
        kind = kinds[p, :OWN]
        speed = speed + pick(kind == 0.0, kind == 1.0, sound_table)
        return jnp.maximum(peak, jnp.where(lane < HALF, speed, 0.0))

    peak = lax.fori_loop(0, PLANES, peaks, peak)
    top[...] = jnp.full(top.shape, jnp.max(peak), jnp.float32)

    def messages(i, carry):
        for f in range(FIELDS):
            even, odd = out[f, 2 * i], out[f, 2 * i + 1]
            up[f, i] = stack_rows(even, odd, True)
            down[f, i] = stack_rows(even, odd, False)
        return carry

    lax.fori_loop(0, PLANES // 2, messages, 0)


def second_kernel(
    place, timestep, tops, own, kinds, low, high, mine, to1, to2, to3,
    state, moved, stress, courants, weights, scales, inside, face_y, face_z, out,
):
    set_masks(place, 4, inside, face_y, face_z)
    clear_ends(state)
    dt = step_size(1, timestep, tops)

    def gather(i, carry):
        ok = inside[...] > 0.0
        for f in range(FIELDS):
            for odd in range(2):
                p = 2 * i + odd
                tile = halo_tile(high[f, i], low[f, i], odd == 1)
                value = jnp.concatenate([own[f, p], tile], axis=0)
                state[f, p + PAD] = jnp.where(ok, value, 0.0)
        for odd in range(2):
            state[FIELDS, 2 * i + odd + PAD] = kinds[2 * i + odd]
        return carry

    lax.fori_loop(0, PLANES // 2, gather, 0)
    advance(dt, state, moved, stress, courants, weights, scales, inside, face_y, face_z, out)

    left = iota((OWN, LANES), 1) < HALF
    for k, dest in enumerate((mine, to1, to2, to3)):
        block = place[0] ^ k
        for f in range(FIELDS):
            for j in range(2):
                even, odd = out[f, 4 * block + 2 * j], out[f, 4 * block + 2 * j + 1]
                dest[f, j] = jnp.where(left, even, roll(odd, HALF, 1))


def unpack_kernel(place, mine, from1, from2, from3, dens, ener, vel, plas, dama, devi, held):
    me = place[0]
    refs = [dens, ener] + [vel.at[i] for i in range(3)] + [plas, dama]
    refs = refs + [devi.at[i] for i in range(6)]
    for k, src in enumerate((mine, from1, from2, from3)):
        held[me ^ k] = src[...]
    left = iota((OWN, LANES), 1) < HALF
    for f in range(FIELDS):
        for j in range(2):
            for t in range(2):
                first, second = held[2 * t, f, j], held[2 * t + 1, f, j]
                cols = slice(t * LANES, (t + 1) * LANES)
                refs[f][2 * j, :, cols] = jnp.where(left, first, roll(second, HALF, 1))
                refs[f][2 * j + 1, :, cols] = jnp.where(left, roll(first, HALF, 1), second)


IN_VMEM = pl.BlockSpec(memory_space=pltpu.VMEM)
IN_SMEM = pl.BlockSpec(memory_space=pltpu.SMEM)


def call(kernel, scalars, outs, scratch, *args):
    return pl.pallas_call(
        kernel,
        out_shape=[jax.ShapeDtypeStruct(shape, jnp.float32) for shape in outs],
        in_specs=[IN_SMEM] * scalars + [IN_VMEM] * (len(args) - scalars),
        out_specs=[IN_VMEM] * len(outs),
        scratch_shapes=[pltpu.VMEM(shape, jnp.float32) for shape in scratch],
        compiler_params=pltpu.CompilerParams(vmem_limit_bytes=48 * 1024 * 1024),
    )(*args)


def ring_pair(to_next, to_last, axes, order):
    after = order[1:] + order[:1]
    low = lax.ppermute(to_next, axes, list(zip(order, after)))
    high = lax.ppermute(to_last, axes, list(zip(after, order)))
    return low, high


def swap_blocks(parts):
    count = lax.axis_size("gx")
    return [
        lax.ppermute(part, "gx", [(i, i ^ (k + 1)) for i in range(count)])
        for k, part in enumerate(parts)
    ]


def shards(density, energy, velocity, plastic_strain, damage, deviator, materials, timestep):
    size_x, size_y, size_z = lax.axis_size("gx"), lax.axis_size("gy"), lax.axis_size("gz")
    place_x, place_y, place_z = lax.axis_index("gx"), lax.axis_index("gy"), lax.axis_index("gz")
    total = size_x * size_y * size_z
    chunks = size_z * size_x
    place = jnp.stack(
        [place_x, place_y, place_z * size_x + place_x, jnp.int32(size_y - 1), jnp.int32(chunks - 1)]
    ).astype(jnp.int32)
    z_order = [x * size_z + z for z in range(size_z) for x in range(size_x)]
    all_fields = FIELDS + 1
    part = (all_fields, 2, OWN, LANES)
    own, *parts, top = call(
        pack_kernel, 1, [part] * 4 + [(total, LANES)], [],
        place, density, energy, velocity, plastic_strain, damage, deviator, materials,
    )
    parts = swap_blocks(parts)
    tops = lax.all_to_all(top, ALL_AXES, 0, 0)
    state, up, down = call(
        spread_kernel,
        1,
        [(all_fields, PLANES, OWN, LANES)] + [(all_fields, 4, 8, LANES)] * 2,
        [],
        place,
        own,
        *parts,
    )
    low, high = ring_pair(up, down, "gy", list(range(size_y)))
    tiles, z_up, z_down = call(
        rows_kernel,
        0,
        [(all_fields, PLANES, 8, LANES)] + [(PLANES, ROWS, LANES)] * 2,
        [],
        state,
        low,
        high,
    )
    z_low, z_high = ring_pair(z_up, z_down, ("gx", "gz"), z_order)
    full = (ROWS, LANES)
    scratch = [
        (all_fields, PLANES + 2 * PAD) + full,
        (FIELDS, PLANES) + full,
        (6, PLANES + 2) + full,
        (PLANES,) + full,
        (PLANES,) + full,
        (PLANES,) + full,
        full,
        full,
        full,
    ]
    block = (FIELDS, PLANES, OWN, LANES)
    state, kinds, up, down, top = call(
        first_kernel,
        2,
        [block, (PLANES,) + full] + [(FIELDS, PLANES // 2, 8, LANES)] * 2 + [(total, LANES)],
        scratch,
        place,
        timestep,
        tops,
        state,
        tiles,
        z_low,
        z_high,
    )
    low, high = ring_pair(up, down, "gy", list(range(size_y)))
    tops = lax.all_to_all(top, ALL_AXES, 0, 0)
    mine, *parts = call(
        second_kernel,
        2,
        [(FIELDS, 2, OWN, LANES)] * 4,
        scratch + [block],
        place,
        timestep,
        tops,
        state,
        kinds,
        low,
        high,
    )
    parts = swap_blocks(parts)
    cells = density.shape
    return tuple(
        call(
            unpack_kernel,
            1,
            [cells, cells, (3,) + cells, cells, cells, (6,) + cells],
            [(4, FIELDS, 2, OWN, LANES)],
            place,
            mine,
            *parts,
        )
    )


def solution(mesh):
    cells = P("gx", "gy", "gz")
    vectors = P(None, "gx", "gy", "gz")
    return jax.shard_map(
        shards,
        mesh=mesh,
        in_specs=(cells, cells, vectors, cells, cells, vectors, cells, P()),
        out_specs=(cells, cells, vectors, cells, cells, vectors),
        check_vma=False,
    )
```

time: 390 us -> 135 us (0.35); the launches traced: 383 us -> 134 us
  blocking collectives: 159 us -> 26.4 us
  waiting for transfers between devices: 102 us -> 25.8 us
  starting transfers between devices: 87.2 us -> 37.1 us
  Pallas kernels: 0 us -> 38.2 us
  other arithmetic: 22.8 us -> 0 us
  between operations: 5.8 us -> 0.7 us
    pmax x2 -> x0, blocking collectives: 159 us -> none  [shards(): top_speed = lax.pmax(local_speed, ('gx', 'gy', 'gz'))]
    ppermute x36 -> x12, waiting for transfers between devices: 102 us -> 22.3 us  [the longest x6 22.1 us: swap_blocks(): lax.ppermute(part, 'gx', [(i, i ^ k + 1) for i in range(count)])]
    ppermute x36 -> x12, starting transfers between devices: 87.2 us -> 24.6 us  [the longest x3 11.3 us: ring_pair(): low = lax.ppermute(to_next, axes, list(zip(order, after)))]
    pallas_call x0 -> x6, Pallas kernels: none -> 38.2 us  [call(): pl.pallas_call(kernel, out_shape=[jax.ShapeDtypeStruct(shape, jnp.float32...]
    all_to_all x0 -> x1, blocking collectives: none -> 26.4 us  [shards(): tops = lax.all_to_all(top, ALL_AXES, 0, 0)]
    all_to_all x0 -> x1, starting transfers between devices: none -> 12.5 us  [shards(): tops = lax.all_to_all(top, ALL_AXES, 0, 0)]
    select_n x12 -> x0, other arithmetic: 6.77 us -> none  [the longest x6 4.14 us: sweep(): face_flux = jnp.where(closed, 0.0, face_flux)]
    unnamed x17 -> x16, local copies, waits for them, and re-layouts: 1.08 us -> 6.12 us
  transfers between devices with their start and end apart: 36 -> 13, of which waited for: 24 -> 8; matrix products, arithmetic and copies ran while one was open for 1% -> 0% of each run, Pallas kernels for 0% -> 2%
where the time goes in v1:
time: 135 us; the launch traced here: 134 us
  Pallas kernels  38.2 us (28%)
  starting transfers between devices  37.1 us (27%)
  blocking collectives  26.4 us (20%)
  waiting for transfers between devices  25.8 us (19%)
  local copies, waits for them, and re-layouts  6.21 us (5%)
    pallas_call x6, Pallas kernels, call(): pl.pallas_call(kernel, out_shape=[jax.ShapeDtypeStruct(shape, jnp.float32...  38.2 us
    all_to_all x1, blocking collectives, shards(): tops = lax.all_to_all(top, ALL_AXES, 0, 0)  26.4 us
    ppermute x6, waiting for transfers between devices, swap_blocks(): lax.ppermute(part, 'gx', [(i, i ^ k + 1) for i in range(count)])  22.1 us
    all_to_all x1, starting transfers between devices, shards(): tops = lax.all_to_all(top, ALL_AXES, 0, 0)  12.5 us
    ppermute x3, starting transfers between devices, ring_pair(): low = lax.ppermute(to_next, axes, list(zip(order, after)))  11.3 us
    ppermute x6, starting transfers between devices, swap_blocks(): lax.ppermute(part, 'gx', [(i, i ^ k + 1) for i in range(count)])  8.7 us
    unnamed x16, local copies, waits for them, and re-layouts  6.12 us
    ppermute x3, starting transfers between devices, ring_pair(): high = lax.ppermute(to_last, axes, list(zip(after, order)))  4.6 us
  transfers between devices with their start and end apart: 13, of which 8 were waited for; matrix products, arithmetic and copies ran while one was open for 0% of the time, Pallas kernels for 2%

profile of v1, /device:TPU:1, one launch (start us, length us, event | category | flops | bytes accessed | tf_op | source)
XLA Modules:
  0.0 134.3 jit_solution(5362242687244024027)
XLA Ops:
  0.7 1.0 copy-done
  1.7 0.9 copy-done.1
  2.6 0.8 copy-done.2
  3.5 0.8 copy-done.3
  4.3 0.8 copy-done.4
  5.2 0.8 copy-done.5
  6.0 0.8 copy-done.6
  6.8 1.7 %shard_map.127 = (f32[14,2,16,128]{3,2,1,0:T(8,128)S(1)}, f32[14,2,16,128]{3,2,1,0:T(8,128)S(1)}, f32[14,2,16,128]{3,2,1,0:T(8,128)S(1)}, f32[14,2,16,128]{3,2,1,0:T(8,128)S(1)}, f32[256,128]{1,0:T(8,128)}) custom-call(s32[5]{0:T(128)S(1)} %stack.15.place, f32[4,16,256]{2,1,0:T(8,128)S(1)} %copy-done.2, f32[4,16,256]{2,1,0:T(8,128)S(1)} %copy-done.3, ...), custom_call_target="tpu_custom_call" | custom-call | tf_op jit(solution)/shard_map/pallas_call | solution.py:459
  8.5 2.1 %collective-permute-start = (f32[14,2,16,128]{3,2,1,0:T(8,128)S(1)}, f32[14,2,16,128]{3,2,1,0:T(8,128)S(1)}, u32[]{:S(2)}, u32[]{:S(2)}) collective-permute-start(f32[14,2,16,128]{3,2,1,0:T(8,128)S(1)} %get-tuple-element.28), channel_id=1, source_target_pairs={{0,64},{64,0},{128,192},{192,128},{1,65},{65,1},{129,193},{193,129... | collective-permute-start | bytes 688136 | tf_op jit(solution)/shard_map/ppermute | solution.py:479
  10.7 2.6 %collective-permute-start.1 = (f32[14,2,16,128]{3,2,1,0:T(8,128)S(1)}, f32[14,2,16,128]{3,2,1,0:T(8,128)S(1)}, u32[]{:S(2)}, u32[]{:S(2)}) collective-permute-start(f32[14,2,16,128]{3,2,1,0:T(8,128)S(1)} %get-tuple-element.29), channel_id=1, source_target_pairs={{0,128},{64,192},{128,0},{192,64},{1,129},{65,193},{129,1},{193,65... | collective-permute-start | bytes 688136 | tf_op jit(solution)/shard_map/ppermute | solution.py:479
  13.3 1.5 %collective-permute-done.from1 = f32[14,2,16,128]{3,2,1,0:T(8,128)S(1)} collective-permute-done((f32[14,2,16,128]{3,2,1,0:T(8,128)S(1)}, f32[14,2,16,128]{3,2,1,0:T(8,128)S(1)}, u32[]{:S(2)}, u32[]{:S(2)}) %collective-permute-start) | collective-permute-done | bytes 229408 | tf_op jit(solution)/shard_map/ppermute | solution.py:479
  14.8 8.5 %collective-permute-done.1.from2 = f32[14,2,16,128]{3,2,1,0:T(8,128)S(1)} collective-permute-done((f32[14,2,16,128]{3,2,1,0:T(8,128)S(1)}, f32[14,2,16,128]{3,2,1,0:T(8,128)S(1)}, u32[]{:S(2)}, u32[]{:S(2)}) %collective-permute-start.1) | collective-permute-done | bytes 229408 | tf_op jit(solution)/shard_map/ppermute | solution.py:479
  23.3 2.3 %collective-permute-done.2.from3 = f32[14,2,16,128]{3,2,1,0:T(8,128)S(1)} collective-permute-done((f32[14,2,16,128]{3,2,1,0:T(8,128)S(1)}, f32[14,2,16,128]{3,2,1,0:T(8,128)S(1)}, u32[]{:S(2)}, u32[]{:S(2)}) %collective-permute-start.2) | collective-permute-done | bytes 229408 | tf_op jit(solution)/shard_map/ppermute | solution.py:479
  25.6 0.9 shard_map.128
  26.5 4.8 %collective-permute-start.3 = (f32[14,4,8,128]{3,2,1,0:T(8,128)S(1)}, f32[14,4,8,128]{3,2,1,0:T(8,128)S(1)}, u32[]{:S(2)}, u32[]{:S(2)}) collective-permute-start(f32[14,4,8,128]{3,2,1,0:T(8,128)S(1)} %get-tuple-element.32), channel_id=1, source_target_pairs={{0,8},{8,16},{16,24},{24,32},{32,40},{40,48},{48,56},{56,0},{1,9},... | collective-permute-start | bytes 688136 | tf_op jit(solution)/shard_map/ppermute | solution.py:471
  31.3 12.5 %all-to-all-start = ((f32[256,1,128]{2,1,0:T(1,128)}), f32[256,1,128]{2,1,0:T(1,128)S(1)}, u32[]{:S(2)}, u32[]{:S(2)}) async-start(f32[256,1,128]{2,1,0:T(1,128)} %bitcast.4), calls=%async_computation | async-start | bytes 262144 | tf_op jit(solution)/shard_map/all_to_all | solution.py:500
  43.8 3.3 %shard_map.129 = (f32[14,16,8,128]{3,2,1,0:T(8,128)S(1)}, f32[16,24,128]{2,1,0:T(8,128)}, f32[16,24,128]{2,1,0:T(8,128)S(1)}) custom-call(f32[14,16,16,128]{3,2,1,0:T(8,128)S(1)} %get-tuple-element.31.state.own, f32[14,4,8,128]{3,2,1,0:T(8,128)S(1)} %collective-permute-done.3.low, f32[14,4,8,128]{3,2,1,0:T(8,128)S(1)} %collective-permute-done.4.high), custom_call_target="tpu_custom_call" | custom-call | tf_op jit(solution)/shard_map/pallas_call | solution.py:459
  47.1 1.4 %collective-permute-start.5 = (f32[16,24,128]{2,1,0:T(8,128)}, f32[16,24,128]{2,1,0:T(8,128)S(1)}, u32[]{:S(2)}, u32[]{:S(2)}) collective-permute-start(f32[16,24,128]{2,1,0:T(8,128)} %get-tuple-element.35), channel_id=1, source_target_pairs={{0,64},{64,128},{128,192},{192,1},{1,65},{65,129},{129,193},{193,2... | collective-permute-start | bytes 589832 | tf_op jit(solution)/shard_map/ppermute | solution.py:471
  48.5 4.6 %collective-permute-start.6 = (f32[16,24,128]{2,1,0:T(8,128)S(1)}, f32[16,24,128]{2,1,0:T(8,128)S(1)}, u32[]{:S(2)}, u32[]{:S(2)}) collective-permute-start(f32[16,24,128]{2,1,0:T(8,128)S(1)} %get-tuple-element.36), channel_id=1, source_target_pairs={{64,0},{128,64},{192,128},{1,192},{65,1},{129,65},{193,129},{2,193... | collective-permute-start | bytes 589832 | tf_op jit(solution)/shard_map/ppermute | solution.py:472
  53.1 3.5 %all-to-all-done = f32[256,1,128]{2,1,0:T(1,128)S(1)} async-done(((f32[256,1,128]{2,1,0:T(1,128)}), f32[256,1,128]{2,1,0:T(1,128)S(1)}, u32[]{:S(2)}, u32[]{:S(2)}) %all-to-all-start) | async-done | bytes 131104 | tf_op jit(solution)/shard_map/all_to_all | solution.py:500
  56.6 0.2 collective-permute-done.5.z_low
  56.8 16.5 %shard_map.130 = (f32[13,16,16,128]{3,2,1,0:T(8,128)S(1)}, f32[16,24,128]{2,1,0:T(8,128)S(1)}, f32[13,8,8,128]{3,2,1,0:T(8,128)S(1)}, f32[13,8,8,128]{3,2,1,0:T(8,128)S(1)}, f32[256,128]{1,0:T(8,128)S(1)}) custom-call(s32[5]{0:T(128)S(1)} %stack.15.place, f32[2]{0:T(128)S(1)} %copy-done.7, f32[256,128]{1,0:T(8,128)S(1)} %bitcast.11, ...), custom_call_target="tpu_custom_call" | custom-call | tf_op jit(solution)/shard_map/pallas_call | solution.py:459
  73.3 5.1 %collective-permute-start.7 = (f32[13,8,8,128]{3,2,1,0:T(8,128)S(1)}, f32[13,8,8,128]{3,2,1,0:T(8,128)S(1)}, u32[]{:S(2)}, u32[]{:S(2)}) collective-permute-start(f32[13,8,8,128]{3,2,1,0:T(8,128)S(1)} %get-tuple-element.40), channel_id=1, source_target_pairs={{0,8},{8,16},{16,24},{24,32},{32,40},{40,48},{48,56},{56,0},{1,9},... | collective-permute-start | bytes 1277960 | tf_op jit(solution)/shard_map/ppermute | solution.py:471
  78.4 26.4 %all_to_all.22 = f32[256,1,128]{2,1,0:T(1,128)S(1)} all-to-all(f32[256,1,128]{2,1,0:T(1,128)S(1)} %bitcast.13), channel_id=1, replica_groups=mesh['gx'=4,'gy'=8,'gz'=8] {'gx','gy','gz'}, dimensions={0} | all-to-all | bytes 262144 | tf_op jit(solution)/shard_map/all_to_all | solution.py:548
  104.8 14.2 %shard_map.131 = (f32[13,2,16,128]{3,2,1,0:T(8,128)S(1)}, f32[13,2,16,128]{3,2,1,0:T(8,128)S(1)}, f32[13,2,16,128]{3,2,1,0:T(8,128)S(1)}, f32[13,2,16,128]{3,2,1,0:T(8,128)S(1)}) custom-call(s32[5]{0:T(128)S(1)} %stack.15.place, f32[2]{0:T(128)S(1)} %copy-done.7, f32[256,128]{1,0:T(8,128)S(1)} %bitcast.12, f32[13,16,16,128]{3,2,1,0:T(8,128)S(1)} %get-tuple-element.38.own, ...), custom_call_target="tpu_custom_call" | custom-call | tf_op jit(solution)/shard_map/pallas_call | solution.py:459
  119.0 0.3 collective-permute-start.9
  119.3 1.7 %collective-permute-start.10 = (f32[13,2,16,128]{3,2,1,0:T(8,128)S(1)}, f32[13,2,16,128]{3,2,1,0:T(8,128)S(1)}, u32[]{:S(2)}, u32[]{:S(2)}) collective-permute-start(f32[13,2,16,128]{3,2,1,0:T(8,128)S(1)} %get-tuple-element.44), channel_id=1, source_target_pairs={{0,128},{64,192},{128,0},{192,64},{1,129},{65,193},{129,1},{193,65... | collective-permute-start | bytes 638984 | tf_op jit(solution)/shard_map/ppermute | solution.py:479
  120.9 2.0 %collective-permute-start.11 = (f32[13,2,16,128]{3,2,1,0:T(8,128)S(1)}, f32[13,2,16,128]{3,2,1,0:T(8,128)S(1)}, u32[]{:S(2)}, u32[]{:S(2)}) collective-permute-start(f32[13,2,16,128]{3,2,1,0:T(8,128)S(1)} %get-tuple-element.45), channel_id=1, source_target_pairs={{0,192},{64,128},{128,64},{192,0},{1,193},{65,129},{129,65},{193,1... | collective-permute-start | bytes 638984 | tf_op jit(solution)/shard_map/ppermute | solution.py:479
  122.9 1.9 %collective-permute-done.9.from1 = f32[13,2,16,128]{3,2,1,0:T(8,128)S(1)} collective-permute-done((f32[13,2,16,128]{3,2,1,0:T(8,128)S(1)}, f32[13,2,16,128]{3,2,1,0:T(8,128)S(1)}, u32[]{:S(2)}, u32[]{:S(2)}) %collective-permute-start.9) | collective-permute-done | bytes 213024 | tf_op jit(solution)/shard_map/ppermute | solution.py:479
  124.8 4.8 %collective-permute-done.10.from2 = f32[13,2,16,128]{3,2,1,0:T(8,128)S(1)} collective-permute-done((f32[13,2,16,128]{3,2,1,0:T(8,128)S(1)}, f32[13,2,16,128]{3,2,1,0:T(8,128)S(1)}, u32[]{:S(2)}, u32[]{:S(2)}) %collective-permute-start.10) | collective-permute-done | bytes 213024 | tf_op jit(solution)/shard_map/ppermute | solution.py:479
  129.6 3.1 %collective-permute-done.11.from3 = f32[13,2,16,128]{3,2,1,0:T(8,128)S(1)} collective-permute-done((f32[13,2,16,128]{3,2,1,0:T(8,128)S(1)}, f32[13,2,16,128]{3,2,1,0:T(8,128)S(1)}, u32[]{:S(2)}, u32[]{:S(2)}) %collective-permute-start.11) | collective-permute-done | bytes 213024 | tf_op jit(solution)/shard_map/ppermute | solution.py:479
  132.7 1.6 %shard_map.132 = (f32[4,16,256]{2,1,0:T(8,128)}, f32[4,16,256]{2,1,0:T(8,128)}, f32[3,4,16,256]{3,2,1,0:T(8,128)}, f32[4,16,256]{2,1,0:T(8,128)}, f32[4,16,256]{2,1,0:T(8,128)}, /*index=5*/f32[6,4,16,256]{3,2,1,0:T(8,128)}) custom-call(s32[5]{0:T(128)S(1)} %stack.15.place, f32[13,2,16,128]{3,2,1,0:T(8,128)S(1)} %get-tuple-element.42.mine, ...), custom_call_target="tpu_custom_call" | custom-call | tf_op jit(solution)/shard_map/pallas_call | solution.py:459
  (18 shorter events, 0.1 us)
Async XLA Ops:
  0.7 1.0 copy-start
  1.7 0.9 copy-start.1
  2.6 0.8 copy-start.2
  3.5 0.8 copy-start.3
  4.3 0.8 copy-start.4
  5.2 0.8 copy-start.5
  6.0 0.8 copy-start.6
  8.5 48.2 %copy-start.7 = (f32[2]{0:T(128)S(1)}, f32[2]{0:T(128)}, u32[]{:S(2)}) copy-start(f32[2]{0:T(128)} %timestep.3) | copy-start | bytes 28
  8.5 6.2 %collective-permute-start = (f32[14,2,16,128]{3,2,1,0:T(8,128)S(1)}, f32[14,2,16,128]{3,2,1,0:T(8,128)S(1)}, u32[]{:S(2)}, u32[]{:S(2)}) collective-permute-start(f32[14,2,16,128]{3,2,1,0:T(8,128)S(1)} %get-tuple-element.28), channel_id=1, source_target_pairs={{0,64},{64,0},{128,192},{192,128},{1,65},{65,1},{129,193},{193,129... | collective-permute-start | bytes 688136 | tf_op jit(solution)/shard_map/ppermute | solution.py:479
  10.7 12.6 %collective-permute-start.1 = (f32[14,2,16,128]{3,2,1,0:T(8,128)S(1)}, f32[14,2,16,128]{3,2,1,0:T(8,128)S(1)}, u32[]{:S(2)}, u32[]{:S(2)}) collective-permute-start(f32[14,2,16,128]{3,2,1,0:T(8,128)S(1)} %get-tuple-element.29), channel_id=1, source_target_pairs={{0,128},{64,192},{128,0},{192,64},{1,129},{65,193},{129,1},{193,65... | collective-permute-start | bytes 688136 | tf_op jit(solution)/shard_map/ppermute | solution.py:479
  13.3 12.3 %collective-permute-start.2 = (f32[14,2,16,128]{3,2,1,0:T(8,128)S(1)}, f32[14,2,16,128]{3,2,1,0:T(8,128)S(1)}, u32[]{:S(2)}, u32[]{:S(2)}) collective-permute-start(f32[14,2,16,128]{3,2,1,0:T(8,128)S(1)} %get-tuple-element.30), channel_id=1, source_target_pairs={{0,192},{64,128},{128,64},{192,0},{1,193},{65,129},{129,65},{193,1... | collective-permute-start | bytes 688136 | tf_op jit(solution)/shard_map/ppermute | solution.py:479
  26.5 17.3 %collective-permute-start.3 = (f32[14,4,8,128]{3,2,1,0:T(8,128)S(1)}, f32[14,4,8,128]{3,2,1,0:T(8,128)S(1)}, u32[]{:S(2)}, u32[]{:S(2)}) collective-permute-start(f32[14,4,8,128]{3,2,1,0:T(8,128)S(1)} %get-tuple-element.32), channel_id=1, source_target_pairs={{0,8},{8,16},{16,24},{24,32},{32,40},{40,48},{48,56},{56,0},{1,9},... | collective-permute-start | bytes 688136 | tf_op jit(solution)/shard_map/ppermute | solution.py:471
  31.3 12.5 %collective-permute-start.4 = (f32[14,4,8,128]{3,2,1,0:T(8,128)S(1)}, f32[14,4,8,128]{3,2,1,0:T(8,128)S(1)}, u32[]{:S(2)}, u32[]{:S(2)}) collective-permute-start(f32[14,4,8,128]{3,2,1,0:T(8,128)S(1)} %get-tuple-element.33), channel_id=1, source_target_pairs={{8,0},{16,8},{24,16},{32,24},{40,32},{48,40},{56,48},{0,56},{9,1},... | collective-permute-start | bytes 688136 | tf_op jit(solution)/shard_map/ppermute | solution.py:472
  31.3 25.3 %all-to-all-start = ((f32[256,1,128]{2,1,0:T(1,128)}), f32[256,1,128]{2,1,0:T(1,128)S(1)}, u32[]{:S(2)}, u32[]{:S(2)}) async-start(f32[256,1,128]{2,1,0:T(1,128)} %bitcast.4), calls=%async_computation | async-start | bytes 262144 | tf_op jit(solution)/shard_map/all_to_all | solution.py:500
  47.1 9.7 %collective-permute-start.5 = (f32[16,24,128]{2,1,0:T(8,128)}, f32[16,24,128]{2,1,0:T(8,128)S(1)}, u32[]{:S(2)}, u32[]{:S(2)}) collective-permute-start(f32[16,24,128]{2,1,0:T(8,128)} %get-tuple-element.35), channel_id=1, source_target_pairs={{0,64},{64,128},{128,192},{192,1},{1,65},{65,129},{129,193},{193,2... | collective-permute-start | bytes 589832 | tf_op jit(solution)/shard_map/ppermute | solution.py:471
  48.5 8.3 %collective-permute-start.6 = (f32[16,24,128]{2,1,0:T(8,128)S(1)}, f32[16,24,128]{2,1,0:T(8,128)S(1)}, u32[]{:S(2)}, u32[]{:S(2)}) collective-permute-start(f32[16,24,128]{2,1,0:T(8,128)S(1)} %get-tuple-element.36), channel_id=1, source_target_pairs={{64,0},{128,64},{192,128},{1,192},{65,1},{129,65},{193,129},{2,193... | collective-permute-start | bytes 589832 | tf_op jit(solution)/shard_map/ppermute | solution.py:472
  73.3 31.5 %collective-permute-start.7 = (f32[13,8,8,128]{3,2,1,0:T(8,128)S(1)}, f32[13,8,8,128]{3,2,1,0:T(8,128)S(1)}, u32[]{:S(2)}, u32[]{:S(2)}) collective-permute-start(f32[13,8,8,128]{3,2,1,0:T(8,128)S(1)} %get-tuple-element.40), channel_id=1, source_target_pairs={{0,8},{8,16},{16,24},{24,32},{32,40},{40,48},{48,56},{56,0},{1,9},... | collective-permute-start | bytes 1277960 | tf_op jit(solution)/shard_map/ppermute | solution.py:471
  78.4 26.4 %collective-permute-start.8 = (f32[13,8,8,128]{3,2,1,0:T(8,128)S(1)}, f32[13,8,8,128]{3,2,1,0:T(8,128)S(1)}, u32[]{:S(2)}, u32[]{:S(2)}) collective-permute-start(f32[13,8,8,128]{3,2,1,0:T(8,128)S(1)} %get-tuple-element.41), channel_id=1, source_target_pairs={{8,0},{16,8},{24,16},{32,24},{40,32},{48,40},{56,48},{0,56},{9,1},... | collective-permute-start | bytes 1277960 | tf_op jit(solution)/shard_map/ppermute | solution.py:472
  119.0 5.8 %collective-permute-start.9 = (f32[13,2,16,128]{3,2,1,0:T(8,128)S(1)}, f32[13,2,16,128]{3,2,1,0:T(8,128)S(1)}, u32[]{:S(2)}, u32[]{:S(2)}) collective-permute-start(f32[13,2,16,128]{3,2,1,0:T(8,128)S(1)} %get-tuple-element.43), channel_id=1, source_target_pairs={{0,64},{64,0},{128,192},{192,128},{1,65},{65,1},{129,193},{193,129... | collective-permute-start | bytes 638984 | tf_op jit(solution)/shard_map/ppermute | solution.py:479
  119.3 10.4 %collective-permute-start.10 = (f32[13,2,16,128]{3,2,1,0:T(8,128)S(1)}, f32[13,2,16,128]{3,2,1,0:T(8,128)S(1)}, u32[]{:S(2)}, u32[]{:S(2)}) collective-permute-start(f32[13,2,16,128]{3,2,1,0:T(8,128)S(1)} %get-tuple-element.44), channel_id=1, source_target_pairs={{0,128},{64,192},{128,0},{192,64},{1,129},{65,193},{129,1},{193,65... | collective-permute-start | bytes 638984 | tf_op jit(solution)/shard_map/ppermute | solution.py:479
  120.9 11.8 %collective-permute-start.11 = (f32[13,2,16,128]{3,2,1,0:T(8,128)S(1)}, f32[13,2,16,128]{3,2,1,0:T(8,128)S(1)}, u32[]{:S(2)}, u32[]{:S(2)}) collective-permute-start(f32[13,2,16,128]{3,2,1,0:T(8,128)S(1)} %get-tuple-element.45), channel_id=1, source_target_pairs={{0,192},{64,128},{128,64},{192,0},{1,193},{65,129},{129,65},{193,1... | collective-permute-start | bytes 638984 | tf_op jit(solution)/shard_map/ppermute | solution.py:479

commit v2 on v1

v2 whole, which is shorter than its diff:
```python
import jax
import jax.numpy as jnp
from jax import lax
from jax.experimental import pallas as pl
from jax.experimental.pallas import tpu as pltpu
from jax.sharding import PartitionSpec as P


FIELDS = 13
PLANES = 16
ROWS = 24
OWN = 16
LANES = 128
HALF = 64
PAD = 2

shear_table = (1.0, 0.5, 0.8)
sound_table = (1.5, 1.2, 1.0)
gruneisen_table = (2.0, 2.1, 1.9)
rest_table = (4.0, 3.0, 5.0)
yield_table = (0.3, 0.2, 0.25)
harden_table = (0.5, 0.3, 0.4)
exponent_table = (0.3, 0.4, 0.35)
rate_table = (0.02, 0.015, 0.01)
cfl_number = 0.2

PACK_LIMIT = 62 * 1024 * 1024
ACROSS = ((0, 3, 5), (3, 1, 4), (5, 4, 2))


def roll(value, shift, axis):
    shift = shift % value.shape[axis]
    return value if shift == 0 else pltpu.roll(value, shift, axis)


def position():
    size_x = lax.axis_size("gx")
    place_x = lax.axis_index("gx")
    chunk = lax.axis_index("gz") * size_x + place_x
    return place_x, lax.axis_index("gy"), chunk, lax.axis_size("gy") - 1, size_x * lax.axis_size("gz") - 1


def iota(shape, axis):
    return lax.broadcasted_iota(jnp.int32, shape, axis)


def inverse(value):
    guess = pl.reciprocal(value, approx=True)
    return guess * (2.0 - value * guess)


def pick(first, second, table):
    return jnp.where(first, table[0], jnp.where(second, table[1], table[2]))


def stack_rows(even, odd, upper):
    low_rows = iota((8, LANES), 0) < 4
    if upper:
        return jnp.where(low_rows, roll(even[8:], 4, 0), odd[8:])
    return jnp.where(low_rows, even[:8], roll(odd[:8], 4, 0))


def halo_tile(high, low, odd):
    low_rows = iota((8, LANES), 0) < 4
    if odd:
        return jnp.where(low_rows, roll(high, 4, 0), low)
    return jnp.where(low_rows, high, roll(low, 4, 0))


PART_ROWS = (FIELDS + 1) * 2 * OWN


def part_rows(f, j):
    return slice((2 * f + j) * OWN, (2 * f + j + 1) * OWN)


def pack_kernel(*args):
    sources, (own, to1, to2, to3, edges, z_up, z_down) = args[:7], args[7:14]
    buffers, arrived = args[14:21], args[21]
    copies = [
        pltpu.make_async_copy(source, buffer, arrived.at[i])
        for i, (source, buffer) in enumerate(zip(sources, buffers))
    ]
    for copy in copies:
        copy.start()
    for copy in copies:
        copy.wait()
    dens, ener, vel, plas, dama, devi, mat = buffers
    me = position()[0]
    refs = [dens, ener] + [vel.at[i] for i in range(3)] + [plas, dama]
    refs = refs + [devi.at[i] for i in range(6)] + [mat]
    peak = None
    for x in range(4):
        for t in range(2):
            cols = slice(t * LANES, (t + 1) * LANES)
            speed = jnp.maximum(jnp.abs(vel[0, x, :, cols]), jnp.abs(vel[1, x, :, cols]))
            speed = jnp.maximum(speed, jnp.abs(vel[2, x, :, cols]))
            kind = mat[x, :, cols]
            speed = speed + pick(kind == 0, kind == 1, sound_table)
            peak = speed if peak is None else jnp.maximum(peak, speed)
    peak = jnp.full((8, LANES), jnp.max(peak), jnp.float32)
    left = iota((OWN, LANES), 1) < HALF
    for k, out in enumerate((own, to1, to2, to3)):
        out[PART_ROWS:] = peak
        target = me ^ k
        cols = pl.ds(pl.multiple_of((target >> 1) * LANES, LANES), LANES)
        odd = target & 1
        for f in range(FIELDS + 1):
            for j in range(2):
                even_plane = refs[f][2 * j, :, cols].astype(jnp.float32)
                odd_plane = refs[f][2 * j + 1, :, cols].astype(jnp.float32)
                out[part_rows(f, j)] = jnp.where(
                    left,
                    pltpu.roll(even_plane, odd * HALF, 1),
                    pltpu.roll(odd_plane, (1 - odd) * HALF, 1),
                )


    group = iota((OWN, LANES), 1) >> 3

    def plane(x, carry):
        zero = jnp.zeros((OWN, LANES), jnp.float32)
        below, above = [zero] * 5, [zero] * 5
        for f in range(FIELDS + 1):
            in_below, in_above = group == (f + 7) % 16, group == f
            for t in range(2):
                tile = refs[f][x, :, t * LANES : (t + 1) * LANES].astype(jnp.float32)
                near, far = roll(tile, 8 * f, 1), roll(tile, 8 * f - HALF, 1)
                below[2 * t + 1] = jnp.where(in_below, near, below[2 * t + 1])
                below[2 * t + 2] = jnp.where(in_below, far, below[2 * t + 2])
                above[2 * t] = jnp.where(in_above, near, above[2 * t])
                above[2 * t + 1] = jnp.where(in_above, far, above[2 * t + 1])
        for g in range(4):
            edges[g, 0, x] = below[g]
            edges[g, 1, x] = above[g + 1]
        z_up[x] = below[4]
        z_down[x] = above[0]
        return carry

    lax.fori_loop(0, 4, plane, 0)


def edge_kernel(edges, from_below, from_above, own, to1, to2, to3):
    me = position()[0]
    for k, out in enumerate((own, to1, to2, to3)):
        target = me ^ k
        out[0] = jnp.where(target == 0, from_below[...], edges[target, 0])
        out[1] = jnp.where(target == 3, from_above[...], edges[target, 1])


MAIN_TILES = (FIELDS + 1) * 4


def spread_kernel(own, from1, from2, from3, own_z, z1, z2, z3, state, sides, up, down, top):
    me = position()[0]
    peak = jnp.maximum(
        jnp.maximum(own[PART_ROWS:], from1[PART_ROWS:]), jnp.maximum(from2[PART_ROWS:], from3[PART_ROWS:])
    )
    top[...] = jnp.broadcast_to(peak[:1], top.shape)
    for k, (src, side) in enumerate(((own, own_z), (from1, z1), (from2, z2), (from3, z3))):
        block = me ^ k
        for f in range(FIELDS + 1):
            first, second = src[part_rows(f, 0)], src[part_rows(f, 1)]
            state[f, 4 * block] = first
            state[f, 4 * block + 1] = roll(first, HALF, 1)
            state[f, 4 * block + 2] = second
            state[f, 4 * block + 3] = roll(second, HALF, 1)
            up[4 * f + block] = stack_rows(first, second, True)
            down[4 * f + block] = stack_rows(first, second, False)
        for which in range(2):
            for j in range(2):
                even, odd = side[which, 2 * j], side[which, 2 * j + 1]
                sides[which, 4 * block + 2 * j] = even
                sides[which, 4 * block + 2 * j + 1] = odd
                at = MAIN_TILES + 8 * which + 2 * block + j
                up[at] = stack_rows(even, odd, True)
                down[at] = stack_rows(even, odd, False)


def set_masks(width, inside, face_y, face_z):
    _, place_y, chunk, last_y, last_chunk = position()
    shape = (ROWS, LANES)
    row, lane = iota(shape, 0), iota(shape, 1)
    row_ok = (row < OWN) | ((row < OWN + 4) & (place_y < last_y)) | ((row >= OWN + 4) & (place_y > 0))
    lane_ok = (
        (lane < HALF)
        | ((lane < HALF + width) & (chunk < last_chunk))
        | ((lane >= LANES - width) & (chunk > 0))
    )
    ok = jnp.where(row_ok & lane_ok, 1.0, 0.0)
    inside[...] = ok
    face_y[...] = ok * roll(ok, -1, 0)
    face_z[...] = ok * roll(ok, -1, 1)


def step_size(step_no, timestep, tops):
    top_speed = jnp.max(tops[...], axis=0, keepdims=True)
    asked = timestep[step_no]
    return asked / (1.0 + asked * top_speed / cfl_number)


def central(upper, lower):
    return 0.5 * (upper - lower)


def limited(back, fore):
    product = back * fore
    return jnp.where(product > 0.0, product * inverse(back + fore), 0.0)


def carried(positive, here, there, slope_here, slope_there, courant, weight):
    return courant * (
        jnp.where(positive, here, there) + weight * jnp.where(positive, slope_here, slope_there)
    )


def weigh(courant):
    return jnp.where(courant > 0.0, 1.0, -1.0) - courant


def rolled_change(q, positive, courant, weight, axis):
    q_next = roll(q, -1, axis)
    fore = q_next - q
    slope = limited(roll(fore, 1, axis), fore)
    flux = carried(positive, q, q_next, slope, roll(slope, -1, axis), courant, weight)
    return q - (flux - roll(flux, 1, axis))


def rolled_courant(dt, density, momentum, closed, axis):
    velocity = momentum * inverse(density)
    return dt * 0.5 * (velocity + roll(velocity, -1, axis)) * closed


def strain_pass(dt, state, stress, rest, inside):
    def strain_plane(p, carry):
        at = p + PAD
        ok = inside[...] > 0.0
        vel = [state[2 + i, at] for i in range(3)]
        grad = [
            [
                central(state[2 + i, at + 1], state[2 + i, at - 1]),
                central(roll(vel[i], -1, 0), roll(vel[i], 1, 0)),
                central(roll(vel[i], -1, 1), roll(vel[i], 1, 1)),
            ]
            for i in range(3)
        ]
        third_div = (grad[0][0] + grad[1][1] + grad[2][2]) * (1.0 / 3.0)
        strain = [
            grad[0][0] - third_div,
            grad[1][1] - third_div,
            grad[2][2] - third_div,
            0.5 * (grad[0][1] + grad[1][0]),
            0.5 * (grad[1][2] + grad[2][1]),
            0.5 * (grad[0][2] + grad[2][0]),
        ]
        kind = state[FIELDS, at]
        first, second = kind == 0.0, kind == 1.0
        density, energy = state[0, at], state[1, at]
        plastic, damage = state[5, at], state[6, at]
        pressure = (
            pick(first, second, tuple(c * c for c in sound_table))
            * (density - pick(first, second, rest_table))
            + pick(first, second, gruneisen_table) * density * energy
        )
        shear_dt = pick(first, second, tuple(2.0 * g for g in shear_table)) * dt
        trial = [state[7 + k, at] + shear_dt * strain[k] for k in range(6)]
        trial_sq = (
            trial[0] * trial[0]
            + trial[1] * trial[1]
            + trial[2] * trial[2]
            + 2.0 * (trial[3] * trial[3] + trial[4] * trial[4] + trial[5] * trial[5])
        )
        strain_sq = (
            strain[0] * strain[0]
            + strain[1] * strain[1]
            + strain[2] * strain[2]
            + 2.0 * (strain[3] * strain[3] + strain[4] * strain[4] + strain[5] * strain[5])
        )
        equivalent = jnp.sqrt(1.5 * trial_sq)
        strain_rate = jnp.sqrt(strain_sq * (2.0 / 3.0))
        hardened = pick(first, second, yield_table) + pick(first, second, harden_table) * jnp.exp(
            pick(first, second, exponent_table) * jnp.log(plastic)
        )
        flow = (
            hardened
            * (1.0 + pick(first, second, rate_table) * jnp.log(1.0 + strain_rate))
            * (1.0 - damage)
        )
        bound = jnp.maximum(equivalent, flow)
        per_bound = inverse(bound)
        factor = flow * per_bound
        increment = (bound - flow) * pick(first, second, tuple(1.0 / (3.0 * g) for g in shear_table))
        triaxial = jnp.clip(-pressure * per_bound, -1.5, 1.5)
        failure = 0.05 + 0.8 * jnp.exp(-1.5 * triaxial)
        rest[1, p] = jnp.where(ok, density * (plastic + increment), 0.0)
        worn = jnp.minimum(damage + increment * inverse(failure), 0.9)
        rest[2, p] = jnp.where(ok, density * worn, 0.0)
        dev = [jnp.where(ok, trial[k] * factor, 0.0) for k in range(6)]
        held = jnp.where(ok, pressure, 0.0)
        full = [dev[0] - held, dev[1] - held, dev[2] - held, dev[3], dev[4], dev[5]]
        for k in range(6):
            rest[3 + k, p] = density * dev[k]
            stress[k, p + 1] = full[k]
        work = (
            full[0] * grad[0][0]
            + full[1] * grad[1][1]
            + full[2] * grad[2][2]
            + 2.0 * (full[3] * strain[3] + full[4] * strain[4] + full[5] * strain[5])
        )
        rest[0, p] = jnp.where(ok, density * energy + dt * work, 0.0)
        return carry

    zero = jnp.zeros((ROWS, LANES), jnp.float32)
    for k in range(6):
        stress[k, 0] = zero
        stress[k, PLANES + 1] = zero
    lax.fori_loop(0, PLANES, strain_plane, 0)


def force_pass(dt, state, stress, lead, inside):
    def force_plane(p, carry):
        at = p + PAD
        density = state[0, at]
        here = [stress[k, p + 1] for k in range(6)]
        lead[0, p] = density
        for i in range(3):
            along_x, along_y, along_z = ACROSS[0][i], ACROSS[1][i], ACROSS[2][i]
            force = (
                central(stress[along_x, p + 2], stress[along_x, p])
                + central(roll(here[along_y], -1, 0), roll(here[along_y], 1, 0))
                + central(roll(here[along_z], -1, 1), roll(here[along_z], 1, 1))
            )
            lead[1 + i, p] = density * state[2 + i, at] + jnp.where(inside[...] > 0.0, dt * force, 0.0)
        return carry

    lax.fori_loop(0, PLANES, force_plane, 0)


def first_sweep(fields, moved, courants):
    def field(f, carry):
        here = fields[f, 0]
        ahead = fields[f, 1]
        fore = ahead - here
        slope = limited(here, fore)
        last_flux = None
        for p in range(PLANES - 1):
            further = fields[f, p + 2] if p + 2 < PLANES else 0.0
            next_fore = further - ahead
            next_slope = limited(fore, next_fore)
            courant = courants[p]
            flux = carried(courant > 0.0, here, ahead, slope, next_slope, courant, weigh(courant))
            moved[f, p] = here - (flux if last_flux is None else flux - last_flux)
            last_flux, here, ahead, fore, slope = flux, ahead, further, next_fore, next_slope
        moved[f, PLANES - 1] = here + last_flux
        return carry

    lax.fori_loop(0, fields.shape[0], field, 0)


def first_courants(dt, lead, courants, inside):
    ok = inside[...] > 0.0
    here = None
    for p in range(PLANES):
        ahead = lead[1, p] * inverse(jnp.where(ok, lead[0, p], 1.0))
        if p > 0:
            courants[p - 1] = dt * 0.5 * (here + ahead)
        here = ahead


def later_sweeps(count, moved, mids, second_courant, third_courant, finish):
    def second(p, mid):
        courant = second_courant(p)
        positive, weight = courant > 0.0, weigh(courant)
        for f in range(count):
            mid[f] = rolled_change(moved[f, p], positive, courant, weight, 0)[:OWN]
            yield

    def third(p, mid):
        courant = third_courant(p, mid)
        positive, weight = courant > 0.0, weigh(courant)
        scale = None
        for f in range(count):
            value = rolled_change(mid[f], positive, courant, weight, 1)
            scale = finish(p, f, value, scale)
            yield

    def beside(*parts):
        for _ in zip(*parts):
            pass

    def pair(i, carry):
        beside(second(2 * i + 1, mids.at[1]), third(2 * i, mids.at[0]))
        beside(second(jnp.minimum(2 * i + 2, PLANES - 1), mids.at[0]), third(2 * i + 1, mids.at[1]))
        return carry

    beside(second(0, mids.at[0]))
    lax.fori_loop(0, PLANES // 2, pair, 0)


LEAD = 4
REST = 9
LEAD_AT = (0, 2, 3, 4)
REST_AT = (1, 5, 6, 7, 8, 9, 10, 11, 12)


def sweep_lead(dt, lead, moved, mids, courants, scales, inside, face_y, face_z, put):
    along_x, along_y, along_z = courants
    first_courants(dt, lead, along_x, inside)
    first_sweep(lead, moved, along_x)

    def second_courant(p):
        density = jnp.where(inside[...] > 0.0, moved[0, p], 1.0)
        courant = rolled_courant(dt, density, moved[2, p], face_y[...], 0)
        along_y[p] = courant
        return courant

    def third_courant(p, mid):
        density = jnp.where(inside[:OWN] > 0.0, mid[0], 1.0)
        courant = rolled_courant(dt, density, mid[3], face_z[:OWN], 1)
        along_z[p] = courant
        return courant

    def finish(p, f, value, scale):
        if f == 0:
            ok = inside[:OWN] > 0.0
            scale = jnp.where(ok, inverse(jnp.where(ok, value, 1.0)), 0.0)
            scales[p] = scale
            put(0, p, jnp.where(ok, value, 0.0))
        else:
            put(f, p, value * scale)
        return scale

    later_sweeps(LEAD, moved, mids, second_courant, third_courant, finish)


def sweep_rest(rest, moved, mids, courants, scales, put):
    along_x, along_y, along_z = courants
    first_sweep(rest, moved, along_x)

    def finish(p, f, value, scale):
        put(f, p, value * scales[p])

    later_sweeps(REST, moved, mids, lambda p: along_y[p], lambda p, mid: along_z[p], finish)


def clear_ends(state):
    zero = jnp.zeros((ROWS, LANES), jnp.float32)
    for f in range(FIELDS + 1):
        for p in (0, 1, PLANES + PAD, PLANES + PAD + 1):
            state[f, p] = zero


def lead_kernel(
    timestep, tops, own, sides, low, high, out, rest, along_x, along_y, along_z, scales, kinds, top,
    state, stress, lead, moved, mids, inside, face_y, face_z,
):
    set_masks(8, inside, face_y, face_z)
    clear_ends(state)
    dt = step_size(0, timestep, tops)

    def gather(block, carry):
        ok = inside[...] > 0.0
        lane = iota((ROWS, LANES), 1)
        group = lane >> 3
        for j in range(2):
            around = []
            for odd in range(2):
                p = 4 * block + 2 * j + odd
                for which in range(2):
                    at = MAIN_TILES + 8 * which + 2 * block + j
                    tile = halo_tile(high[at], low[at], odd == 1)
                    around.append(jnp.concatenate([sides[which, p], tile], axis=0))
            for f in range(FIELDS + 1):
                tile = halo_tile(high[4 * f + block], low[4 * f + block], j == 1)
                for odd in range(2):
                    p = 4 * block + 2 * j + odd
                    below, above = around[2 * odd], around[2 * odd + 1]
                    value = jnp.concatenate([own[f, p], roll(tile, HALF * odd, 1)], axis=0)
                    side = roll(jnp.where(group == f, above, below), HALF - 8 * f, 1)
                    value = jnp.where(ok, jnp.where(lane < HALF, value, side), 0.0)
                    state[f, p + PAD] = value
                    if f == FIELDS:
                        kinds[p] = value
        return carry

    lax.fori_loop(0, 4, gather, 0)
    strain_pass(dt, state, stress, rest, inside)
    force_pass(dt, state, stress, lead, inside)

    def put(f, p, value):
        out[f, p] = value

    sweep_lead(
        dt, lead, moved, mids, (along_x, along_y, along_z), scales, inside, face_y, face_z, put
    )

    def peaks(p, peak):
        speed = jnp.maximum(jnp.abs(out[1, p]), jnp.abs(out[2, p]))
        speed = jnp.maximum(speed, jnp.abs(out[3, p]))
        kind = kinds[p, :OWN]
        speed = speed + pick(kind == 0.0, kind == 1.0, sound_table)
        lane = iota((OWN, LANES), 1)
        return jnp.maximum(peak, jnp.where(lane < HALF, speed, 0.0))

    peak = lax.fori_loop(0, PLANES, peaks, jnp.zeros((OWN, LANES), jnp.float32))
    top[...] = jnp.full(top.shape, jnp.max(peak), jnp.float32)


def rest_kernel(lead, rest, along_x, along_y, along_z, scales, out, up, down, moved, mids):
    def put(f, p, value):
        out[f, p] = value

    sweep_rest(rest, moved, mids, (along_x, along_y, along_z), scales, put)

    def messages(i, carry):
        for f in range(FIELDS):
            src, at = (lead, LEAD_AT.index(f)) if f in LEAD_AT else (out, REST_AT.index(f))
            even, odd = src[at, 2 * i], src[at, 2 * i + 1]
            up[f, i] = stack_rows(even, odd, True)
            down[f, i] = stack_rows(even, odd, False)
        return carry

    lax.fori_loop(0, PLANES // 2, messages, 0)


def second_kernel(
    timestep, tops, own_lead, own_rest, kinds, low, high, mine, to1, to2, to3,
    state, stress, lead, moved, mids, inside, face_y, face_z,
    rest, rest_moved, rest_mids, along_x, along_y, along_z, scales, out,
):
    set_masks(4, inside, face_y, face_z)
    clear_ends(state)
    dt = step_size(1, timestep, tops)

    def gather(i, carry):
        ok = inside[...] > 0.0
        for f in range(FIELDS):
            src, at = (own_lead, LEAD_AT.index(f)) if f in LEAD_AT else (own_rest, REST_AT.index(f))
            for odd in range(2):
                p = 2 * i + odd
                tile = halo_tile(high[f, i], low[f, i], odd == 1)
                value = jnp.concatenate([src[at, p], tile], axis=0)
                state[f, p + PAD] = jnp.where(ok, value, 0.0)
        for odd in range(2):
            state[FIELDS, 2 * i + odd + PAD] = kinds[2 * i + odd]
        return carry

    lax.fori_loop(0, PLANES // 2, gather, 0)
    strain_pass(dt, state, stress, rest, inside)
    force_pass(dt, state, stress, lead, inside)
    courants = (along_x, along_y, along_z)

    def put_lead(f, p, value):
        out[LEAD_AT[f], p] = value

    def put_rest(f, p, value):
        out[REST_AT[f], p] = value

    sweep_lead(dt, lead, moved, mids, courants, scales, inside, face_y, face_z, put_lead)
    sweep_rest(rest, rest_moved, rest_mids, courants, scales, put_rest)

    left = iota((OWN, LANES), 1) < HALF
    for k, dest in enumerate((mine, to1, to2, to3)):
        block = position()[0] ^ k
        for f in range(FIELDS):
            for j in range(2):
                even, odd = out[f, 4 * block + 2 * j], out[f, 4 * block + 2 * j + 1]
                dest[f, j] = jnp.where(left, even, roll(odd, HALF, 1))


def unpack_kernel(mine, from1, from2, from3, dens, ener, vel, plas, dama, devi, held):
    me = position()[0]
    refs = [dens, ener] + [vel.at[i] for i in range(3)] + [plas, dama]
    refs = refs + [devi.at[i] for i in range(6)]
    for k, src in enumerate((mine, from1, from2, from3)):
        held[me ^ k] = src[...]
    left = iota((OWN, LANES), 1) < HALF
    for f in range(FIELDS):
        for j in range(2):
            for t in range(2):
                first, second = held[2 * t, f, j], held[2 * t + 1, f, j]
                cols = slice(t * LANES, (t + 1) * LANES)
                refs[f][2 * j, :, cols] = jnp.where(left, first, roll(second, HALF, 1))
                refs[f][2 * j + 1, :, cols] = jnp.where(left, roll(first, HALF, 1), second)


IN_VMEM = pl.BlockSpec(memory_space=pltpu.VMEM)
IN_SMEM = pl.BlockSpec(memory_space=pltpu.SMEM)


def call(kernel, scalars, outs, scratch, *args):
    return pl.pallas_call(
        kernel,
        out_shape=[jax.ShapeDtypeStruct(shape, jnp.float32) for shape in outs],
        in_specs=[IN_SMEM] * scalars + [IN_VMEM] * (len(args) - scalars),
        out_specs=[IN_VMEM] * len(outs),
        scratch_shapes=[pltpu.VMEM(shape, jnp.float32) for shape in scratch],
        compiler_params=pltpu.CompilerParams(vmem_limit_bytes=48 * 1024 * 1024),
    )(*args)


def ring_pair(to_next, to_last, axes, order):
    after = order[1:] + order[:1]
    low = lax.ppermute(to_next, axes, list(zip(order, after)))
    high = lax.ppermute(to_last, axes, list(zip(after, order)))
    return low, high


def swap_blocks(parts):
    count = lax.axis_size("gx")
    return [
        lax.ppermute(part, "gx", [(i, i ^ (k + 1)) for i in range(count)])
        for k, part in enumerate(parts)
    ]


def shards(density, energy, velocity, plastic_strain, damage, deviator, materials, timestep):
    size_y, size_z = lax.axis_size("gy"), lax.axis_size("gz")
    all_fields = FIELDS + 1
    part = (PART_ROWS + 8, LANES)
    inputs = (density, energy, velocity, plastic_strain, damage, deviator, materials)
    edge = (4, OWN, LANES)
    own, *parts, edges, z_up, z_down = pl.pallas_call(
        pack_kernel,
        out_shape=[
            jax.ShapeDtypeStruct(shape, jnp.float32) for shape in [part] * 4 + [(4, 2) + edge, edge, edge]
        ],
        in_specs=[pl.BlockSpec(memory_space=pltpu.HBM)] * len(inputs),
        out_specs=[IN_VMEM] * 7,
        scratch_shapes=[pltpu.VMEM(array.shape, array.dtype) for array in inputs]
        + [pltpu.SemaphoreType.DMA((len(inputs),))],
        compiler_params=pltpu.CompilerParams(vmem_limit_bytes=PACK_LIMIT),
    )(*inputs)
    z_low, z_high = ring_pair(z_up, z_down, "gz", list(range(size_z)))
    parts = swap_blocks(parts)
    own_z, *z_parts = call(edge_kernel, 0, [(2,) + edge] * 4, [], edges, z_low, z_high)
    z_parts = swap_blocks(z_parts)
    message = (MAIN_TILES + PLANES, 8, LANES)
    state, sides, up, down, top = call(
        spread_kernel,
        0,
        [(all_fields, PLANES, OWN, LANES), (2, PLANES, OWN, LANES), message, message]
        + [(size_y * size_z, LANES)],
        [],
        own,
        *parts,
        own_z,
        *z_parts,
    )
    low, high = ring_pair(up, down, "gy", list(range(size_y)))
    tops = lax.all_to_all(top, ("gy", "gz"), 0, 0)
    full = (ROWS, LANES)
    scratch = [
        (all_fields, PLANES + 2 * PAD) + full,
        (6, PLANES + 2) + full,
        (LEAD, PLANES) + full,
        (LEAD, PLANES) + full,
        (2, LEAD, OWN, LANES),
        full,
        full,
        full,
    ]
    left_over = [
        (REST, PLANES) + full,
        (PLANES - 1,) + full,
        (PLANES,) + full,
        (PLANES, OWN, LANES),
        (PLANES, OWN, LANES),
    ]
    rest_scratch = [(REST, PLANES) + full, (2, REST, OWN, LANES)]
    lead, *rest, kinds, top = call(
        lead_kernel,
        1,
        [(LEAD, PLANES, OWN, LANES)] + left_over + [(PLANES,) + full, (8, LANES)],
        scratch,
        timestep,
        tops,
        state,
        sides,
        low,
        high,
    )
    others = swap_blocks([top] * 3)
    rest, up, down = call(
        rest_kernel,
        0,
        [(REST, PLANES, OWN, LANES)] + [(FIELDS, PLANES // 2, 8, LANES)] * 2,
        rest_scratch,
        lead,
        *rest,
    )
    low, high = ring_pair(up, down, "gy", list(range(size_y)))
    for other in others:
        top = jnp.maximum(top, other)
    tops = lax.all_to_all(jnp.broadcast_to(top[:1], (size_y * size_z, LANES)), ("gy", "gz"), 0, 0)
    mine, *parts = call(
        second_kernel,
        1,
        [(FIELDS, 2, OWN, LANES)] * 4,
        scratch + left_over[:1] + rest_scratch + left_over[1:] + [(FIELDS, PLANES, OWN, LANES)],
        timestep,
        tops,
        lead,
        rest,
        kinds,
        low,
        high,
    )
    parts = swap_blocks(parts)
    cells = density.shape
    return tuple(
        call(
            unpack_kernel,
            0,
            [cells, cells, (3,) + cells, cells, cells, (6,) + cells],
            [(4, FIELDS, 2, OWN, LANES)],
            mine,
            *parts,
        )
    )


def solution(mesh):
    cells = P("gx", "gy", "gz")
    vectors = P(None, "gx", "gy", "gz")
    return jax.shard_map(
        shards,
        mesh=mesh,
        in_specs=(cells, cells, vectors, cells, cells, vectors, cells, P()),
        out_specs=(cells, cells, vectors, cells, cells, vectors),
        check_vma=False,
    )
```

time: 135 us -> 122 us (0.904)
  blocking collectives: 26.4 us -> 38.3 us
  waiting for transfers between devices: 25.8 us -> 16.8 us
  starting transfers between devices: 37.1 us -> 29.9 us
  local copies, waits for them, and re-layouts: 6.21 us -> 1.91 us
  Pallas kernels: 38.2 us -> 34.2 us
    all_to_all x1 -> x0, starting transfers between devices: 12.5 us -> none  [shards(): tops = lax.all_to_all(top, ALL_AXES, 0, 0)]
    all_to_all x1 -> x2, blocking collectives: 26.4 us -> 38.3 us  [the longest x1 22.1 us: shards(): tops = lax.all_to_all(top, ('gy', 'gz'), 0, 0)]
    ppermute x6 -> x12, starting transfers between devices: 8.7 us -> 18.3 us  [swap_blocks(): lax.ppermute(part, 'gx', [(i, i ^ k + 1) for i in range(count)])]
    pallas_call x6, Pallas kernels: 38.2 us -> 30.6 us  [call(): pl.pallas_call(kernel, out_shape=[jax.ShapeDtypeStruct(shape, jnp.float32...]
    ppermute x6 -> x12, waiting for transfers between devices: 22.1 us -> 15.2 us  [swap_blocks(): lax.ppermute(part, 'gx', [(i, i ^ k + 1) for i in range(count)])]
    unnamed x16 -> x6, local copies, waits for them, and re-layouts: 6.12 us -> 1.89 us
    all_to_all x1 -> x0, waiting for transfers between devices: 3.53 us -> none  [shards(): tops = lax.all_to_all(top, ALL_AXES, 0, 0)]
    pallas_call x0 -> x1, Pallas kernels: none -> 3.52 us  [shards(): pl.pallas_call(pack_kernel, out_shape=[jax.ShapeDtypeStruct(shape, jnp.fl...]
  transfers between devices with their start and end apart: 13 -> 18, of which waited for: 8 -> 6; matrix products, arithmetic and copies ran while one was open for 0% -> 0% of each run, Pallas kernels for 2% -> 4%
where the time goes in v2:
time: 122 us
  blocking collectives  38.3 us (31%)
  Pallas kernels  34.2 us (28%)
  starting transfers between devices  29.9 us (25%)
  waiting for transfers between devices  16.8 us (14%)
  local copies, waits for them, and re-layouts  1.91 us (2%)
    pallas_call x6, Pallas kernels, call(): pl.pallas_call(kernel, out_shape=[jax.ShapeDtypeStruct(shape, jnp.float32...  30.6 us
    all_to_all x1, blocking collectives, shards(): tops = lax.all_to_all(top, ('gy', 'gz'), 0, 0)  22.1 us
    ppermute x12, starting transfers between devices, swap_blocks(): lax.ppermute(part, 'gx', [(i, i ^ k + 1) for i in range(count)])  18.3 us
    all_to_all x1, blocking collectives, shards(): lax.all_to_all(jnp.broadcast_to(top[:1], (size_y * size_z, LANES)), ('gy'...  16.2 us
    ppermute x12, waiting for transfers between devices, swap_blocks(): lax.ppermute(part, 'gx', [(i, i ^ k + 1) for i in range(count)])  15.2 us
    ppermute x3, starting transfers between devices, ring_pair(): low = lax.ppermute(to_next, axes, list(zip(order, after)))  9.01 us
    pallas_call x1, Pallas kernels, shards(): pl.pallas_call(pack_kernel, out_shape=[jax.ShapeDtypeStruct(shape, jnp.fl...  3.52 us
    ppermute x3, starting transfers between devices, ring_pair(): high = lax.ppermute(to_last, axes, list(zip(after, order)))  2.63 us
  transfers between devices with their start and end apart: 18, of which 6 were waited for; matrix products, arithmetic and copies ran while one was open for 0% of the time, Pallas kernels for 4%

profile of v2, /device:TPU:1, one launch (start us, length us, event | category | flops | bytes accessed | tf_op | source)
XLA Modules:
  0.0 121.8 jit_solution(4932641025306200541)
XLA Ops:
  0.6 3.5 %shard_map.127 = (f32[456,128]{1,0:T(8,128)}, f32[456,128]{1,0:T(8,128)}, f32[456,128]{1,0:T(8,128)}, f32[456,128]{1,0:T(8,128)}, f32[4,2,4,16,128]{4,3,2,1,0:T(...) custom-call(f32[4,16,256]{2,1,0:T(8,128)} %args_0_.4, f32[4,16,256]{2,1,0:T(8,128)} %args_1_.4, ...), custom_call_target="tpu_custom_call" | custom-call | tf_op jit(solution)/shard_map/pallas_call | solution.py:623
  4.2 2.2 %collective-permute-start = (f32[456,128]{1,0:T(8,128)}, f32[456,128]{1,0:T(8,128)S(1)}, u32[]{:S(2)}, u32[]{:S(2)}) collective-permute-start(f32[456,128]{1,0:T(8,128)} %get-tuple-element.38), channel_id=1, source_target_pairs={{0,64},{64,0},{128,192},{192,128},{1,65},{65,1},{129,193},{193,129... | collective-permute-start | bytes 700424 | tf_op jit(solution)/shard_map/ppermute | solution.py:612
  6.4 2.6 %collective-permute-start.1 = (f32[456,128]{1,0:T(8,128)}, f32[456,128]{1,0:T(8,128)S(1)}, u32[]{:S(2)}, u32[]{:S(2)}) collective-permute-start(f32[456,128]{1,0:T(8,128)} %get-tuple-element.39), channel_id=1, source_target_pairs={{0,128},{64,192},{128,0},{192,64},{1,129},{65,193},{129,1},{193,65... | collective-permute-start | bytes 700424 | tf_op jit(solution)/shard_map/ppermute | solution.py:612
  9.0 0.0 collective-permute-start.2
  9.0 1.2 collective-permute-start.3
  10.2 2.6 %collective-permute-start.4 = (f32[4,16,128]{2,1,0:T(8,128)}, f32[4,16,128]{2,1,0:T(8,128)S(1)}, u32[]{:S(2)}, u32[]{:S(2)}) collective-permute-start(f32[4,16,128]{2,1,0:T(8,128)} %get-tuple-element.43), channel_id=1, source_target_pairs={{1,0},{2,1},{3,2},{4,3},{5,4},{6,5},{7,6},{0,7},{9,8},{10,9},{11,1... | collective-permute-start | bytes 98312 | tf_op jit(solution)/shard_map/ppermute | solution.py:605
  12.8 1.5 %collective-permute-done.3.from_below = f32[4,16,128]{2,1,0:T(8,128)S(1)} collective-permute-done((f32[4,16,128]{2,1,0:T(8,128)}, f32[4,16,128]{2,1,0:T(8,128)S(1)}, u32[]{:S(2)}, u32[]{:S(2)}) %collective-permute-start.3) | collective-permute-done | bytes 32800 | tf_op jit(solution)/shard_map/ppermute | solution.py:604
  14.4 0.9 copy-done
  15.3 0.1 collective-permute-start.5
  15.5 3.8 %collective-permute-start.6 = (f32[2,4,16,128]{3,2,1,0:T(8,128)S(1)}, f32[2,4,16,128]{3,2,1,0:T(8,128)S(1)}, u32[]{:S(2)}, u32[]{:S(2)}) collective-permute-start(f32[2,4,16,128]{3,2,1,0:T(8,128)S(1)} %get-tuple-element.46), channel_id=1, source_target_pairs={{0,128},{64,192},{128,0},{192,64},{1,129},{65,193},{129,1},{193,65... | collective-permute-start | bytes 196616 | tf_op jit(solution)/shard_map/ppermute | solution.py:612
  19.3 0.0 collective-permute-done.5.z1
  19.3 2.2 %collective-permute-start.7 = (f32[2,4,16,128]{3,2,1,0:T(8,128)S(1)}, f32[2,4,16,128]{3,2,1,0:T(8,128)S(1)}, u32[]{:S(2)}, u32[]{:S(2)}) collective-permute-start(f32[2,4,16,128]{3,2,1,0:T(8,128)S(1)} %get-tuple-element.47), channel_id=1, source_target_pairs={{0,192},{64,128},{128,64},{192,0},{1,193},{65,129},{129,65},{193,1... | collective-permute-start | bytes 196616 | tf_op jit(solution)/shard_map/ppermute | solution.py:612
  21.5 0.2 collective-permute-done.6.z2
  21.7 3.4 %collective-permute-done.7.z3 = f32[2,4,16,128]{3,2,1,0:T(8,128)S(1)} collective-permute-done((f32[2,4,16,128]{3,2,1,0:T(8,128)S(1)}, f32[2,4,16,128]{3,2,1,0:T(8,128)S(1)}, u32[]{:S(2)}, u32[]{:S(2)}) %collective-permute-start.7) | collective-permute-done | bytes 65568 | tf_op jit(solution)/shard_map/ppermute | solution.py:612
  25.1 0.9 copy-done.1
  26.1 0.4 shard_map.129
  26.4 5.6 %collective-permute-start.8 = (f32[72,8,128]{2,1,0:T(8,128)S(1)}, f32[72,8,128]{2,1,0:T(8,128)S(1)}, u32[]{:S(2)}, u32[]{:S(2)}) collective-permute-start(f32[72,8,128]{2,1,0:T(8,128)S(1)} %get-tuple-element.51), channel_id=1, source_target_pairs={{0,8},{8,16},{16,24},{24,32},{32,40},{40,48},{48,56},{56,0},{1,9},... | collective-permute-start | bytes 884744 | tf_op jit(solution)/shard_map/ppermute | solution.py:604
  32.0 22.1 %all_to_all.19 = f32[64,1,128]{2,1,0:T(1,128)S(1)} all-to-all(f32[64,1,128]{2,1,0:T(1,128)S(1)} %bitcast.9), channel_id=1, replica_groups=mesh['gx'=4,'gy'=8,'gz'=8] {'gy','gz'}, dimensions={0} | all-to-all | bytes 65536 | tf_op jit(solution)/shard_map/all_to_all | solution.py:651
  54.1 9.8 %shard_map.130 = (f32[4,16,16,128]{3,2,1,0:T(8,128)S(1)}, f32[9,16,24,128]{3,2,1,0:T(8,128)S(1)}, f32[15,24,128]{2,1,0:T(8,128)S(1)}, f32[16,24,128]{2,1,0:T(8,1...) custom-call(f32[2]{0:T(128)S(1)} %copy-done.2, ...), custom_call_target="tpu_custom_call" | custom-call | tf_op jit(solution)/shard_map/pallas_call | solution.py:592
  64.0 2.6 %collective-permute-start.12 = (f32[8,128]{1,0:T(8,128)S(1)}, f32[8,128]{1,0:T(8,128)S(1)}, u32[]{:S(2)}, u32[]{:S(2)}) collective-permute-start(f32[8,128]{1,0:T(8,128)S(1)} %get-tuple-element.53), channel_id=1, source_target_pairs={{0,192},{64,128},{128,64},{192,0},{1,193},{65,129},{129,65},{193,1... | collective-permute-start | bytes 12296 | tf_op jit(solution)/shard_map/ppermute | solution.py:612
  66.6 0.7 collective-permute-start.10
  67.3 5.3 %shard_map.131 = (f32[9,16,16,128]{3,2,1,0:T(8,128)S(1)}, f32[13,8,8,128]{3,2,1,0:T(8,128)S(1)}, f32[13,8,8,128]{3,2,1,0:T(8,128)S(1)}) custom-call(f32[4,16,16,128]{3,2,1,0:T(8,128)S(1)} %get-tuple-element.54.lead.own_lead, f32[9,16,24,128]{3,2,1,0:T(8,128)S(1)} %get-tuple-element.55.rest, f32[15,24,128]{2,1,0:T(8,128)S(1)} %get-tuple-element.56.along_x, ...), custom_call_target="tpu_custom_call" | custom-call | tf_op jit(solution)/shard_map/pallas_call | solution.py:592
  72.6 2.2 %collective-permute-start.13 = (f32[13,8,8,128]{3,2,1,0:T(8,128)S(1)}, f32[13,8,8,128]{3,2,1,0:T(8,128)S(1)}, u32[]{:S(2)}, u32[]{:S(2)}) collective-permute-start(f32[13,8,8,128]{3,2,1,0:T(8,128)S(1)} %get-tuple-element.62), channel_id=1, source_target_pairs={{0,8},{8,16},{16,24},{24,32},{32,40},{40,48},{48,56},{56,0},{1,9},... | collective-permute-start | bytes 1277960 | tf_op jit(solution)/shard_map/ppermute | solution.py:604
  74.9 16.2 %all_to_all.20 = f32[64,1,128]{2,1,0:T(1,128)S(1)} all-to-all(f32[64,1,128]{2,1,0:T(1,128)S(1)} %broadcast_in_dim.2), channel_id=1, replica_groups=mesh['gx'=4,'gy'=8,'gz'=8] {'gy','gz'}, dimensions={0} | all-to-all | bytes 65536 | tf_op jit(solution)/shard_map/all_to_all | solution.py:695
  91.0 14.1 %shard_map.132 = (f32[13,2,16,128]{3,2,1,0:T(8,128)S(1)}, f32[13,2,16,128]{3,2,1,0:T(8,128)S(1)}, f32[13,2,16,128]{3,2,1,0:T(8,128)S(1)}, f32[13,2,16,128]{3,2,1,0:T(8,128)S(1)}) custom-call(f32[2]{0:T(128)S(1)} %copy-done.2, f32[64,128]{1,0:T(8,128)S(1)} %bitcast.8, f32[4,16,16,128]{3,2,1,0:T(8,128)S(1)} %get-tuple-element.54.lead.own_lead, ...), custom_call_target="tpu_custom_call" | custom-call | tf_op jit(solution)/shard_map/pallas_call | solution.py:592
  105.2 0.5 collective-permute-start.15
  105.7 3.2 %collective-permute-start.16 = (f32[13,2,16,128]{3,2,1,0:T(8,128)S(1)}, f32[13,2,16,128]{3,2,1,0:T(8,128)S(1)}, u32[]{:S(2)}, u32[]{:S(2)}) collective-permute-start(f32[13,2,16,128]{3,2,1,0:T(8,128)S(1)} %get-tuple-element.66), channel_id=1, source_target_pairs={{0,128},{64,192},{128,0},{192,64},{1,129},{65,193},{129,1},{193,65... | collective-permute-start | bytes 638984 | tf_op jit(solution)/shard_map/ppermute | solution.py:612
  109.0 0.2 collective-permute-start.17
  109.1 2.1 %collective-permute-done.15.from1 = f32[13,2,16,128]{3,2,1,0:T(8,128)S(1)} collective-permute-done((f32[13,2,16,128]{3,2,1,0:T(8,128)S(1)}, f32[13,2,16,128]{3,2,1,0:T(8,128)S(1)}, u32[]{:S(2)}, u32[]{:S(2)}) %collective-permute-start.15) | collective-permute-done | bytes 213024 | tf_op jit(solution)/shard_map/ppermute | solution.py:612
  111.2 6.8 %collective-permute-done.16.from2 = f32[13,2,16,128]{3,2,1,0:T(8,128)S(1)} collective-permute-done((f32[13,2,16,128]{3,2,1,0:T(8,128)S(1)}, f32[13,2,16,128]{3,2,1,0:T(8,128)S(1)}, u32[]{:S(2)}, u32[]{:S(2)}) %collective-permute-start.16) | collective-permute-done | bytes 213024 | tf_op jit(solution)/shard_map/ppermute | solution.py:612
  118.0 2.7 %collective-permute-done.17.from3 = f32[13,2,16,128]{3,2,1,0:T(8,128)S(1)} collective-permute-done((f32[13,2,16,128]{3,2,1,0:T(8,128)S(1)}, f32[13,2,16,128]{3,2,1,0:T(8,128)S(1)}, u32[]{:S(2)}, u32[]{:S(2)}) %collective-permute-start.17) | collective-permute-done | bytes 213024 | tf_op jit(solution)/shard_map/ppermute | solution.py:612
  120.7 1.1 shard_map.133
  (22 shorter events, 0.1 us)
Async XLA Ops:
  0.6 53.5 %copy-start.2 = (f32[2]{0:T(128)S(1)}, f32[2]{0:T(128)}, u32[]{:S(2)}) copy-start(f32[2]{0:T(128)} %timestep.3) | copy-start | bytes 28
  4.2 21.0 %collective-permute-start = (f32[456,128]{1,0:T(8,128)}, f32[456,128]{1,0:T(8,128)S(1)}, u32[]{:S(2)}, u32[]{:S(2)}) collective-permute-start(f32[456,128]{1,0:T(8,128)} %get-tuple-element.38), channel_id=1, source_target_pairs={{0,64},{64,0},{128,192},{192,128},{1,65},{65,1},{129,193},{193,129... | collective-permute-start | bytes 700424 | tf_op jit(solution)/shard_map/ppermute | solution.py:612
  6.4 18.7 %collective-permute-start.1 = (f32[456,128]{1,0:T(8,128)}, f32[456,128]{1,0:T(8,128)S(1)}, u32[]{:S(2)}, u32[]{:S(2)}) collective-permute-start(f32[456,128]{1,0:T(8,128)} %get-tuple-element.39), channel_id=1, source_target_pairs={{0,128},{64,192},{128,0},{192,64},{1,129},{65,193},{129,1},{193,65... | collective-permute-start | bytes 700424 | tf_op jit(solution)/shard_map/ppermute | solution.py:612
  9.0 16.1 %collective-permute-start.2 = (f32[456,128]{1,0:T(8,128)}, f32[456,128]{1,0:T(8,128)S(1)}, u32[]{:S(2)}, u32[]{:S(2)}) collective-permute-start(f32[456,128]{1,0:T(8,128)} %get-tuple-element.40), channel_id=1, source_target_pairs={{0,192},{64,128},{128,64},{192,0},{1,193},{65,129},{129,65},{193,1... | collective-permute-start | bytes 700424 | tf_op jit(solution)/shard_map/ppermute | solution.py:612
  9.0 5.3 %collective-permute-start.3 = (f32[4,16,128]{2,1,0:T(8,128)}, f32[4,16,128]{2,1,0:T(8,128)S(1)}, u32[]{:S(2)}, u32[]{:S(2)}) collective-permute-start(f32[4,16,128]{2,1,0:T(8,128)} %get-tuple-element.42), channel_id=1, source_target_pairs={{0,1},{1,2},{2,3},{3,4},{4,5},{5,6},{6,7},{7,0},{8,9},{9,10},{10,1... | collective-permute-start | bytes 98312 | tf_op jit(solution)/shard_map/ppermute | solution.py:604
  10.2 4.1 %collective-permute-start.4 = (f32[4,16,128]{2,1,0:T(8,128)}, f32[4,16,128]{2,1,0:T(8,128)S(1)}, u32[]{:S(2)}, u32[]{:S(2)}) collective-permute-start(f32[4,16,128]{2,1,0:T(8,128)} %get-tuple-element.43), channel_id=1, source_target_pairs={{1,0},{2,1},{3,2},{4,3},{5,4},{6,5},{7,6},{0,7},{9,8},{10,9},{11,1... | collective-permute-start | bytes 98312 | tf_op jit(solution)/shard_map/ppermute | solution.py:605
  14.4 1.0 copy-start
  15.3 3.9 %collective-permute-start.5 = (f32[2,4,16,128]{3,2,1,0:T(8,128)S(1)}, f32[2,4,16,128]{3,2,1,0:T(8,128)S(1)}, u32[]{:S(2)}, u32[]{:S(2)}) collective-permute-start(f32[2,4,16,128]{3,2,1,0:T(8,128)S(1)} %get-tuple-element.45), channel_id=1, source_target_pairs={{0,64},{64,0},{128,192},{192,128},{1,65},{65,1},{129,193},{193,129... | collective-permute-start | bytes 196616 | tf_op jit(solution)/shard_map/ppermute | solution.py:612
  15.5 6.2 %collective-permute-start.6 = (f32[2,4,16,128]{3,2,1,0:T(8,128)S(1)}, f32[2,4,16,128]{3,2,1,0:T(8,128)S(1)}, u32[]{:S(2)}, u32[]{:S(2)}) collective-permute-start(f32[2,4,16,128]{3,2,1,0:T(8,128)S(1)} %get-tuple-element.46), channel_id=1, source_target_pairs={{0,128},{64,192},{128,0},{192,64},{1,129},{65,193},{129,1},{193,65... | collective-permute-start | bytes 196616 | tf_op jit(solution)/shard_map/ppermute | solution.py:612
  19.3 5.8 %collective-permute-start.7 = (f32[2,4,16,128]{3,2,1,0:T(8,128)S(1)}, f32[2,4,16,128]{3,2,1,0:T(8,128)S(1)}, u32[]{:S(2)}, u32[]{:S(2)}) collective-permute-start(f32[2,4,16,128]{3,2,1,0:T(8,128)S(1)} %get-tuple-element.47), channel_id=1, source_target_pairs={{0,192},{64,128},{128,64},{192,0},{1,193},{65,129},{129,65},{193,1... | collective-permute-start | bytes 196616 | tf_op jit(solution)/shard_map/ppermute | solution.py:612
  25.1 0.9 copy-start.1
  26.4 27.7 %collective-permute-start.8 = (f32[72,8,128]{2,1,0:T(8,128)S(1)}, f32[72,8,128]{2,1,0:T(8,128)S(1)}, u32[]{:S(2)}, u32[]{:S(2)}) collective-permute-start(f32[72,8,128]{2,1,0:T(8,128)S(1)} %get-tuple-element.51), channel_id=1, source_target_pairs={{0,8},{8,16},{16,24},{24,32},{32,40},{40,48},{48,56},{56,0},{1,9},... | collective-permute-start | bytes 884744 | tf_op jit(solution)/shard_map/ppermute | solution.py:604
  32.0 22.1 %collective-permute-start.9 = (f32[72,8,128]{2,1,0:T(8,128)S(1)}, f32[72,8,128]{2,1,0:T(8,128)S(1)}, u32[]{:S(2)}, u32[]{:S(2)}) collective-permute-start(f32[72,8,128]{2,1,0:T(8,128)S(1)} %get-tuple-element.52), channel_id=1, source_target_pairs={{8,0},{16,8},{24,16},{32,24},{40,32},{48,40},{56,48},{0,56},{9,1},... | collective-permute-start | bytes 884744 | tf_op jit(solution)/shard_map/ppermute | solution.py:605
  64.0 10.9 %collective-permute-start.12 = (f32[8,128]{1,0:T(8,128)S(1)}, f32[8,128]{1,0:T(8,128)S(1)}, u32[]{:S(2)}, u32[]{:S(2)}) collective-permute-start(f32[8,128]{1,0:T(8,128)S(1)} %get-tuple-element.53), channel_id=1, source_target_pairs={{0,192},{64,128},{128,64},{192,0},{1,193},{65,129},{129,65},{193,1... | collective-permute-start | bytes 12296 | tf_op jit(solution)/shard_map/ppermute | solution.py:612
  66.6 8.2 %collective-permute-start.11 = (f32[8,128]{1,0:T(8,128)S(1)}, f32[8,128]{1,0:T(8,128)S(1)}, u32[]{:S(2)}, u32[]{:S(2)}) collective-permute-start(f32[8,128]{1,0:T(8,128)S(1)} %get-tuple-element.53), channel_id=1, source_target_pairs={{0,128},{64,192},{128,0},{192,64},{1,129},{65,193},{129,1},{193,65... | collective-permute-start | bytes 12296 | tf_op jit(solution)/shard_map/ppermute | solution.py:612
  66.6 8.3 %collective-permute-start.10 = (f32[8,128]{1,0:T(8,128)S(1)}, f32[8,128]{1,0:T(8,128)S(1)}, u32[]{:S(2)}, u32[]{:S(2)}) collective-permute-start(f32[8,128]{1,0:T(8,128)S(1)} %get-tuple-element.53), channel_id=1, source_target_pairs={{0,64},{64,0},{128,192},{192,128},{1,65},{65,1},{129,193},{193,129... | collective-permute-start | bytes 12296 | tf_op jit(solution)/shard_map/ppermute | solution.py:612
  72.6 18.5 %collective-permute-start.13 = (f32[13,8,8,128]{3,2,1,0:T(8,128)S(1)}, f32[13,8,8,128]{3,2,1,0:T(8,128)S(1)}, u32[]{:S(2)}, u32[]{:S(2)}) collective-permute-start(f32[13,8,8,128]{3,2,1,0:T(8,128)S(1)} %get-tuple-element.62), channel_id=1, source_target_pairs={{0,8},{8,16},{16,24},{24,32},{32,40},{40,48},{48,56},{56,0},{1,9},... | collective-permute-start | bytes 1277960 | tf_op jit(solution)/shard_map/ppermute | solution.py:604
  74.8 16.2 %collective-permute-start.14 = (f32[13,8,8,128]{3,2,1,0:T(8,128)S(1)}, f32[13,8,8,128]{3,2,1,0:T(8,128)S(1)}, u32[]{:S(2)}, u32[]{:S(2)}) collective-permute-start(f32[13,8,8,128]{3,2,1,0:T(8,128)S(1)} %get-tuple-element.63), channel_id=1, source_target_pairs={{8,0},{16,8},{24,16},{32,24},{40,32},{48,40},{56,48},{0,56},{9,1},... | collective-permute-start | bytes 1277960 | tf_op jit(solution)/shard_map/ppermute | solution.py:605
  105.2 6.0 %collective-permute-start.15 = (f32[13,2,16,128]{3,2,1,0:T(8,128)S(1)}, f32[13,2,16,128]{3,2,1,0:T(8,128)S(1)}, u32[]{:S(2)}, u32[]{:S(2)}) collective-permute-start(f32[13,2,16,128]{3,2,1,0:T(8,128)S(1)} %get-tuple-element.65), channel_id=1, source_target_pairs={{0,64},{64,0},{128,192},{192,128},{1,65},{65,1},{129,193},{193,129... | collective-permute-start | bytes 638984 | tf_op jit(solution)/shard_map/ppermute | solution.py:612
  105.7 12.3 %collective-permute-start.16 = (f32[13,2,16,128]{3,2,1,0:T(8,128)S(1)}, f32[13,2,16,128]{3,2,1,0:T(8,128)S(1)}, u32[]{:S(2)}, u32[]{:S(2)}) collective-permute-start(f32[13,2,16,128]{3,2,1,0:T(8,128)S(1)} %get-tuple-element.66), channel_id=1, source_target_pairs={{0,128},{64,192},{128,0},{192,64},{1,129},{65,193},{129,1},{193,65... | collective-permute-start | bytes 638984 | tf_op jit(solution)/shard_map/ppermute | solution.py:612
  109.0 11.8 %collective-permute-start.17 = (f32[13,2,16,128]{3,2,1,0:T(8,128)S(1)}, f32[13,2,16,128]{3,2,1,0:T(8,128)S(1)}, u32[]{:S(2)}, u32[]{:S(2)}) collective-permute-start(f32[13,2,16,128]{3,2,1,0:T(8,128)S(1)} %get-tuple-element.67), channel_id=1, source_target_pairs={{0,192},{64,128},{128,64},{192,0},{1,193},{65,129},{129,65},{193,1... | collective-permute-start | bytes 638984 | tf_op jit(solution)/shard_map/ppermute | solution.py:612

commit v3 on v2

--- a/solution.py
+++ b/solution.py
@@ -12,6 +12,8 @@
 OWN = 16
 LANES = 128
 HALF = 64
+DEPTH = 80
+GROUP = 8
 PAD = 2
 
 shear_table = (1.0, 0.5, 0.8)
@@ -190,7 +192,15 @@
     ok = jnp.where(row_ok & lane_ok, 1.0, 0.0)
     inside[...] = ok
     face_y[...] = ok * roll(ok, -1, 0)
-    face_z[...] = ok * roll(ok, -1, 1)
+    row = iota((DEPTH, LANES), 0)
+    row_ok = (
+        (row < HALF)
+        | ((row < HALF + width) & (chunk < last_chunk))
+        | ((row >= DEPTH - width) & (chunk > 0))
+    )
+    ok = jnp.where(row_ok, 1.0, 0.0)
+    face_z[0] = ok
+    face_z[1] = ok * roll(ok, -1, 0)
 
 
 def step_size(step_no, timestep, tops):
@@ -218,17 +228,17 @@
     return jnp.where(courant > 0.0, 1.0, -1.0) - courant
 
 
-def rolled_change(q, positive, courant, weight, axis):
-    q_next = roll(q, -1, axis)
+def rolled_change(q, positive, courant, weight):
+    q_next = roll(q, -1, 0)
     fore = q_next - q
-    slope = limited(roll(fore, 1, axis), fore)
-    flux = carried(positive, q, q_next, slope, roll(slope, -1, axis), courant, weight)
-    return q - (flux - roll(flux, 1, axis))
-
-
-def rolled_courant(dt, density, momentum, closed, axis):
+    slope = limited(roll(fore, 1, 0), fore)
+    flux = carried(positive, q, q_next, slope, roll(slope, -1, 0), courant, weight)
+    return q - (flux - roll(flux, 1, 0))
+
+
+def rolled_courant(dt, density, momentum, closed):
     velocity = momentum * inverse(density)
-    return dt * 0.5 * (velocity + roll(velocity, -1, axis)) * closed
+    return dt * 0.5 * (velocity + roll(velocity, -1, 0)) * closed
 
 
 def strain_pass(dt, state, stress, rest, inside):
@@ -367,40 +377,31 @@
         here = ahead
 
 
-def later_sweeps(count, moved, mids, second_courant, third_courant, finish):
-    def second(p, mid):
-        courant = second_courant(p)
-        positive, weight = courant > 0.0, weigh(courant)
-        for f in range(count):
-            mid[f] = rolled_change(moved[f, p], positive, courant, weight, 0)[:OWN]
-            yield
-
-    def third(p, mid):
-        courant = third_courant(p, mid)
-        positive, weight = courant > 0.0, weigh(courant)
-        scale = None
-        for f in range(count):
-            value = rolled_change(mid[f], positive, courant, weight, 1)
-            scale = finish(p, f, value, scale)
-            yield
-
-    def beside(*parts):
-        for _ in zip(*parts):
-            pass
-
-    def pair(i, carry):
-        beside(second(2 * i + 1, mids.at[1]), third(2 * i, mids.at[0]))
-        beside(second(jnp.minimum(2 * i + 2, PLANES - 1), mids.at[0]), third(2 * i + 1, mids.at[1]))
-        return carry
-
-    beside(second(0, mids.at[0]))
-    lax.fori_loop(0, PLANES // 2, pair, 0)
+def second_sweep(moved, f, group, courant_of, mid):
+    for i in range(GROUP):
+        p = GROUP * group + i
+        courant = courant_of(p)
+        value = rolled_change(moved[f, p], courant > 0.0, courant, weigh(courant))
+        mid[OWN * i : OWN * (i + 1)] = value[:OWN]
+
+
+def turned(mid):
+    value = mid[...].T
+    return jnp.concatenate([value[: HALF + 8], value[LANES - 8 :]], axis=0)
+
+
+def turn_back(value, put, f, group):
+    gap = jnp.zeros((LANES - DEPTH, LANES), jnp.float32)
+    value = jnp.concatenate([value[: HALF + 8], gap, value[HALF + 8 :]], axis=0).T
+    for i in range(GROUP):
+        put(f, GROUP * group + i, value[OWN * i : OWN * (i + 1)])
 
 
 LEAD = 4
 REST = 9
 LEAD_AT = (0, 2, 3, 4)
 REST_AT = (1, 5, 6, 7, 8, 9, 10, 11, 12)
+ORDER = tuple((LEAD_AT + REST_AT).index(f) for f in range(FIELDS))
 
 
 def sweep_lead(dt, lead, moved, mids, courants, scales, inside, face_y, face_z, put):
@@ -410,37 +411,51 @@
 
     def second_courant(p):
         density = jnp.where(inside[...] > 0.0, moved[0, p], 1.0)
-        courant = rolled_courant(dt, density, moved[2, p], face_y[...], 0)
+        courant = rolled_courant(dt, density, moved[2, p], face_y[...])
         along_y[p] = courant
         return courant
 
-    def third_courant(p, mid):
-        density = jnp.where(inside[:OWN] > 0.0, mid[0], 1.0)
-        courant = rolled_courant(dt, density, mid[3], face_z[:OWN], 1)
-        along_z[p] = courant
-        return courant
-
-    def finish(p, f, value, scale):
-        if f == 0:
-            ok = inside[:OWN] > 0.0
-            scale = jnp.where(ok, inverse(jnp.where(ok, value, 1.0)), 0.0)
-            scales[p] = scale
-            put(0, p, jnp.where(ok, value, 0.0))
-        else:
-            put(f, p, value * scale)
-        return scale
-
-    later_sweeps(LEAD, moved, mids, second_courant, third_courant, finish)
+    def second(group):
+        second_sweep(moved, 0, group, second_courant, mids.at[group, 0])
+        for f in range(1, LEAD):
+            second_sweep(moved, f, group, lambda p: along_y[p], mids.at[group, f])
+
+    def third(group):
+        ok = face_z[0] > 0.0
+        density = turned(mids.at[group, 0])
+        momentum = turned(mids.at[group, 3])
+        courant = rolled_courant(dt, jnp.where(ok, density, 1.0), momentum, face_z[1])
+        along_z[group] = courant
+        positive, weight = courant > 0.0, weigh(courant)
+        value = rolled_change(density, positive, courant, weight)
+        scale = jnp.where(ok, inverse(jnp.where(ok, value, 1.0)), 0.0)
+        scales[group] = scale
+        turn_back(jnp.where(ok, value, 0.0), put, 0, group)
+        for f in range(1, LEAD):
+            value = turned(mids.at[group, f]) if f < 3 else momentum
+            turn_back(rolled_change(value, positive, courant, weight) * scale, put, f, group)
+
+    second(0)
+    second(1)
+    third(0)
+    third(1)
 
 
 def sweep_rest(rest, moved, mids, courants, scales, put):
     along_x, along_y, along_z = courants
     first_sweep(rest, moved, along_x)
 
-    def finish(p, f, value, scale):
-        put(f, p, value * scales[p])
-
-    later_sweeps(REST, moved, mids, lambda p: along_y[p], lambda p, mid: along_z[p], finish)
+    def field(f, carry):
+        for group in range(2):
+            courant = along_z[group]
+            value = rolled_change(turned(mids.at[group]), courant > 0.0, courant, weigh(courant))
+            turn_back(value * scales[group], put, f, group)
+            second_sweep(moved, jnp.minimum(f + 1, REST - 1), group, lambda p: along_y[p], mids.at[group])
+        return carry
+
+    for group in range(2):
+        second_sweep(moved, 0, group, lambda p: along_y[p], mids.at[group])
+    lax.fori_loop(0, REST, field, 0)
 
 
 def clear_ends(state):
@@ -551,10 +566,10 @@
     courants = (along_x, along_y, along_z)
 
     def put_lead(f, p, value):
-        out[LEAD_AT[f], p] = value
+        out[f, p] = value
 
     def put_rest(f, p, value):
-        out[REST_AT[f], p] = value
+        out[LEAD + f, p] = value
 
     sweep_lead(dt, lead, moved, mids, courants, scales, inside, face_y, face_z, put_lead)
     sweep_rest(rest, rest_moved, rest_mids, courants, scales, put_rest)
@@ -564,7 +579,7 @@
         block = position()[0] ^ k
         for f in range(FIELDS):
             for j in range(2):
-                even, odd = out[f, 4 * block + 2 * j], out[f, 4 * block + 2 * j + 1]
+                even, odd = out[ORDER[f], 4 * block + 2 * j], out[ORDER[f], 4 * block + 2 * j + 1]
                 dest[f, j] = jnp.where(left, even, roll(odd, HALF, 1))
 
 
@@ -655,19 +670,19 @@
         (6, PLANES + 2) + full,
         (LEAD, PLANES) + full,
         (LEAD, PLANES) + full,
-        (2, LEAD, OWN, LANES),
+        (2, LEAD, LANES, LANES),
         full,
         full,
-        full,
+        (2, DEPTH, LANES),
     ]
     left_over = [
         (REST, PLANES) + full,
         (PLANES - 1,) + full,
         (PLANES,) + full,
-        (PLANES, OWN, LANES),
-        (PLANES, OWN, LANES),
+        (2, DEPTH, LANES),
+        (2, DEPTH, LANES),
     ]
-    rest_scratch = [(REST, PLANES) + full, (2, REST, OWN, LANES)]
+    rest_scratch = [(REST, PLANES) + full, (2, LANES, LANES)]
     lead, *rest, kinds, top = call(
         lead_kernel,
         1,

time: 122 us -> 117 us (0.959)
  Pallas kernels: 34.2 us -> 29.2 us
    pallas_call x6, Pallas kernels: 30.6 us -> 25.7 us  [call(): pl.pallas_call(kernel, out_shape=[jax.ShapeDtypeStruct(shape, jnp.float32...]
where the time goes in v3:
time: 117 us
  blocking collectives  38.3 us (33%)
  starting transfers between devices  29.8 us (25%)
  Pallas kernels  29.2 us (25%)
  waiting for transfers between devices  16.8 us (14%)
  local copies, waits for them, and re-layouts  1.91 us (2%)
    pallas_call x6, Pallas kernels, call(): pl.pallas_call(kernel, out_shape=[jax.ShapeDtypeStruct(shape, jnp.float32...  25.7 us
    all_to_all x1, blocking collectives, shards(): tops = lax.all_to_all(top, ('gy', 'gz'), 0, 0)  22.1 us
    ppermute x12, starting transfers between devices, swap_blocks(): lax.ppermute(part, 'gx', [(i, i ^ k + 1) for i in range(count)])  18.3 us
    all_to_all x1, blocking collectives, shards(): lax.all_to_all(jnp.broadcast_to(top[:1], (size_y * size_z, LANES)), ('gy'...  16.2 us
    ppermute x12, waiting for transfers between devices, swap_blocks(): lax.ppermute(part, 'gx', [(i, i ^ k + 1) for i in range(count)])  15.2 us
    ppermute x3, starting transfers between devices, ring_pair(): low = lax.ppermute(to_next, axes, list(zip(order, after)))  8.83 us
    pallas_call x1, Pallas kernels, shards(): pl.pallas_call(pack_kernel, out_shape=[jax.ShapeDtypeStruct(shape, jnp.fl...  3.52 us
    ppermute x3, starting transfers between devices, ring_pair(): high = lax.ppermute(to_last, axes, list(zip(after, order)))  2.63 us
  transfers between devices with their start and end apart: 18, of which 6 were waited for; matrix products, arithmetic and copies ran while one was open for 0% of the time, Pallas kernels for 4%

profile of v3, /device:TPU:1, one launch (start us, length us, event | category | flops | bytes accessed | tf_op | source)
XLA Modules:
  0.0 116.7 jit_solution(13577588799418349335)
XLA Ops:
  0.6 3.5 %shard_map.127 = (f32[456,128]{1,0:T(8,128)}, f32[456,128]{1,0:T(8,128)}, f32[456,128]{1,0:T(8,128)}, f32[456,128]{1,0:T(8,128)}, f32[4,2,4,16,128]{4,3,2,1,0:T(...) custom-call(f32[4,16,256]{2,1,0:T(8,128)} %args_0_.4, f32[4,16,256]{2,1,0:T(8,128)} %args_1_.4, ...), custom_call_target="tpu_custom_call" | custom-call | tf_op jit(solution)/shard_map/pallas_call | solution.py:638
  4.2 2.2 %collective-permute-start = (f32[456,128]{1,0:T(8,128)}, f32[456,128]{1,0:T(8,128)S(1)}, u32[]{:S(2)}, u32[]{:S(2)}) collective-permute-start(f32[456,128]{1,0:T(8,128)} %get-tuple-element.38), channel_id=1, source_target_pairs={{0,64},{64,0},{128,192},{192,128},{1,65},{65,1},{129,193},{193,129... | collective-permute-start | bytes 700424 | tf_op jit(solution)/shard_map/ppermute | solution.py:627
  6.4 2.6 %collective-permute-start.1 = (f32[456,128]{1,0:T(8,128)}, f32[456,128]{1,0:T(8,128)S(1)}, u32[]{:S(2)}, u32[]{:S(2)}) collective-permute-start(f32[456,128]{1,0:T(8,128)} %get-tuple-element.39), channel_id=1, source_target_pairs={{0,128},{64,192},{128,0},{192,64},{1,129},{65,193},{129,1},{193,65... | collective-permute-start | bytes 700424 | tf_op jit(solution)/shard_map/ppermute | solution.py:627
  9.0 0.0 collective-permute-start.2
  9.0 1.2 %collective-permute-start.3 = (f32[4,16,128]{2,1,0:T(8,128)}, f32[4,16,128]{2,1,0:T(8,128)S(1)}, u32[]{:S(2)}, u32[]{:S(2)}) collective-permute-start(f32[4,16,128]{2,1,0:T(8,128)} %get-tuple-element.42), channel_id=1, source_target_pairs={{0,1},{1,2},{2,3},{3,4},{4,5},{5,6},{6,7},{7,0},{8,9},{9,10},{10,1... | collective-permute-start | bytes 98312 | tf_op jit(solution)/shard_map/ppermute | solution.py:619
  10.2 2.6 %collective-permute-start.4 = (f32[4,16,128]{2,1,0:T(8,128)}, f32[4,16,128]{2,1,0:T(8,128)S(1)}, u32[]{:S(2)}, u32[]{:S(2)}) collective-permute-start(f32[4,16,128]{2,1,0:T(8,128)} %get-tuple-element.43), channel_id=1, source_target_pairs={{1,0},{2,1},{3,2},{4,3},{5,4},{6,5},{7,6},{0,7},{9,8},{10,9},{11,1... | collective-permute-start | bytes 98312 | tf_op jit(solution)/shard_map/ppermute | solution.py:620
  12.8 1.5 %collective-permute-done.3.from_below = f32[4,16,128]{2,1,0:T(8,128)S(1)} collective-permute-done((f32[4,16,128]{2,1,0:T(8,128)}, f32[4,16,128]{2,1,0:T(8,128)S(1)}, u32[]{:S(2)}, u32[]{:S(2)}) %collective-permute-start.3) | collective-permute-done | bytes 32800 | tf_op jit(solution)/shard_map/ppermute | solution.py:619
  14.4 0.9 copy-done
  15.3 0.1 collective-permute-start.5
  15.5 3.8 %collective-permute-start.6 = (f32[2,4,16,128]{3,2,1,0:T(8,128)S(1)}, f32[2,4,16,128]{3,2,1,0:T(8,128)S(1)}, u32[]{:S(2)}, u32[]{:S(2)}) collective-permute-start(f32[2,4,16,128]{3,2,1,0:T(8,128)S(1)} %get-tuple-element.46), channel_id=1, source_target_pairs={{0,128},{64,192},{128,0},{192,64},{1,129},{65,193},{129,1},{193,65... | collective-permute-start | bytes 196616 | tf_op jit(solution)/shard_map/ppermute | solution.py:627
  19.3 0.0 collective-permute-done.5.z1
  19.3 2.2 %collective-permute-start.7 = (f32[2,4,16,128]{3,2,1,0:T(8,128)S(1)}, f32[2,4,16,128]{3,2,1,0:T(8,128)S(1)}, u32[]{:S(2)}, u32[]{:S(2)}) collective-permute-start(f32[2,4,16,128]{3,2,1,0:T(8,128)S(1)} %get-tuple-element.47), channel_id=1, source_target_pairs={{0,192},{64,128},{128,64},{192,0},{1,193},{65,129},{129,65},{193,1... | collective-permute-start | bytes 196616 | tf_op jit(solution)/shard_map/ppermute | solution.py:627
  21.5 0.2 collective-permute-done.6.z2
  21.7 3.4 %collective-permute-done.7.z3 = f32[2,4,16,128]{3,2,1,0:T(8,128)S(1)} collective-permute-done((f32[2,4,16,128]{3,2,1,0:T(8,128)S(1)}, f32[2,4,16,128]{3,2,1,0:T(8,128)S(1)}, u32[]{:S(2)}, u32[]{:S(2)}) %collective-permute-start.7) | collective-permute-done | bytes 65568 | tf_op jit(solution)/shard_map/ppermute | solution.py:627
  25.1 0.9 copy-done.1
  26.1 0.4 shard_map.129
  26.4 5.6 %collective-permute-start.8 = (f32[72,8,128]{2,1,0:T(8,128)S(1)}, f32[72,8,128]{2,1,0:T(8,128)S(1)}, u32[]{:S(2)}, u32[]{:S(2)}) collective-permute-start(f32[72,8,128]{2,1,0:T(8,128)S(1)} %get-tuple-element.51), channel_id=1, source_target_pairs={{0,8},{8,16},{16,24},{24,32},{32,40},{40,48},{48,56},{56,0},{1,9},... | collective-permute-start | bytes 884744 | tf_op jit(solution)/shard_map/ppermute | solution.py:619
  32.0 22.1 %all_to_all.19 = f32[64,1,128]{2,1,0:T(1,128)S(1)} all-to-all(f32[64,1,128]{2,1,0:T(1,128)S(1)} %bitcast.9), channel_id=1, replica_groups=mesh['gx'=4,'gy'=8,'gz'=8] {'gy','gz'}, dimensions={0} | all-to-all | bytes 65536 | tf_op jit(solution)/shard_map/all_to_all | solution.py:666
  54.1 8.0 %shard_map.130 = (f32[4,16,16,128]{3,2,1,0:T(8,128)S(1)}, f32[9,16,24,128]{3,2,1,0:T(8,128)S(1)}, f32[15,24,128]{2,1,0:T(8,128)S(1)}, f32[16,24,128]{2,1,0:T(8,1...) custom-call(f32[2]{0:T(128)S(1)} %copy-done.2, ...), custom_call_target="tpu_custom_call" | custom-call | tf_op jit(solution)/shard_map/pallas_call | solution.py:607
  62.1 2.6 %collective-permute-start.12 = (f32[8,128]{1,0:T(8,128)S(1)}, f32[8,128]{1,0:T(8,128)S(1)}, u32[]{:S(2)}, u32[]{:S(2)}) collective-permute-start(f32[8,128]{1,0:T(8,128)S(1)} %get-tuple-element.53), channel_id=1, source_target_pairs={{0,192},{64,128},{128,64},{192,0},{1,193},{65,129},{129,65},{193,1... | collective-permute-start | bytes 12296 | tf_op jit(solution)/shard_map/ppermute | solution.py:627
  64.7 0.7 collective-permute-start.10
  65.5 4.6 %shard_map.131 = (f32[9,16,16,128]{3,2,1,0:T(8,128)S(1)}, f32[13,8,8,128]{3,2,1,0:T(8,128)S(1)}, f32[13,8,8,128]{3,2,1,0:T(8,128)S(1)}) custom-call(f32[4,16,16,128]{3,2,1,0:T(8,128)S(1)} %get-tuple-element.54.lead.own_lead, f32[9,16,24,128]{3,2,1,0:T(8,128)S(1)} %get-tuple-element.55.rest, f32[15,24,128]{2,1,0:T(8,128)S(1)} %get-tuple-element.56.along_x, ...), custom_call_target="tpu_custom_call" | custom-call | tf_op jit(solution)/shard_map/pallas_call | solution.py:607
  70.1 2.1 %collective-permute-start.13 = (f32[13,8,8,128]{3,2,1,0:T(8,128)S(1)}, f32[13,8,8,128]{3,2,1,0:T(8,128)S(1)}, u32[]{:S(2)}, u32[]{:S(2)}) collective-permute-start(f32[13,8,8,128]{3,2,1,0:T(8,128)S(1)} %get-tuple-element.62), channel_id=1, source_target_pairs={{0,8},{8,16},{16,24},{24,32},{32,40},{40,48},{48,56},{56,0},{1,9},... | collective-permute-start | bytes 1277960 | tf_op jit(solution)/shard_map/ppermute | solution.py:619
  72.2 16.2 %all_to_all.20 = f32[64,1,128]{2,1,0:T(1,128)S(1)} all-to-all(f32[64,1,128]{2,1,0:T(1,128)S(1)} %broadcast_in_dim.2), channel_id=1, replica_groups=mesh['gx'=4,'gy'=8,'gz'=8] {'gy','gz'}, dimensions={0} | all-to-all | bytes 65536 | tf_op jit(solution)/shard_map/all_to_all | solution.py:710
  88.4 11.6 %shard_map.132 = (f32[13,2,16,128]{3,2,1,0:T(8,128)S(1)}, f32[13,2,16,128]{3,2,1,0:T(8,128)S(1)}, f32[13,2,16,128]{3,2,1,0:T(8,128)S(1)}, f32[13,2,16,128]{3,2,1,0:T(8,128)S(1)}) custom-call(f32[2]{0:T(128)S(1)} %copy-done.2, f32[64,128]{1,0:T(8,128)S(1)} %bitcast.8, f32[4,16,16,128]{3,2,1,0:T(8,128)S(1)} %get-tuple-element.54.lead.own_lead, ...), custom_call_target="tpu_custom_call" | custom-call | tf_op jit(solution)/shard_map/pallas_call | solution.py:607
  100.0 0.5 collective-permute-start.15
  100.6 3.2 %collective-permute-start.16 = (f32[13,2,16,128]{3,2,1,0:T(8,128)S(1)}, f32[13,2,16,128]{3,2,1,0:T(8,128)S(1)}, u32[]{:S(2)}, u32[]{:S(2)}) collective-permute-start(f32[13,2,16,128]{3,2,1,0:T(8,128)S(1)} %get-tuple-element.66), channel_id=1, source_target_pairs={{0,128},{64,192},{128,0},{192,64},{1,129},{65,193},{129,1},{193,65... | collective-permute-start | bytes 638984 | tf_op jit(solution)/shard_map/ppermute | solution.py:627
  103.8 0.2 collective-permute-start.17
  104.0 2.1 %collective-permute-done.15.from1 = f32[13,2,16,128]{3,2,1,0:T(8,128)S(1)} collective-permute-done((f32[13,2,16,128]{3,2,1,0:T(8,128)S(1)}, f32[13,2,16,128]{3,2,1,0:T(8,128)S(1)}, u32[]{:S(2)}, u32[]{:S(2)}) %collective-permute-start.15) | collective-permute-done | bytes 213024 | tf_op jit(solution)/shard_map/ppermute | solution.py:627
  106.1 6.8 %collective-permute-done.16.from2 = f32[13,2,16,128]{3,2,1,0:T(8,128)S(1)} collective-permute-done((f32[13,2,16,128]{3,2,1,0:T(8,128)S(1)}, f32[13,2,16,128]{3,2,1,0:T(8,128)S(1)}, u32[]{:S(2)}, u32[]{:S(2)}) %collective-permute-start.16) | collective-permute-done | bytes 213024 | tf_op jit(solution)/shard_map/ppermute | solution.py:627
  112.9 2.7 %collective-permute-done.17.from3 = f32[13,2,16,128]{3,2,1,0:T(8,128)S(1)} collective-permute-done((f32[13,2,16,128]{3,2,1,0:T(8,128)S(1)}, f32[13,2,16,128]{3,2,1,0:T(8,128)S(1)}, u32[]{:S(2)}, u32[]{:S(2)}) %collective-permute-start.17) | collective-permute-done | bytes 213024 | tf_op jit(solution)/shard_map/ppermute | solution.py:627
  115.6 1.1 shard_map.133
  (22 shorter events, 0.1 us)
Async XLA Ops:
  0.6 53.5 %copy-start.2 = (f32[2]{0:T(128)S(1)}, f32[2]{0:T(128)}, u32[]{:S(2)}) copy-start(f32[2]{0:T(128)} %timestep.3) | copy-start | bytes 28
  4.2 21.0 %collective-permute-start = (f32[456,128]{1,0:T(8,128)}, f32[456,128]{1,0:T(8,128)S(1)}, u32[]{:S(2)}, u32[]{:S(2)}) collective-permute-start(f32[456,128]{1,0:T(8,128)} %get-tuple-element.38), channel_id=1, source_target_pairs={{0,64},{64,0},{128,192},{192,128},{1,65},{65,1},{129,193},{193,129... | collective-permute-start | bytes 700424 | tf_op jit(solution)/shard_map/ppermute | solution.py:627
  6.4 18.7 %collective-permute-start.1 = (f32[456,128]{1,0:T(8,128)}, f32[456,128]{1,0:T(8,128)S(1)}, u32[]{:S(2)}, u32[]{:S(2)}) collective-permute-start(f32[456,128]{1,0:T(8,128)} %get-tuple-element.39), channel_id=1, source_target_pairs={{0,128},{64,192},{128,0},{192,64},{1,129},{65,193},{129,1},{193,65... | collective-permute-start | bytes 700424 | tf_op jit(solution)/shard_map/ppermute | solution.py:627
  9.0 16.1 %collective-permute-start.2 = (f32[456,128]{1,0:T(8,128)}, f32[456,128]{1,0:T(8,128)S(1)}, u32[]{:S(2)}, u32[]{:S(2)}) collective-permute-start(f32[456,128]{1,0:T(8,128)} %get-tuple-element.40), channel_id=1, source_target_pairs={{0,192},{64,128},{128,64},{192,0},{1,193},{65,129},{129,65},{193,1... | collective-permute-start | bytes 700424 | tf_op jit(solution)/shard_map/ppermute | solution.py:627
  9.0 5.3 %collective-permute-start.3 = (f32[4,16,128]{2,1,0:T(8,128)}, f32[4,16,128]{2,1,0:T(8,128)S(1)}, u32[]{:S(2)}, u32[]{:S(2)}) collective-permute-start(f32[4,16,128]{2,1,0:T(8,128)} %get-tuple-element.42), channel_id=1, source_target_pairs={{0,1},{1,2},{2,3},{3,4},{4,5},{5,6},{6,7},{7,0},{8,9},{9,10},{10,1... | collective-permute-start | bytes 98312 | tf_op jit(solution)/shard_map/ppermute | solution.py:619
  10.2 4.1 %collective-permute-start.4 = (f32[4,16,128]{2,1,0:T(8,128)}, f32[4,16,128]{2,1,0:T(8,128)S(1)}, u32[]{:S(2)}, u32[]{:S(2)}) collective-permute-start(f32[4,16,128]{2,1,0:T(8,128)} %get-tuple-element.43), channel_id=1, source_target_pairs={{1,0},{2,1},{3,2},{4,3},{5,4},{6,5},{7,6},{0,7},{9,8},{10,9},{11,1... | collective-permute-start | bytes 98312 | tf_op jit(solution)/shard_map/ppermute | solution.py:620
  14.4 1.0 copy-start
  15.3 3.9 %collective-permute-start.5 = (f32[2,4,16,128]{3,2,1,0:T(8,128)S(1)}, f32[2,4,16,128]{3,2,1,0:T(8,128)S(1)}, u32[]{:S(2)}, u32[]{:S(2)}) collective-permute-start(f32[2,4,16,128]{3,2,1,0:T(8,128)S(1)} %get-tuple-element.45), channel_id=1, source_target_pairs={{0,64},{64,0},{128,192},{192,128},{1,65},{65,1},{129,193},{193,129... | collective-permute-start | bytes 196616 | tf_op jit(solution)/shard_map/ppermute | solution.py:627
  15.5 6.2 %collective-permute-start.6 = (f32[2,4,16,128]{3,2,1,0:T(8,128)S(1)}, f32[2,4,16,128]{3,2,1,0:T(8,128)S(1)}, u32[]{:S(2)}, u32[]{:S(2)}) collective-permute-start(f32[2,4,16,128]{3,2,1,0:T(8,128)S(1)} %get-tuple-element.46), channel_id=1, source_target_pairs={{0,128},{64,192},{128,0},{192,64},{1,129},{65,193},{129,1},{193,65... | collective-permute-start | bytes 196616 | tf_op jit(solution)/shard_map/ppermute | solution.py:627
  19.3 5.8 %collective-permute-start.7 = (f32[2,4,16,128]{3,2,1,0:T(8,128)S(1)}, f32[2,4,16,128]{3,2,1,0:T(8,128)S(1)}, u32[]{:S(2)}, u32[]{:S(2)}) collective-permute-start(f32[2,4,16,128]{3,2,1,0:T(8,128)S(1)} %get-tuple-element.47), channel_id=1, source_target_pairs={{0,192},{64,128},{128,64},{192,0},{1,193},{65,129},{129,65},{193,1... | collective-permute-start | bytes 196616 | tf_op jit(solution)/shard_map/ppermute | solution.py:627
  25.1 0.9 copy-start.1
  26.4 27.7 %collective-permute-start.8 = (f32[72,8,128]{2,1,0:T(8,128)S(1)}, f32[72,8,128]{2,1,0:T(8,128)S(1)}, u32[]{:S(2)}, u32[]{:S(2)}) collective-permute-start(f32[72,8,128]{2,1,0:T(8,128)S(1)} %get-tuple-element.51), channel_id=1, source_target_pairs={{0,8},{8,16},{16,24},{24,32},{32,40},{40,48},{48,56},{56,0},{1,9},... | collective-permute-start | bytes 884744 | tf_op jit(solution)/shard_map/ppermute | solution.py:619
  32.0 22.1 %collective-permute-start.9 = (f32[72,8,128]{2,1,0:T(8,128)S(1)}, f32[72,8,128]{2,1,0:T(8,128)S(1)}, u32[]{:S(2)}, u32[]{:S(2)}) collective-permute-start(f32[72,8,128]{2,1,0:T(8,128)S(1)} %get-tuple-element.52), channel_id=1, source_target_pairs={{8,0},{16,8},{24,16},{32,24},{40,32},{48,40},{56,48},{0,56},{9,1},... | collective-permute-start | bytes 884744 | tf_op jit(solution)/shard_map/ppermute | solution.py:620
  62.1 10.0 %collective-permute-start.12 = (f32[8,128]{1,0:T(8,128)S(1)}, f32[8,128]{1,0:T(8,128)S(1)}, u32[]{:S(2)}, u32[]{:S(2)}) collective-permute-start(f32[8,128]{1,0:T(8,128)S(1)} %get-tuple-element.53), channel_id=1, source_target_pairs={{0,192},{64,128},{128,64},{192,0},{1,193},{65,129},{129,65},{193,1... | collective-permute-start | bytes 12296 | tf_op jit(solution)/shard_map/ppermute | solution.py:627
  64.7 7.4 %collective-permute-start.11 = (f32[8,128]{1,0:T(8,128)S(1)}, f32[8,128]{1,0:T(8,128)S(1)}, u32[]{:S(2)}, u32[]{:S(2)}) collective-permute-start(f32[8,128]{1,0:T(8,128)S(1)} %get-tuple-element.53), channel_id=1, source_target_pairs={{0,128},{64,192},{128,0},{192,64},{1,129},{65,193},{129,1},{193,65... | collective-permute-start | bytes 12296 | tf_op jit(solution)/shard_map/ppermute | solution.py:627
  64.7 7.4 %collective-permute-start.10 = (f32[8,128]{1,0:T(8,128)S(1)}, f32[8,128]{1,0:T(8,128)S(1)}, u32[]{:S(2)}, u32[]{:S(2)}) collective-permute-start(f32[8,128]{1,0:T(8,128)S(1)} %get-tuple-element.53), channel_id=1, source_target_pairs={{0,64},{64,0},{128,192},{192,128},{1,65},{65,1},{129,193},{193,129... | collective-permute-start | bytes 12296 | tf_op jit(solution)/shard_map/ppermute | solution.py:627
  70.1 18.3 %collective-permute-start.13 = (f32[13,8,8,128]{3,2,1,0:T(8,128)S(1)}, f32[13,8,8,128]{3,2,1,0:T(8,128)S(1)}, u32[]{:S(2)}, u32[]{:S(2)}) collective-permute-start(f32[13,8,8,128]{3,2,1,0:T(8,128)S(1)} %get-tuple-element.62), channel_id=1, source_target_pairs={{0,8},{8,16},{16,24},{24,32},{32,40},{40,48},{48,56},{56,0},{1,9},... | collective-permute-start | bytes 1277960 | tf_op jit(solution)/shard_map/ppermute | solution.py:619
  72.2 16.2 %collective-permute-start.14 = (f32[13,8,8,128]{3,2,1,0:T(8,128)S(1)}, f32[13,8,8,128]{3,2,1,0:T(8,128)S(1)}, u32[]{:S(2)}, u32[]{:S(2)}) collective-permute-start(f32[13,8,8,128]{3,2,1,0:T(8,128)S(1)} %get-tuple-element.63), channel_id=1, source_target_pairs={{8,0},{16,8},{24,16},{32,24},{40,32},{48,40},{56,48},{0,56},{9,1},... | collective-permute-start | bytes 1277960 | tf_op jit(solution)/shard_map/ppermute | solution.py:620
  100.0 6.0 %collective-permute-start.15 = (f32[13,2,16,128]{3,2,1,0:T(8,128)S(1)}, f32[13,2,16,128]{3,2,1,0:T(8,128)S(1)}, u32[]{:S(2)}, u32[]{:S(2)}) collective-permute-start(f32[13,2,16,128]{3,2,1,0:T(8,128)S(1)} %get-tuple-element.65), channel_id=1, source_target_pairs={{0,64},{64,0},{128,192},{192,128},{1,65},{65,1},{129,193},{193,129... | collective-permute-start | bytes 638984 | tf_op jit(solution)/shard_map/ppermute | solution.py:627
  100.6 12.3 %collective-permute-start.16 = (f32[13,2,16,128]{3,2,1,0:T(8,128)S(1)}, f32[13,2,16,128]{3,2,1,0:T(8,128)S(1)}, u32[]{:S(2)}, u32[]{:S(2)}) collective-permute-start(f32[13,2,16,128]{3,2,1,0:T(8,128)S(1)} %get-tuple-element.66), channel_id=1, source_target_pairs={{0,128},{64,192},{128,0},{192,64},{1,129},{65,193},{129,1},{193,65... | collective-permute-start | bytes 638984 | tf_op jit(solution)/shard_map/ppermute | solution.py:627
  103.8 11.8 %collective-permute-start.17 = (f32[13,2,16,128]{3,2,1,0:T(8,128)S(1)}, f32[13,2,16,128]{3,2,1,0:T(8,128)S(1)}, u32[]{:S(2)}, u32[]{:S(2)}) collective-permute-start(f32[13,2,16,128]{3,2,1,0:T(8,128)S(1)} %get-tuple-element.67), channel_id=1, source_target_pairs={{0,192},{64,128},{128,64},{192,0},{1,193},{65,129},{129,65},{193,1... | collective-permute-start | bytes 638984 | tf_op jit(solution)/shard_map/ppermute | solution.py:627

commit v4 on v3

--- a/solution.py
+++ b/solution.py
@@ -27,6 +27,7 @@
 cfl_number = 0.2
 
 PACK_LIMIT = 62 * 1024 * 1024
+CALL_LIMIT = 48 * 1024 * 1024
 ACROSS = ((0, 3, 5), (3, 1, 4), (5, 4, 2))
 
 
@@ -107,16 +108,14 @@
         target = me ^ k
         cols = pl.ds(pl.multiple_of((target >> 1) * LANES, LANES), LANES)
         odd = target & 1
+        side = left == (odd == 0)
         for f in range(FIELDS + 1):
             for j in range(2):
                 even_plane = refs[f][2 * j, :, cols].astype(jnp.float32)
                 odd_plane = refs[f][2 * j + 1, :, cols].astype(jnp.float32)
-                out[part_rows(f, j)] = jnp.where(
-                    left,
-                    pltpu.roll(even_plane, odd * HALF, 1),
-                    pltpu.roll(odd_plane, (1 - odd) * HALF, 1),
-                )
-
+                stays = jnp.where(odd == 1, odd_plane, even_plane)
+                turns = jnp.where(odd == 1, even_plane, odd_plane)
+                out[part_rows(f, j)] = jnp.where(side, stays, roll(turns, HALF, 1))
 
     group = iota((OWN, LANES), 1) >> 3
 
@@ -241,130 +240,139 @@
     return dt * 0.5 * (velocity + roll(velocity, -1, 0)) * closed
 
 
-def strain_pass(dt, state, stress, rest, inside):
-    def strain_plane(p, carry):
-        at = p + PAD
-        ok = inside[...] > 0.0
-        vel = [state[2 + i, at] for i in range(3)]
-        grad = [
-            [
-                central(state[2 + i, at + 1], state[2 + i, at - 1]),
-                central(roll(vel[i], -1, 0), roll(vel[i], 1, 0)),
-                central(roll(vel[i], -1, 1), roll(vel[i], 1, 1)),
-            ]
-            for i in range(3)
+def strain_at(dt, p, state, stress, rest, inside):
+    at = p + PAD
+    ok = inside[...] > 0.0
+    vel = [state[2 + i, at] for i in range(3)]
+    grad = [
+        [
+            central(state[2 + i, at + 1], state[2 + i, at - 1]),
+            central(roll(vel[i], -1, 0), roll(vel[i], 1, 0)),
+            central(roll(vel[i], -1, 1), roll(vel[i], 1, 1)),
         ]
-        third_div = (grad[0][0] + grad[1][1] + grad[2][2]) * (1.0 / 3.0)
-        strain = [
-            grad[0][0] - third_div,
-            grad[1][1] - third_div,
-            grad[2][2] - third_div,
-            0.5 * (grad[0][1] + grad[1][0]),
-            0.5 * (grad[1][2] + grad[2][1]),
-            0.5 * (grad[0][2] + grad[2][0]),
-        ]
-        kind = state[FIELDS, at]
-        first, second = kind == 0.0, kind == 1.0
-        density, energy = state[0, at], state[1, at]
-        plastic, damage = state[5, at], state[6, at]
-        pressure = (
-            pick(first, second, tuple(c * c for c in sound_table))
-            * (density - pick(first, second, rest_table))
-            + pick(first, second, gruneisen_table) * density * energy
+        for i in range(3)
+    ]
+    third_div = (grad[0][0] + grad[1][1] + grad[2][2]) * (1.0 / 3.0)
+    strain = [
+        grad[0][0] - third_div,
+        grad[1][1] - third_div,
+        grad[2][2] - third_div,
+        0.5 * (grad[0][1] + grad[1][0]),
+        0.5 * (grad[1][2] + grad[2][1]),
+        0.5 * (grad[0][2] + grad[2][0]),
+    ]
+    kind = state[FIELDS, at]
+    first, second = kind == 0.0, kind == 1.0
+    density, energy = state[0, at], state[1, at]
+    plastic, damage = state[5, at], state[6, at]
+    pressure = (
+        pick(first, second, tuple(c * c for c in sound_table))
+        * (density - pick(first, second, rest_table))
+        + pick(first, second, gruneisen_table) * density * energy
+    )
+    shear_dt = pick(first, second, tuple(2.0 * g for g in shear_table)) * dt
+    trial = [state[7 + k, at] + shear_dt * strain[k] for k in range(6)]
+    trial_sq = (
+        trial[0] * trial[0]
+        + trial[1] * trial[1]
+        + trial[2] * trial[2]
+        + 2.0 * (trial[3] * trial[3] + trial[4] * trial[4] + trial[5] * trial[5])
+    )
+    strain_sq = (
+        strain[0] * strain[0]
+        + strain[1] * strain[1]
+        + strain[2] * strain[2]
+        + 2.0 * (strain[3] * strain[3] + strain[4] * strain[4] + strain[5] * strain[5])
+    )
+    equivalent = jnp.sqrt(1.5 * trial_sq)
+    strain_rate = jnp.sqrt(strain_sq * (2.0 / 3.0))
+    hardened = pick(first, second, yield_table) + pick(first, second, harden_table) * jnp.exp(
+        pick(first, second, exponent_table) * jnp.log(plastic)
+    )
+    flow = (
+        hardened
+        * (1.0 + pick(first, second, rate_table) * jnp.log(1.0 + strain_rate))
+        * (1.0 - damage)
+    )
+    bound = jnp.maximum(equivalent, flow)
+    per_bound = inverse(bound)
+    factor = flow * per_bound
+    increment = (bound - flow) * pick(first, second, tuple(1.0 / (3.0 * g) for g in shear_table))
+    triaxial = jnp.clip(-pressure * per_bound, -1.5, 1.5)
+    failure = 0.05 + 0.8 * jnp.exp(-1.5 * triaxial)
+    rest[1, p] = jnp.where(ok, density * (plastic + increment), 0.0)
+    worn = jnp.minimum(damage + increment * inverse(failure), 0.9)
+    rest[2, p] = jnp.where(ok, density * worn, 0.0)
+    dev = [jnp.where(ok, trial[k] * factor, 0.0) for k in range(6)]
+    held = jnp.where(ok, pressure, 0.0)
+    full = [dev[0] - held, dev[1] - held, dev[2] - held, dev[3], dev[4], dev[5]]
+    for k in range(6):
+        rest[3 + k, p] = density * dev[k]
+        stress[k, p + 1] = full[k]
+    work = (
+        full[0] * grad[0][0]
+        + full[1] * grad[1][1]
+        + full[2] * grad[2][2]
+        + 2.0 * (full[3] * strain[3] + full[4] * strain[4] + full[5] * strain[5])
+    )
+    rest[0, p] = jnp.where(ok, density * energy + dt * work, 0.0)
+    return full
+
+
+def force_at(dt, p, state, stress, lead, inside, ahead):
+    density = state[0, p + PAD]
+    here = [stress[k, p + 1] for k in range(6)]
+    lead[0, p] = density
+    for i in range(3):
+        along_x, along_y, along_z = ACROSS[0][i], ACROSS[1][i], ACROSS[2][i]
+        force = (
+            central(ahead[along_x], stress[along_x, p])
+            + central(roll(here[along_y], -1, 0), roll(here[along_y], 1, 0))
+            + central(roll(here[along_z], -1, 1), roll(here[along_z], 1, 1))
         )
-        shear_dt = pick(first, second, tuple(2.0 * g for g in shear_table)) * dt
-        trial = [state[7 + k, at] + shear_dt * strain[k] for k in range(6)]
-        trial_sq = (
-            trial[0] * trial[0]
-            + trial[1] * trial[1]
-            + trial[2] * trial[2]
-            + 2.0 * (trial[3] * trial[3] + trial[4] * trial[4] + trial[5] * trial[5])
-        )
-        strain_sq = (
-            strain[0] * strain[0]
-            + strain[1] * strain[1]
-            + strain[2] * strain[2]
-            + 2.0 * (strain[3] * strain[3] + strain[4] * strain[4] + strain[5] * strain[5])
-        )
-        equivalent = jnp.sqrt(1.5 * trial_sq)
-        strain_rate = jnp.sqrt(strain_sq * (2.0 / 3.0))
-        hardened = pick(first, second, yield_table) + pick(first, second, harden_table) * jnp.exp(
-            pick(first, second, exponent_table) * jnp.log(plastic)
-        )
-        flow = (
-            hardened
-            * (1.0 + pick(first, second, rate_table) * jnp.log(1.0 + strain_rate))
-            * (1.0 - damage)
-        )
-        bound = jnp.maximum(equivalent, flow)
-        per_bound = inverse(bound)
-        factor = flow * per_bound
-        increment = (bound - flow) * pick(first, second, tuple(1.0 / (3.0 * g) for g in shear_table))
-        triaxial = jnp.clip(-pressure * per_bound, -1.5, 1.5)
-        failure = 0.05 + 0.8 * jnp.exp(-1.5 * triaxial)
-        rest[1, p] = jnp.where(ok, density * (plastic + increment), 0.0)
-        worn = jnp.minimum(damage + increment * inverse(failure), 0.9)
-        rest[2, p] = jnp.where(ok, density * worn, 0.0)
-        dev = [jnp.where(ok, trial[k] * factor, 0.0) for k in range(6)]
-        held = jnp.where(ok, pressure, 0.0)
-        full = [dev[0] - held, dev[1] - held, dev[2] - held, dev[3], dev[4], dev[5]]
-        for k in range(6):
-            rest[3 + k, p] = density * dev[k]
-            stress[k, p + 1] = full[k]
-        work = (
-            full[0] * grad[0][0]
-            + full[1] * grad[1][1]
-            + full[2] * grad[2][2]
-            + 2.0 * (full[3] * strain[3] + full[4] * strain[4] + full[5] * strain[5])
-        )
-        rest[0, p] = jnp.where(ok, density * energy + dt * work, 0.0)
-        return carry
-
+        pushed = jnp.where(inside[...] > 0.0, dt * force, 0.0)
+        lead[1 + i, p] = density * state[2 + i, p + PAD] + pushed
+
+
+def stress_and_force(dt, gather, state, stress, rest, lead, inside):
     zero = jnp.zeros((ROWS, LANES), jnp.float32)
     for k in range(6):
         stress[k, 0] = zero
-        stress[k, PLANES + 1] = zero
-    lax.fori_loop(0, PLANES, strain_plane, 0)
-
-
-def force_pass(dt, state, stress, lead, inside):
-    def force_plane(p, carry):
-        at = p + PAD
-        density = state[0, at]
-        here = [stress[k, p + 1] for k in range(6)]
-        lead[0, p] = density
-        for i in range(3):
-            along_x, along_y, along_z = ACROSS[0][i], ACROSS[1][i], ACROSS[2][i]
-            force = (
-                central(stress[along_x, p + 2], stress[along_x, p])
-                + central(roll(here[along_y], -1, 0), roll(here[along_y], 1, 0))
-                + central(roll(here[along_z], -1, 1), roll(here[along_z], 1, 1))
-            )
-            lead[1 + i, p] = density * state[2 + i, at] + jnp.where(inside[...] > 0.0, dt * force, 0.0)
+    gather(0, 0, PAD)
+    gather(0, 1, PAD + 1)
+
+    def block(b, carry):
+        for i in range(4):
+            p = 4 * b + i
+            full = strain_at(dt, p, state, stress, rest, inside)
+            if i > 0:
+                force_at(dt, p - 1, state, stress, lead, inside, full)
+            else:
+                force_at(dt, jnp.maximum(p - 1, 0), state, stress, lead, inside, full)
+            soon = p + 2
+            to = jnp.where(soon < PLANES, soon + PAD, PLANES + 2 * PAD - 1)
+            gather(jnp.minimum(b + (i + 2) // 4, 3), (i + 2) % 4, to)
         return carry
 
-    lax.fori_loop(0, PLANES, force_plane, 0)
-
-
-def first_sweep(fields, moved, courants):
-    def field(f, carry):
-        here = fields[f, 0]
-        ahead = fields[f, 1]
-        fore = ahead - here
-        slope = limited(here, fore)
-        last_flux = None
-        for p in range(PLANES - 1):
-            further = fields[f, p + 2] if p + 2 < PLANES else 0.0
-            next_fore = further - ahead
-            next_slope = limited(fore, next_fore)
-            courant = courants[p]
-            flux = carried(courant > 0.0, here, ahead, slope, next_slope, courant, weigh(courant))
-            moved[f, p] = here - (flux if last_flux is None else flux - last_flux)
-            last_flux, here, ahead, fore, slope = flux, ahead, further, next_fore, next_slope
-        moved[f, PLANES - 1] = here + last_flux
-        return carry
-
-    lax.fori_loop(0, fields.shape[0], field, 0)
+    lax.fori_loop(0, PLANES // 4, block, 0)
+    force_at(dt, PLANES - 1, state, stress, lead, inside, [zero] * 6)
+
+
+def first_sweep(fields, f, moved, courants):
+    here = fields[f, 0]
+    ahead = fields[f, 1]
+    fore = ahead - here
+    slope = limited(here, fore)
+    last_flux = None
+    for p in range(PLANES - 1):
+        further = fields[f, p + 2] if p + 2 < PLANES else 0.0
+        next_fore = further - ahead
+        next_slope = limited(fore, next_fore)
+        courant = courants[p]
+        flux = carried(courant > 0.0, here, ahead, slope, next_slope, courant, weigh(courant))
+        moved[f, p] = here - (flux if last_flux is None else flux - last_flux)
+        last_flux, here, ahead, fore, slope = flux, ahead, further, next_fore, next_slope
+    moved[f, PLANES - 1] = here + last_flux
 
 
 def first_courants(dt, lead, courants, inside):
@@ -407,7 +415,8 @@
 def sweep_lead(dt, lead, moved, mids, courants, scales, inside, face_y, face_z, put):
     along_x, along_y, along_z = courants
     first_courants(dt, lead, along_x, inside)
-    first_sweep(lead, moved, along_x)
+    for f in range(LEAD):
+        first_sweep(lead, f, moved, along_x)
 
     def second_courant(p):
         density = jnp.where(inside[...] > 0.0, moved[0, p], 1.0)
@@ -443,18 +452,26 @@
 
 def sweep_rest(rest, moved, mids, courants, scales, put):
     along_x, along_y, along_z = courants
-    first_sweep(rest, moved, along_x)
+    last = REST - 1
+
+    def second(f, group):
+        second_sweep(moved, f, group, lambda p: along_y[p], mids.at[group])
 
     def field(f, carry):
         for group in range(2):
             courant = along_z[group]
             value = rolled_change(turned(mids.at[group]), courant > 0.0, courant, weigh(courant))
             turn_back(value * scales[group], put, f, group)
-            second_sweep(moved, jnp.minimum(f + 1, REST - 1), group, lambda p: along_y[p], mids.at[group])
+            second(jnp.minimum(f + 1, last), group)
         return carry
 
+    def first(f, carry):
+        first_sweep(rest, f, moved, along_x)
+        return carry
+
+    lax.fori_loop(0, REST, first, 0)
     for group in range(2):
-        second_sweep(moved, 0, group, lambda p: along_y[p], mids.at[group])
+        second(0, group)
     lax.fori_loop(0, REST, field, 0)
 
 
@@ -473,34 +490,27 @@
     clear_ends(state)
     dt = step_size(0, timestep, tops)
 
-    def gather(block, carry):
+    def gather(block, i, to):
+        j, odd = i // 2, i % 2
+        p = 4 * block + i
         ok = inside[...] > 0.0
         lane = iota((ROWS, LANES), 1)
         group = lane >> 3
-        for j in range(2):
-            around = []
-            for odd in range(2):
-                p = 4 * block + 2 * j + odd
-                for which in range(2):
-                    at = MAIN_TILES + 8 * which + 2 * block + j
-                    tile = halo_tile(high[at], low[at], odd == 1)
-                    around.append(jnp.concatenate([sides[which, p], tile], axis=0))
-            for f in range(FIELDS + 1):
-                tile = halo_tile(high[4 * f + block], low[4 * f + block], j == 1)
-                for odd in range(2):
-                    p = 4 * block + 2 * j + odd
-                    below, above = around[2 * odd], around[2 * odd + 1]
-                    value = jnp.concatenate([own[f, p], roll(tile, HALF * odd, 1)], axis=0)
-                    side = roll(jnp.where(group == f, above, below), HALF - 8 * f, 1)
-                    value = jnp.where(ok, jnp.where(lane < HALF, value, side), 0.0)
-                    state[f, p + PAD] = value
-                    if f == FIELDS:
-                        kinds[p] = value
-        return carry
-
-    lax.fori_loop(0, 4, gather, 0)
-    strain_pass(dt, state, stress, rest, inside)
-    force_pass(dt, state, stress, lead, inside)
+        around = []
+        for which in range(2):
+            at = MAIN_TILES + 8 * which + 2 * block + j
+            tile = halo_tile(high[at], low[at], odd == 1)
+            around.append(jnp.concatenate([sides[which, p], tile], axis=0))
+        for f in range(FIELDS + 1):
+            tile = roll(halo_tile(high[4 * f + block], low[4 * f + block], j == 1), HALF * odd, 1)
+            value = jnp.concatenate([own[f, p], tile], axis=0)
+            side = roll(jnp.where(group == f, around[1], around[0]), HALF - 8 * f, 1)
+            value = jnp.where(ok, jnp.where(lane < HALF, value, side), 0.0)
+            state[f, to] = value
+            if f == FIELDS:
+                kinds[p] = value
+
+    stress_and_force(dt, gather, state, stress, rest, lead, inside)
 
     def put(f, p, value):
         out[f, p] = value
@@ -547,22 +557,17 @@
     clear_ends(state)
     dt = step_size(1, timestep, tops)
 
-    def gather(i, carry):
+    def gather(block, i, to):
+        p = 4 * block + i
+        pair, odd = 2 * block + i // 2, i % 2
         ok = inside[...] > 0.0
         for f in range(FIELDS):
             src, at = (own_lead, LEAD_AT.index(f)) if f in LEAD_AT else (own_rest, REST_AT.index(f))
-            for odd in range(2):
-                p = 2 * i + odd
-                tile = halo_tile(high[f, i], low[f, i], odd == 1)
-                value = jnp.concatenate([src[at, p], tile], axis=0)
-                state[f, p + PAD] = jnp.where(ok, value, 0.0)
-        for odd in range(2):
-            state[FIELDS, 2 * i + odd + PAD] = kinds[2 * i + odd]
-        return carry
-
-    lax.fori_loop(0, PLANES // 2, gather, 0)
-    strain_pass(dt, state, stress, rest, inside)
-    force_pass(dt, state, stress, lead, inside)
+            tile = halo_tile(high[f, pair], low[f, pair], odd == 1)
+            state[f, to] = jnp.where(ok, jnp.concatenate([src[at, p], tile], axis=0), 0.0)
+        state[FIELDS, to] = kinds[p]
+
+    stress_and_force(dt, gather, state, stress, rest, lead, inside)
     courants = (along_x, along_y, along_z)
 
     def put_lead(f, p, value):
@@ -573,14 +578,18 @@
 
     sweep_lead(dt, lead, moved, mids, courants, scales, inside, face_y, face_z, put_lead)
     sweep_rest(rest, rest_moved, rest_mids, courants, scales, put_rest)
-
+    me = position()[0]
+    for k, part in enumerate((mine, to1, to2, to3)):
+        pack_block(out, me ^ k, part)
+
+
+def pack_block(out, block, part):
     left = iota((OWN, LANES), 1) < HALF
-    for k, dest in enumerate((mine, to1, to2, to3)):
-        block = position()[0] ^ k
-        for f in range(FIELDS):
-            for j in range(2):
-                even, odd = out[ORDER[f], 4 * block + 2 * j], out[ORDER[f], 4 * block + 2 * j + 1]
-                dest[f, j] = jnp.where(left, even, roll(odd, HALF, 1))
+    first = 4 * block
+    for f in range(FIELDS):
+        for j in range(2):
+            even, odd = out[ORDER[f], first + 2 * j], out[ORDER[f], first + 2 * j + 1]
+            part[f, j] = jnp.where(left, even, roll(odd, HALF, 1))
 
 
 def unpack_kernel(mine, from1, from2, from3, dens, ener, vel, plas, dama, devi, held):
@@ -603,14 +612,15 @@
 IN_SMEM = pl.BlockSpec(memory_space=pltpu.SMEM)
 
 
-def call(kernel, scalars, outs, scratch, *args):
+def call(kernel, scalars, outs, scratch, *args, micros=1):
     return pl.pallas_call(
         kernel,
         out_shape=[jax.ShapeDtypeStruct(shape, jnp.float32) for shape in outs],
         in_specs=[IN_SMEM] * scalars + [IN_VMEM] * (len(args) - scalars),
         out_specs=[IN_VMEM] * len(outs),
         scratch_shapes=[pltpu.VMEM(shape, jnp.float32) for shape in scratch],
-        compiler_params=pltpu.CompilerParams(vmem_limit_bytes=48 * 1024 * 1024),
+        compiler_params=pltpu.CompilerParams(vmem_limit_bytes=CALL_LIMIT),
+        cost_estimate=pl.CostEstimate(flops=0, bytes_accessed=micros * 3_600_000, transcendentals=0),
     )(*args)
 
 
@@ -621,12 +631,12 @@
     return low, high
 
 
+def swap_block(part, k):
+    return lax.ppermute(part, "gx", [(i, i ^ k) for i in range(lax.axis_size("gx"))])
+
+
 def swap_blocks(parts):
-    count = lax.axis_size("gx")
-    return [
-        lax.ppermute(part, "gx", [(i, i ^ (k + 1)) for i in range(count)])
-        for k, part in enumerate(parts)
-    ]
+    return [swap_block(part, k + 1) for k, part in enumerate(parts)]
 
 
 def shards(density, energy, velocity, plastic_strain, damage, deviator, materials, timestep):
@@ -703,6 +713,7 @@
         rest_scratch,
         lead,
         *rest,
+        micros=5,
     )
     low, high = ring_pair(up, down, "gy", list(range(size_y)))
     for other in others:

time: 117 us -> 112 us (0.957)
  Pallas kernels: 29.2 us -> 24.6 us
    pallas_call x6, Pallas kernels: 25.7 us -> 21.4 us  [call(): pl.pallas_call(kernel, out_shape=[jax.ShapeDtypeStruct(shape, jnp.float32...]
where the time goes in v4:
time: 112 us
  blocking collectives  38.3 us (34%)
  starting transfers between devices  29.8 us (27%)
  Pallas kernels  24.6 us (22%)
  waiting for transfers between devices  16.8 us (15%)
  local copies, waits for them, and re-layouts  1.91 us (2%)
    all_to_all x1, blocking collectives, shards(): tops = lax.all_to_all(top, ('gy', 'gz'), 0, 0)  22.1 us
    pallas_call x6, Pallas kernels, call(): pl.pallas_call(kernel, out_shape=[jax.ShapeDtypeStruct(shape, jnp.float32...  21.4 us
    ppermute x12, starting transfers between devices, swap_block(): lax.ppermute(part, 'gx', [(i, i ^ k) for i in range(lax.axis_size('gx'))])  18.4 us
    all_to_all x1, blocking collectives, shards(): lax.all_to_all(jnp.broadcast_to(top[:1], (size_y * size_z, LANES)), ('gy'...  16.2 us
    ppermute x12, waiting for transfers between devices, swap_block(): lax.ppermute(part, 'gx', [(i, i ^ k) for i in range(lax.axis_size('gx'))])  15.2 us
    ppermute x3, starting transfers between devices, ring_pair(): low = lax.ppermute(to_next, axes, list(zip(order, after)))  8.71 us
    pallas_call x1, Pallas kernels, shards(): pl.pallas_call(pack_kernel, out_shape=[jax.ShapeDtypeStruct(shape, jnp.fl...  3.29 us
    ppermute x3, starting transfers between devices, ring_pair(): high = lax.ppermute(to_last, axes, list(zip(after, order)))  2.63 us
  transfers between devices with their start and end apart: 18, of which 6 were waited for; matrix products, arithmetic and copies ran while one was open for 0% of the time, Pallas kernels for 4%

profile of v4, /device:TPU:1, one launch (start us, length us, event | category | flops | bytes accessed | tf_op | source)
XLA Modules:
  0.0 112.1 jit_solution(8382534999614827149)
XLA Ops:
  0.6 3.3 %shard_map.127 = (f32[456,128]{1,0:T(8,128)}, f32[456,128]{1,0:T(8,128)}, f32[456,128]{1,0:T(8,128)}, f32[456,128]{1,0:T(8,128)}, f32[4,2,4,16,128]{4,3,2,1,0:T(...) custom-call(f32[4,16,256]{2,1,0:T(8,128)} %args_0_.4, f32[4,16,256]{2,1,0:T(8,128)} %args_1_.4, ...), custom_call_target="tpu_custom_call" | custom-call | tf_op jit(solution)/shard_map/pallas_call | solution.py:648
  3.9 2.2 %collective-permute-start = (f32[456,128]{1,0:T(8,128)}, f32[456,128]{1,0:T(8,128)S(1)}, u32[]{:S(2)}, u32[]{:S(2)}) collective-permute-start(f32[456,128]{1,0:T(8,128)} %get-tuple-element.38), channel_id=1, source_target_pairs={{0,64},{64,0},{128,192},{192,128},{1,65},{65,1},{129,193},{193,129... | collective-permute-start | bytes 700424 | tf_op jit(solution)/shard_map/ppermute | solution.py:635
  6.2 2.6 %collective-permute-start.1 = (f32[456,128]{1,0:T(8,128)}, f32[456,128]{1,0:T(8,128)S(1)}, u32[]{:S(2)}, u32[]{:S(2)}) collective-permute-start(f32[456,128]{1,0:T(8,128)} %get-tuple-element.39), channel_id=1, source_target_pairs={{0,128},{64,192},{128,0},{192,64},{1,129},{65,193},{129,1},{193,65... | collective-permute-start | bytes 700424 | tf_op jit(solution)/shard_map/ppermute | solution.py:635
  8.8 1.2 %collective-permute-start.3 = (f32[4,16,128]{2,1,0:T(8,128)}, f32[4,16,128]{2,1,0:T(8,128)S(1)}, u32[]{:S(2)}, u32[]{:S(2)}) collective-permute-start(f32[4,16,128]{2,1,0:T(8,128)} %get-tuple-element.42), channel_id=1, source_target_pairs={{0,1},{1,2},{2,3},{3,4},{4,5},{5,6},{6,7},{7,0},{8,9},{9,10},{10,1... | collective-permute-start | bytes 98312 | tf_op jit(solution)/shard_map/ppermute | solution.py:629
  10.0 2.6 %collective-permute-start.4 = (f32[4,16,128]{2,1,0:T(8,128)}, f32[4,16,128]{2,1,0:T(8,128)S(1)}, u32[]{:S(2)}, u32[]{:S(2)}) collective-permute-start(f32[4,16,128]{2,1,0:T(8,128)} %get-tuple-element.43), channel_id=1, source_target_pairs={{1,0},{2,1},{3,2},{4,3},{5,4},{6,5},{7,6},{0,7},{9,8},{10,9},{11,1... | collective-permute-start | bytes 98312 | tf_op jit(solution)/shard_map/ppermute | solution.py:630
  12.6 1.5 %collective-permute-done.3.from_below = f32[4,16,128]{2,1,0:T(8,128)S(1)} collective-permute-done((f32[4,16,128]{2,1,0:T(8,128)}, f32[4,16,128]{2,1,0:T(8,128)S(1)}, u32[]{:S(2)}, u32[]{:S(2)}) %collective-permute-start.3) | collective-permute-done | bytes 32800 | tf_op jit(solution)/shard_map/ppermute | solution.py:629
  14.1 0.0 collective-permute-done.4.from_above
  14.1 0.9 copy-done
  15.1 0.1 collective-permute-start.5
  15.2 3.8 %collective-permute-start.6 = (f32[2,4,16,128]{3,2,1,0:T(8,128)S(1)}, f32[2,4,16,128]{3,2,1,0:T(8,128)S(1)}, u32[]{:S(2)}, u32[]{:S(2)}) collective-permute-start(f32[2,4,16,128]{3,2,1,0:T(8,128)S(1)} %get-tuple-element.46), channel_id=1, source_target_pairs={{0,128},{64,192},{128,0},{192,64},{1,129},{65,193},{129,1},{193,65... | collective-permute-start | bytes 196616 | tf_op jit(solution)/shard_map/ppermute | solution.py:635
  19.1 2.2 %collective-permute-start.7 = (f32[2,4,16,128]{3,2,1,0:T(8,128)S(1)}, f32[2,4,16,128]{3,2,1,0:T(8,128)S(1)}, u32[]{:S(2)}, u32[]{:S(2)}) collective-permute-start(f32[2,4,16,128]{3,2,1,0:T(8,128)S(1)} %get-tuple-element.47), channel_id=1, source_target_pairs={{0,192},{64,128},{128,64},{192,0},{1,193},{65,129},{129,65},{193,1... | collective-permute-start | bytes 196616 | tf_op jit(solution)/shard_map/ppermute | solution.py:635
  21.3 0.2 collective-permute-done.6.z2
  21.5 3.4 %collective-permute-done.7.z3 = f32[2,4,16,128]{3,2,1,0:T(8,128)S(1)} collective-permute-done((f32[2,4,16,128]{3,2,1,0:T(8,128)S(1)}, f32[2,4,16,128]{3,2,1,0:T(8,128)S(1)}, u32[]{:S(2)}, u32[]{:S(2)}) %collective-permute-start.7) | collective-permute-done | bytes 65568 | tf_op jit(solution)/shard_map/ppermute | solution.py:635
  24.9 0.9 copy-done.1
  25.8 0.4 shard_map.129
  26.2 5.6 %collective-permute-start.8 = (f32[72,8,128]{2,1,0:T(8,128)S(1)}, f32[72,8,128]{2,1,0:T(8,128)S(1)}, u32[]{:S(2)}, u32[]{:S(2)}) collective-permute-start(f32[72,8,128]{2,1,0:T(8,128)S(1)} %get-tuple-element.51), channel_id=1, source_target_pairs={{0,8},{8,16},{16,24},{24,32},{32,40},{40,48},{48,56},{56,0},{1,9},... | collective-permute-start | bytes 884744 | tf_op jit(solution)/shard_map/ppermute | solution.py:629
  31.8 22.1 %all_to_all.19 = f32[64,1,128]{2,1,0:T(1,128)S(1)} all-to-all(f32[64,1,128]{2,1,0:T(1,128)S(1)} %bitcast.9), channel_id=1, replica_groups=mesh['gx'=4,'gy'=8,'gz'=8] {'gy','gz'}, dimensions={0} | all-to-all | bytes 65536 | tf_op jit(solution)/shard_map/all_to_all | solution.py:676
  53.9 5.8 %shard_map.130 = (f32[4,16,16,128]{3,2,1,0:T(8,128)S(1)}, f32[9,16,24,128]{3,2,1,0:T(8,128)S(1)}, f32[15,24,128]{2,1,0:T(8,128)S(1)}, f32[16,24,128]{2,1,0:T(8,1...) custom-call(f32[2]{0:T(128)S(1)} %copy-done.2, ...), custom_call_target="tpu_custom_call" | custom-call | bytes 3600000 | tf_op jit(solution)/shard_map/pallas_call | solution.py:616
  59.7 2.6 %collective-permute-start.12 = (f32[8,128]{1,0:T(8,128)S(1)}, f32[8,128]{1,0:T(8,128)S(1)}, u32[]{:S(2)}, u32[]{:S(2)}) collective-permute-start(f32[8,128]{1,0:T(8,128)S(1)} %get-tuple-element.53), channel_id=1, source_target_pairs={{0,192},{64,128},{128,64},{192,0},{1,193},{65,129},{129,65},{193,1... | collective-permute-start | bytes 12296 | tf_op jit(solution)/shard_map/ppermute | solution.py:635
  62.3 0.0 collective-permute-start.11
  62.3 0.9 collective-permute-start.10
  63.1 4.6 %shard_map.131 = (f32[9,16,16,128]{3,2,1,0:T(8,128)S(1)}, f32[13,8,8,128]{3,2,1,0:T(8,128)S(1)}, f32[13,8,8,128]{3,2,1,0:T(8,128)S(1)}) custom-call(f32[4,16,16,128]{3,2,1,0:T(8,128)S(1)} %get-tuple-element.54.lead.own_lead, f32[9,16,24,128]{3,2,1,0:T(8,128)S(1)} %get-tuple-element.55.rest, f32[15,24,128]{2,1,0:T(8,128)S(1)} %get-tuple-element.56.along_x, ...), custom_call_target="tpu_custom_call" | custom-call | bytes 18000000 | tf_op jit(solution)/shard_map/pallas_call | solution.py:616
  67.8 1.9 %collective-permute-start.13 = (f32[13,8,8,128]{3,2,1,0:T(8,128)S(1)}, f32[13,8,8,128]{3,2,1,0:T(8,128)S(1)}, u32[]{:S(2)}, u32[]{:S(2)}) collective-permute-start(f32[13,8,8,128]{3,2,1,0:T(8,128)S(1)} %get-tuple-element.62), channel_id=1, source_target_pairs={{0,8},{8,16},{16,24},{24,32},{32,40},{40,48},{48,56},{56,0},{1,9},... | collective-permute-start | bytes 1277960 | tf_op jit(solution)/shard_map/ppermute | solution.py:629
  69.8 16.2 %all_to_all.20 = f32[64,1,128]{2,1,0:T(1,128)S(1)} all-to-all(f32[64,1,128]{2,1,0:T(1,128)S(1)} %broadcast_in_dim.2), channel_id=1, replica_groups=mesh['gx'=4,'gy'=8,'gz'=8] {'gy','gz'}, dimensions={0} | all-to-all | bytes 65536 | tf_op jit(solution)/shard_map/all_to_all | solution.py:721
  86.0 9.5 %shard_map.132 = (f32[13,2,16,128]{3,2,1,0:T(8,128)S(1)}, f32[13,2,16,128]{3,2,1,0:T(8,128)S(1)}, f32[13,2,16,128]{3,2,1,0:T(8,128)S(1)}, f32[13,2,16,128]{3,2,1,0:T(8,128)S(1)}) custom-call(f32[2]{0:T(128)S(1)} %copy-done.2, f32[64,128]{1,0:T(8,128)S(1)} %bitcast.8, f32[4,16,16,128]{3,2,1,0:T(8,128)S(1)} %get-tuple-element.54.lead.own_lead, ...), custom_call_target="tpu_custom_call" | custom-call | bytes 3600000 | tf_op jit(solution)/shard_map/pallas_call | solution.py:616
  95.5 0.5 collective-permute-start.15
  96.0 3.2 %collective-permute-start.16 = (f32[13,2,16,128]{3,2,1,0:T(8,128)S(1)}, f32[13,2,16,128]{3,2,1,0:T(8,128)S(1)}, u32[]{:S(2)}, u32[]{:S(2)}) collective-permute-start(f32[13,2,16,128]{3,2,1,0:T(8,128)S(1)} %get-tuple-element.66), channel_id=1, source_target_pairs={{0,128},{64,192},{128,0},{192,64},{1,129},{65,193},{129,1},{193,65... | collective-permute-start | bytes 638984 | tf_op jit(solution)/shard_map/ppermute | solution.py:635
  99.2 0.2 collective-permute-start.17
  99.4 2.1 %collective-permute-done.15.from1 = f32[13,2,16,128]{3,2,1,0:T(8,128)S(1)} collective-permute-done((f32[13,2,16,128]{3,2,1,0:T(8,128)S(1)}, f32[13,2,16,128]{3,2,1,0:T(8,128)S(1)}, u32[]{:S(2)}, u32[]{:S(2)}) %collective-permute-start.15) | collective-permute-done | bytes 213024 | tf_op jit(solution)/shard_map/ppermute | solution.py:635
  101.5 6.8 %collective-permute-done.16.from2 = f32[13,2,16,128]{3,2,1,0:T(8,128)S(1)} collective-permute-done((f32[13,2,16,128]{3,2,1,0:T(8,128)S(1)}, f32[13,2,16,128]{3,2,1,0:T(8,128)S(1)}, u32[]{:S(2)}, u32[]{:S(2)}) %collective-permute-start.16) | collective-permute-done | bytes 213024 | tf_op jit(solution)/shard_map/ppermute | solution.py:635
  108.3 2.7 %collective-permute-done.17.from3 = f32[13,2,16,128]{3,2,1,0:T(8,128)S(1)} collective-permute-done((f32[13,2,16,128]{3,2,1,0:T(8,128)S(1)}, f32[13,2,16,128]{3,2,1,0:T(8,128)S(1)}, u32[]{:S(2)}, u32[]{:S(2)}) %collective-permute-start.17) | collective-permute-done | bytes 213024 | tf_op jit(solution)/shard_map/ppermute | solution.py:635
  111.0 1.1 shard_map.133
  (22 shorter events, 0.1 us)
Async XLA Ops:
  0.6 53.3 %copy-start.2 = (f32[2]{0:T(128)S(1)}, f32[2]{0:T(128)}, u32[]{:S(2)}) copy-start(f32[2]{0:T(128)} %timestep.3) | copy-start | bytes 28
  3.9 21.0 %collective-permute-start = (f32[456,128]{1,0:T(8,128)}, f32[456,128]{1,0:T(8,128)S(1)}, u32[]{:S(2)}, u32[]{:S(2)}) collective-permute-start(f32[456,128]{1,0:T(8,128)} %get-tuple-element.38), channel_id=1, source_target_pairs={{0,64},{64,0},{128,192},{192,128},{1,65},{65,1},{129,193},{193,129... | collective-permute-start | bytes 700424 | tf_op jit(solution)/shard_map/ppermute | solution.py:635
  6.2 18.7 %collective-permute-start.1 = (f32[456,128]{1,0:T(8,128)}, f32[456,128]{1,0:T(8,128)S(1)}, u32[]{:S(2)}, u32[]{:S(2)}) collective-permute-start(f32[456,128]{1,0:T(8,128)} %get-tuple-element.39), channel_id=1, source_target_pairs={{0,128},{64,192},{128,0},{192,64},{1,129},{65,193},{129,1},{193,65... | collective-permute-start | bytes 700424 | tf_op jit(solution)/shard_map/ppermute | solution.py:635
  8.8 16.1 %collective-permute-start.2 = (f32[456,128]{1,0:T(8,128)}, f32[456,128]{1,0:T(8,128)S(1)}, u32[]{:S(2)}, u32[]{:S(2)}) collective-permute-start(f32[456,128]{1,0:T(8,128)} %get-tuple-element.40), channel_id=1, source_target_pairs={{0,192},{64,128},{128,64},{192,0},{1,193},{65,129},{129,65},{193,1... | collective-permute-start | bytes 700424 | tf_op jit(solution)/shard_map/ppermute | solution.py:635
  8.8 5.3 %collective-permute-start.3 = (f32[4,16,128]{2,1,0:T(8,128)}, f32[4,16,128]{2,1,0:T(8,128)S(1)}, u32[]{:S(2)}, u32[]{:S(2)}) collective-permute-start(f32[4,16,128]{2,1,0:T(8,128)} %get-tuple-element.42), channel_id=1, source_target_pairs={{0,1},{1,2},{2,3},{3,4},{4,5},{5,6},{6,7},{7,0},{8,9},{9,10},{10,1... | collective-permute-start | bytes 98312 | tf_op jit(solution)/shard_map/ppermute | solution.py:629
  10.0 4.1 %collective-permute-start.4 = (f32[4,16,128]{2,1,0:T(8,128)}, f32[4,16,128]{2,1,0:T(8,128)S(1)}, u32[]{:S(2)}, u32[]{:S(2)}) collective-permute-start(f32[4,16,128]{2,1,0:T(8,128)} %get-tuple-element.43), channel_id=1, source_target_pairs={{1,0},{2,1},{3,2},{4,3},{5,4},{6,5},{7,6},{0,7},{9,8},{10,9},{11,1... | collective-permute-start | bytes 98312 | tf_op jit(solution)/shard_map/ppermute | solution.py:630
  14.1 1.0 copy-start
  15.1 3.9 %collective-permute-start.5 = (f32[2,4,16,128]{3,2,1,0:T(8,128)S(1)}, f32[2,4,16,128]{3,2,1,0:T(8,128)S(1)}, u32[]{:S(2)}, u32[]{:S(2)}) collective-permute-start(f32[2,4,16,128]{3,2,1,0:T(8,128)S(1)} %get-tuple-element.45), channel_id=1, source_target_pairs={{0,64},{64,0},{128,192},{192,128},{1,65},{65,1},{129,193},{193,129... | collective-permute-start | bytes 196616 | tf_op jit(solution)/shard_map/ppermute | solution.py:635
  15.2 6.2 %collective-permute-start.6 = (f32[2,4,16,128]{3,2,1,0:T(8,128)S(1)}, f32[2,4,16,128]{3,2,1,0:T(8,128)S(1)}, u32[]{:S(2)}, u32[]{:S(2)}) collective-permute-start(f32[2,4,16,128]{3,2,1,0:T(8,128)S(1)} %get-tuple-element.46), channel_id=1, source_target_pairs={{0,128},{64,192},{128,0},{192,64},{1,129},{65,193},{129,1},{193,65... | collective-permute-start | bytes 196616 | tf_op jit(solution)/shard_map/ppermute | solution.py:635
  19.1 5.8 %collective-permute-start.7 = (f32[2,4,16,128]{3,2,1,0:T(8,128)S(1)}, f32[2,4,16,128]{3,2,1,0:T(8,128)S(1)}, u32[]{:S(2)}, u32[]{:S(2)}) collective-permute-start(f32[2,4,16,128]{3,2,1,0:T(8,128)S(1)} %get-tuple-element.47), channel_id=1, source_target_pairs={{0,192},{64,128},{128,64},{192,0},{1,193},{65,129},{129,65},{193,1... | collective-permute-start | bytes 196616 | tf_op jit(solution)/shard_map/ppermute | solution.py:635
  24.9 0.9 copy-start.1
  26.2 27.7 %collective-permute-start.8 = (f32[72,8,128]{2,1,0:T(8,128)S(1)}, f32[72,8,128]{2,1,0:T(8,128)S(1)}, u32[]{:S(2)}, u32[]{:S(2)}) collective-permute-start(f32[72,8,128]{2,1,0:T(8,128)S(1)} %get-tuple-element.51), channel_id=1, source_target_pairs={{0,8},{8,16},{16,24},{24,32},{32,40},{40,48},{48,56},{56,0},{1,9},... | collective-permute-start | bytes 884744 | tf_op jit(solution)/shard_map/ppermute | solution.py:629
  31.8 22.1 %collective-permute-start.9 = (f32[72,8,128]{2,1,0:T(8,128)S(1)}, f32[72,8,128]{2,1,0:T(8,128)S(1)}, u32[]{:S(2)}, u32[]{:S(2)}) collective-permute-start(f32[72,8,128]{2,1,0:T(8,128)S(1)} %get-tuple-element.52), channel_id=1, source_target_pairs={{8,0},{16,8},{24,16},{32,24},{40,32},{48,40},{56,48},{0,56},{9,1},... | collective-permute-start | bytes 884744 | tf_op jit(solution)/shard_map/ppermute | solution.py:630
  59.7 10.0 %collective-permute-start.12 = (f32[8,128]{1,0:T(8,128)S(1)}, f32[8,128]{1,0:T(8,128)S(1)}, u32[]{:S(2)}, u32[]{:S(2)}) collective-permute-start(f32[8,128]{1,0:T(8,128)S(1)} %get-tuple-element.53), channel_id=1, source_target_pairs={{0,192},{64,128},{128,64},{192,0},{1,193},{65,129},{129,65},{193,1... | collective-permute-start | bytes 12296 | tf_op jit(solution)/shard_map/ppermute | solution.py:635
  62.3 7.4 %collective-permute-start.11 = (f32[8,128]{1,0:T(8,128)S(1)}, f32[8,128]{1,0:T(8,128)S(1)}, u32[]{:S(2)}, u32[]{:S(2)}) collective-permute-start(f32[8,128]{1,0:T(8,128)S(1)} %get-tuple-element.53), channel_id=1, source_target_pairs={{0,128},{64,192},{128,0},{192,64},{1,129},{65,193},{129,1},{193,65... | collective-permute-start | bytes 12296 | tf_op jit(solution)/shard_map/ppermute | solution.py:635
  62.3 7.4 %collective-permute-start.10 = (f32[8,128]{1,0:T(8,128)S(1)}, f32[8,128]{1,0:T(8,128)S(1)}, u32[]{:S(2)}, u32[]{:S(2)}) collective-permute-start(f32[8,128]{1,0:T(8,128)S(1)} %get-tuple-element.53), channel_id=1, source_target_pairs={{0,64},{64,0},{128,192},{192,128},{1,65},{65,1},{129,193},{193,129... | collective-permute-start | bytes 12296 | tf_op jit(solution)/shard_map/ppermute | solution.py:635
  67.8 18.2 %collective-permute-start.13 = (f32[13,8,8,128]{3,2,1,0:T(8,128)S(1)}, f32[13,8,8,128]{3,2,1,0:T(8,128)S(1)}, u32[]{:S(2)}, u32[]{:S(2)}) collective-permute-start(f32[13,8,8,128]{3,2,1,0:T(8,128)S(1)} %get-tuple-element.62), channel_id=1, source_target_pairs={{0,8},{8,16},{16,24},{24,32},{32,40},{40,48},{48,56},{56,0},{1,9},... | collective-permute-start | bytes 1277960 | tf_op jit(solution)/shard_map/ppermute | solution.py:629
  69.7 16.2 %collective-permute-start.14 = (f32[13,8,8,128]{3,2,1,0:T(8,128)S(1)}, f32[13,8,8,128]{3,2,1,0:T(8,128)S(1)}, u32[]{:S(2)}, u32[]{:S(2)}) collective-permute-start(f32[13,8,8,128]{3,2,1,0:T(8,128)S(1)} %get-tuple-element.63), channel_id=1, source_target_pairs={{8,0},{16,8},{24,16},{32,24},{40,32},{48,40},{56,48},{0,56},{9,1},... | collective-permute-start | bytes 1277960 | tf_op jit(solution)/shard_map/ppermute | solution.py:630
  95.5 6.0 %collective-permute-start.15 = (f32[13,2,16,128]{3,2,1,0:T(8,128)S(1)}, f32[13,2,16,128]{3,2,1,0:T(8,128)S(1)}, u32[]{:S(2)}, u32[]{:S(2)}) collective-permute-start(f32[13,2,16,128]{3,2,1,0:T(8,128)S(1)} %get-tuple-element.65), channel_id=1, source_target_pairs={{0,64},{64,0},{128,192},{192,128},{1,65},{65,1},{129,193},{193,129... | collective-permute-start | bytes 638984 | tf_op jit(solution)/shard_map/ppermute | solution.py:635
  96.0 12.3 %collective-permute-start.16 = (f32[13,2,16,128]{3,2,1,0:T(8,128)S(1)}, f32[13,2,16,128]{3,2,1,0:T(8,128)S(1)}, u32[]{:S(2)}, u32[]{:S(2)}) collective-permute-start(f32[13,2,16,128]{3,2,1,0:T(8,128)S(1)} %get-tuple-element.66), channel_id=1, source_target_pairs={{0,128},{64,192},{128,0},{192,64},{1,129},{65,193},{129,1},{193,65... | collective-permute-start | bytes 638984 | tf_op jit(solution)/shard_map/ppermute | solution.py:635
  99.2 11.8 %collective-permute-start.17 = (f32[13,2,16,128]{3,2,1,0:T(8,128)S(1)}, f32[13,2,16,128]{3,2,1,0:T(8,128)S(1)}, u32[]{:S(2)}, u32[]{:S(2)}) collective-permute-start(f32[13,2,16,128]{3,2,1,0:T(8,128)S(1)} %get-tuple-element.67), channel_id=1, source_target_pairs={{0,192},{64,128},{128,64},{192,0},{1,193},{65,129},{129,65},{193,1... | collective-permute-start | bytes 638984 | tf_op jit(solution)/shard_map/ppermute | solution.py:635

commit v5 on v4

--- a/solution.py
+++ b/solution.py
@@ -48,8 +48,7 @@
 
 
 def inverse(value):
-    guess = pl.reciprocal(value, approx=True)
-    return guess * (2.0 - value * guess)
+    return pltpu.reciprocal(value, approx=True)
 
 
 def pick(first, second, table):
@@ -482,7 +481,7 @@
             state[f, p] = zero
 
 
-def lead_kernel(
+def lead_part(
     timestep, tops, own, sides, low, high, out, rest, along_x, along_y, along_z, scales, kinds, top,
     state, stress, lead, moved, mids, inside, face_y, face_z,
 ):
@@ -531,7 +530,7 @@
     top[...] = jnp.full(top.shape, jnp.max(peak), jnp.float32)
 
 
-def rest_kernel(lead, rest, along_x, along_y, along_z, scales, out, up, down, moved, mids):
+def rest_part(lead, rest, along_x, along_y, along_z, scales, out, up, down, moved, mids):
     def put(f, p, value):
         out[f, p] = value
 
@@ -546,6 +545,18 @@
         return carry
 
     lax.fori_loop(0, PLANES // 2, messages, 0)
+
+
+def first_kernel(
+    timestep, tops, own, sides, low, high, out, out_rest, kinds, top, up, down,
+    rest, along_x, along_y, along_z, scales,
+    state, stress, lead, moved, mids, inside, face_y, face_z, rest_moved, rest_mids,
+):
+    lead_part(
+        timestep, tops, own, sides, low, high, out, rest, along_x, along_y, along_z, scales, kinds, top,
+        state, stress, lead, moved, mids, inside, face_y, face_z,
+    )
+    rest_part(out, rest, along_x, along_y, along_z, scales, out_rest, up, down, rest_moved, rest_mids)
 
 
 def second_kernel(
@@ -640,7 +651,7 @@
 
 
 def shards(density, energy, velocity, plastic_strain, damage, deviator, materials, timestep):
-    size_y, size_z = lax.axis_size("gy"), lax.axis_size("gz")
+    size_x, size_y, size_z = lax.axis_size("gx"), lax.axis_size("gy"), lax.axis_size("gz")
     all_fields = FIELDS + 1
     part = (PART_ROWS + 8, LANES)
     inputs = (density, energy, velocity, plastic_strain, damage, deviator, materials)
@@ -693,11 +704,13 @@
         (2, DEPTH, LANES),
     ]
     rest_scratch = [(REST, PLANES) + full, (2, LANES, LANES)]
-    lead, *rest, kinds, top = call(
-        lead_kernel,
+    lead, rest, kinds, top, up, down = call(
+        first_kernel,
         1,
-        [(LEAD, PLANES, OWN, LANES)] + left_over + [(PLANES,) + full, (8, LANES)],
-        scratch,
+        [(LEAD, PLANES, OWN, LANES), (REST, PLANES, OWN, LANES), (PLANES,) + full]
+        + [(size_x * size_y * size_z, LANES)]
+        + [(FIELDS, PLANES // 2, 8, LANES)] * 2,
+        left_over + scratch + rest_scratch,
         timestep,
         tops,
         state,
@@ -705,20 +718,8 @@
         low,
         high,
     )
-    others = swap_blocks([top] * 3)
-    rest, up, down = call(
-        rest_kernel,
-        0,
-        [(REST, PLANES, OWN, LANES)] + [(FIELDS, PLANES // 2, 8, LANES)] * 2,
-        rest_scratch,
-        lead,
-        *rest,
-        micros=5,
-    )
     low, high = ring_pair(up, down, "gy", list(range(size_y)))
-    for other in others:
-        top = jnp.maximum(top, other)
-    tops = lax.all_to_all(jnp.broadcast_to(top[:1], (size_y * size_z, LANES)), ("gy", "gz"), 0, 0)
+    tops = lax.all_to_all(top, ("gx", "gy", "gz"), 0, 0)
     mine, *parts = call(
         second_kernel,
         1,

time: 112 us -> 110 us (0.982)
  blocking collectives: 38.3 us -> 43.7 us
  starting transfers between devices: 29.8 us -> 25.7 us
  waiting for transfers between devices: 16.8 us -> 14.9 us
  Pallas kernels: 24.6 us -> 23.3 us
    all_to_all x1, blocking collectives: 16.2 us -> 21.6 us  [shards(): tops = lax.all_to_all(top, ('gx', 'gy', 'gz'), 0, 0)]
    ppermute x12 -> x9, starting transfers between devices: 18.4 us -> 14.9 us  [swap_block(): lax.ppermute(part, 'gx', [(i, i ^ k) for i in range(lax.axis_size('gx'))])]
    ppermute x12 -> x9, waiting for transfers between devices: 15.2 us -> 13.4 us  [swap_block(): lax.ppermute(part, 'gx', [(i, i ^ k) for i in range(lax.axis_size('gx'))])]
    pallas_call x6 -> x5, Pallas kernels: 21.4 us -> 20 us  [call(): pl.pallas_call(kernel, out_shape=[jax.ShapeDtypeStruct(shape, jnp.float32...]
  transfers between devices with their start and end apart: 18 -> 15, of which waited for: 6 -> 6; matrix products, arithmetic and copies ran while one was open for 0% -> 0% of each run, Pallas kernels for 4% -> 0%
where the time goes in v5:
time: 110 us
  blocking collectives  43.7 us (40%)
  starting transfers between devices  25.7 us (23%)
  Pallas kernels  23.3 us (21%)
  waiting for transfers between devices  14.9 us (14%)
  local copies, waits for them, and re-layouts  1.89 us (2%)
    all_to_all x1, blocking collectives, shards(): tops = lax.all_to_all(top, ('gy', 'gz'), 0, 0)  22.1 us
    all_to_all x1, blocking collectives, shards(): tops = lax.all_to_all(top, ('gx', 'gy', 'gz'), 0, 0)  21.6 us
    pallas_call x5, Pallas kernels, call(): pl.pallas_call(kernel, out_shape=[jax.ShapeDtypeStruct(shape, jnp.float32...  20 us
    ppermute x9, starting transfers between devices, swap_block(): lax.ppermute(part, 'gx', [(i, i ^ k) for i in range(lax.axis_size('gx'))])  14.9 us
    ppermute x9, waiting for transfers between devices, swap_block(): lax.ppermute(part, 'gx', [(i, i ^ k) for i in range(lax.axis_size('gx'))])  13.4 us
    ppermute x3, starting transfers between devices, ring_pair(): low = lax.ppermute(to_next, axes, list(zip(order, after)))  8.17 us
    pallas_call x1, Pallas kernels, shards(): pl.pallas_call(pack_kernel, out_shape=[jax.ShapeDtypeStruct(shape, jnp.fl...  3.29 us
    ppermute x3, starting transfers between devices, ring_pair(): high = lax.ppermute(to_last, axes, list(zip(after, order)))  2.63 us
  transfers between devices with their start and end apart: 15, of which 6 were waited for; matrix products, arithmetic and copies ran while one was open for 0% of the time, Pallas kernels for 0%

profile of v5, /device:TPU:1, one launch (start us, length us, event | category | flops | bytes accessed | tf_op | source)
XLA Modules:
  0.0 110.2 jit_solution(16723396898945856033)
XLA Ops:
  0.6 3.3 %shard_map.127 = (f32[456,128]{1,0:T(8,128)}, f32[456,128]{1,0:T(8,128)}, f32[456,128]{1,0:T(8,128)}, f32[456,128]{1,0:T(8,128)}, f32[4,2,4,16,128]{4,3,2,1,0:T(...) custom-call(f32[4,16,256]{2,1,0:T(8,128)} %args_0_.4, f32[4,16,256]{2,1,0:T(8,128)} %args_1_.4, ...), custom_call_target="tpu_custom_call" | custom-call | tf_op jit(solution)/shard_map/pallas_call | solution.py:659
  3.9 2.2 %collective-permute-start = (f32[456,128]{1,0:T(8,128)}, f32[456,128]{1,0:T(8,128)S(1)}, u32[]{:S(2)}, u32[]{:S(2)}) collective-permute-start(f32[456,128]{1,0:T(8,128)} %get-tuple-element.33), channel_id=1, source_target_pairs={{0,64},{64,0},{128,192},{192,128},{1,65},{65,1},{129,193},{193,129... | collective-permute-start | bytes 700424 | tf_op jit(solution)/shard_map/ppermute | solution.py:646
  6.2 2.6 %collective-permute-start.1 = (f32[456,128]{1,0:T(8,128)}, f32[456,128]{1,0:T(8,128)S(1)}, u32[]{:S(2)}, u32[]{:S(2)}) collective-permute-start(f32[456,128]{1,0:T(8,128)} %get-tuple-element.34), channel_id=1, source_target_pairs={{0,128},{64,192},{128,0},{192,64},{1,129},{65,193},{129,1},{193,65... | collective-permute-start | bytes 700424 | tf_op jit(solution)/shard_map/ppermute | solution.py:646
  8.8 0.0 collective-permute-start.2
  8.8 1.2 %collective-permute-start.3 = (f32[4,16,128]{2,1,0:T(8,128)}, f32[4,16,128]{2,1,0:T(8,128)S(1)}, u32[]{:S(2)}, u32[]{:S(2)}) collective-permute-start(f32[4,16,128]{2,1,0:T(8,128)} %get-tuple-element.37), channel_id=1, source_target_pairs={{0,1},{1,2},{2,3},{3,4},{4,5},{5,6},{6,7},{7,0},{8,9},{9,10},{10,1... | collective-permute-start | bytes 98312 | tf_op jit(solution)/shard_map/ppermute | solution.py:640
  10.0 2.6 %collective-permute-start.4 = (f32[4,16,128]{2,1,0:T(8,128)}, f32[4,16,128]{2,1,0:T(8,128)S(1)}, u32[]{:S(2)}, u32[]{:S(2)}) collective-permute-start(f32[4,16,128]{2,1,0:T(8,128)} %get-tuple-element.38), channel_id=1, source_target_pairs={{1,0},{2,1},{3,2},{4,3},{5,4},{6,5},{7,6},{0,7},{9,8},{10,9},{11,1... | collective-permute-start | bytes 98312 | tf_op jit(solution)/shard_map/ppermute | solution.py:641
  12.6 1.5 %collective-permute-done.3.from_below = f32[4,16,128]{2,1,0:T(8,128)S(1)} collective-permute-done((f32[4,16,128]{2,1,0:T(8,128)}, f32[4,16,128]{2,1,0:T(8,128)S(1)}, u32[]{:S(2)}, u32[]{:S(2)}) %collective-permute-start.3) | collective-permute-done | bytes 32800 | tf_op jit(solution)/shard_map/ppermute | solution.py:640
  14.1 0.0 collective-permute-done.4.from_above
  14.1 0.9 copy-done
  15.1 0.1 collective-permute-start.5
  15.2 3.8 %collective-permute-start.6 = (f32[2,4,16,128]{3,2,1,0:T(8,128)S(1)}, f32[2,4,16,128]{3,2,1,0:T(8,128)S(1)}, u32[]{:S(2)}, u32[]{:S(2)}) collective-permute-start(f32[2,4,16,128]{3,2,1,0:T(8,128)S(1)} %get-tuple-element.41), channel_id=1, source_target_pairs={{0,128},{64,192},{128,0},{192,64},{1,129},{65,193},{129,1},{193,65... | collective-permute-start | bytes 196616 | tf_op jit(solution)/shard_map/ppermute | solution.py:646
  19.1 2.2 %collective-permute-start.7 = (f32[2,4,16,128]{3,2,1,0:T(8,128)S(1)}, f32[2,4,16,128]{3,2,1,0:T(8,128)S(1)}, u32[]{:S(2)}, u32[]{:S(2)}) collective-permute-start(f32[2,4,16,128]{3,2,1,0:T(8,128)S(1)} %get-tuple-element.42), channel_id=1, source_target_pairs={{0,192},{64,128},{128,64},{192,0},{1,193},{65,129},{129,65},{193,1... | collective-permute-start | bytes 196616 | tf_op jit(solution)/shard_map/ppermute | solution.py:646
  21.3 0.2 collective-permute-done.6.z2
  21.5 3.4 %collective-permute-done.7.z3 = f32[2,4,16,128]{3,2,1,0:T(8,128)S(1)} collective-permute-done((f32[2,4,16,128]{3,2,1,0:T(8,128)S(1)}, f32[2,4,16,128]{3,2,1,0:T(8,128)S(1)}, u32[]{:S(2)}, u32[]{:S(2)}) %collective-permute-start.7) | collective-permute-done | bytes 65568 | tf_op jit(solution)/shard_map/ppermute | solution.py:646
  24.9 0.0 collective-permute-done.from1
  24.9 0.9 copy-done.1
  25.8 0.4 shard_map.129
  26.2 5.6 %collective-permute-start.8 = (f32[72,8,128]{2,1,0:T(8,128)S(1)}, f32[72,8,128]{2,1,0:T(8,128)S(1)}, u32[]{:S(2)}, u32[]{:S(2)}) collective-permute-start(f32[72,8,128]{2,1,0:T(8,128)S(1)} %get-tuple-element.46), channel_id=1, source_target_pairs={{0,8},{8,16},{16,24},{24,32},{32,40},{40,48},{48,56},{56,0},{1,9},... | collective-permute-start | bytes 884744 | tf_op jit(solution)/shard_map/ppermute | solution.py:640
  31.8 22.1 %all_to_all.22 = f32[64,1,128]{2,1,0:T(1,128)S(1)} all-to-all(f32[64,1,128]{2,1,0:T(1,128)S(1)} %bitcast.11), channel_id=1, replica_groups=mesh['gx'=4,'gy'=8,'gz'=8] {'gy','gz'}, dimensions={0} | all-to-all | bytes 65536 | tf_op jit(solution)/shard_map/all_to_all | solution.py:687
  53.9 0.0 collective-permute-done.8.low
  53.9 0.0 collective-permute-done.9.high
  53.9 9.8 %shard_map.130 = (f32[4,16,16,128]{3,2,1,0:T(8,128)S(1)}, f32[9,16,16,128]{3,2,1,0:T(8,128)S(1)}, f32[16,24,128]{2,1,0:T(8,128)S(1)}, f32[256,128]{1,0:T(8,128)S...) custom-call(f32[2]{0:T(128)S(1)} %copy-done.2, f32[64,128]{1,0:T(8,128)S(1)} %bitcast.9, ...), custom_call_target="tpu_custom_call" | custom-call | bytes 3600000 | tf_op jit(solution)/shard_map/pallas_call | solution.py:627
  63.7 1.4 %collective-permute-start.10 = (f32[13,8,8,128]{3,2,1,0:T(8,128)S(1)}, f32[13,8,8,128]{3,2,1,0:T(8,128)S(1)}, u32[]{:S(2)}, u32[]{:S(2)}) collective-permute-start(f32[13,8,8,128]{3,2,1,0:T(8,128)S(1)} %get-tuple-element.52), channel_id=1, source_target_pairs={{0,8},{8,16},{16,24},{24,32},{32,40},{40,48},{48,56},{56,0},{1,9},... | collective-permute-start | bytes 1277960 | tf_op jit(solution)/shard_map/ppermute | solution.py:640
  65.1 21.6 %all_to_all.23 = f32[256,1,128]{2,1,0:T(1,128)S(1)} all-to-all(f32[256,1,128]{2,1,0:T(1,128)S(1)} %bitcast.10), channel_id=1, replica_groups=mesh['gx'=4,'gy'=8,'gz'=8] {'gx','gy','gz'}, dimensions={0} | all-to-all | bytes 262144 | tf_op jit(solution)/shard_map/all_to_all | solution.py:722
  86.7 8.7 %shard_map.131 = (f32[13,2,16,128]{3,2,1,0:T(8,128)S(1)}, f32[13,2,16,128]{3,2,1,0:T(8,128)S(1)}, f32[13,2,16,128]{3,2,1,0:T(8,128)S(1)}, f32[13,2,16,128]{3,2,1,0:T(8,128)S(1)}) custom-call(f32[2]{0:T(128)S(1)} %copy-done.2, f32[256,128]{1,0:T(8,128)S(1)} %bitcast.8, f32[4,16,16,128]{3,2,1,0:T(8,128)S(1)} %get-tuple-element.49.own_lead, ...), custom_call_target="tpu_custom_call" | custom-call | bytes 3600000 | tf_op jit(solution)/shard_map/pallas_call | solution.py:627
  95.4 0.1 collective-permute-start.12
  95.5 1.8 %collective-permute-start.13 = (f32[13,2,16,128]{3,2,1,0:T(8,128)S(1)}, f32[13,2,16,128]{3,2,1,0:T(8,128)S(1)}, u32[]{:S(2)}, u32[]{:S(2)}) collective-permute-start(f32[13,2,16,128]{3,2,1,0:T(8,128)S(1)} %get-tuple-element.56), channel_id=1, source_target_pairs={{0,128},{64,192},{128,0},{192,64},{1,129},{65,193},{129,1},{193,65... | collective-permute-start | bytes 638984 | tf_op jit(solution)/shard_map/ppermute | solution.py:646
  97.3 2.0 %collective-permute-start.14 = (f32[13,2,16,128]{3,2,1,0:T(8,128)S(1)}, f32[13,2,16,128]{3,2,1,0:T(8,128)S(1)}, u32[]{:S(2)}, u32[]{:S(2)}) collective-permute-start(f32[13,2,16,128]{3,2,1,0:T(8,128)S(1)} %get-tuple-element.57), channel_id=1, source_target_pairs={{0,192},{64,128},{128,64},{192,0},{1,193},{65,129},{129,65},{193,1... | collective-permute-start | bytes 638984 | tf_op jit(solution)/shard_map/ppermute | solution.py:646
  99.3 1.9 %collective-permute-done.12.from1 = f32[13,2,16,128]{3,2,1,0:T(8,128)S(1)} collective-permute-done((f32[13,2,16,128]{3,2,1,0:T(8,128)S(1)}, f32[13,2,16,128]{3,2,1,0:T(8,128)S(1)}, u32[]{:S(2)}, u32[]{:S(2)}) %collective-permute-start.12) | collective-permute-done | bytes 213024 | tf_op jit(solution)/shard_map/ppermute | solution.py:646
  101.2 4.8 %collective-permute-done.13.from2 = f32[13,2,16,128]{3,2,1,0:T(8,128)S(1)} collective-permute-done((f32[13,2,16,128]{3,2,1,0:T(8,128)S(1)}, f32[13,2,16,128]{3,2,1,0:T(8,128)S(1)}, u32[]{:S(2)}, u32[]{:S(2)}) %collective-permute-start.13) | collective-permute-done | bytes 213024 | tf_op jit(solution)/shard_map/ppermute | solution.py:646
  106.1 3.1 %collective-permute-done.14.from3 = f32[13,2,16,128]{3,2,1,0:T(8,128)S(1)} collective-permute-done((f32[13,2,16,128]{3,2,1,0:T(8,128)S(1)}, f32[13,2,16,128]{3,2,1,0:T(8,128)S(1)}, u32[]{:S(2)}, u32[]{:S(2)}) %collective-permute-start.14) | collective-permute-done | bytes 213024 | tf_op jit(solution)/shard_map/ppermute | solution.py:646
  109.1 1.1 %shard_map.132 = (f32[4,16,256]{2,1,0:T(8,128)}, f32[4,16,256]{2,1,0:T(8,128)}, f32[3,4,16,256]{3,2,1,0:T(8,128)}, f32[4,16,256]{2,1,0:T(8,128)}, f32[4,16,256]{2,1,0:T(8,128)}, /*index=5*/f32[6,4,16,256]{3,2,1,0:T(8,128)}) custom-call(f32[13,2,16,128]{3,2,1,0:T(8,128)S(1)} %get-tuple-element.54.mine, f32[13,2,16,128]{3,2,1,0:T(8,128)S(1)} %collective-permute-done.12.from1, ...), custom_call_target="tpu_custom_call" | custom-call | bytes 3600000 | tf_op jit(solution)/shard_map/pallas_call | solution.py:627
  (12 shorter events, 0.0 us)
Async XLA Ops:
  0.6 53.3 %copy-start.2 = (f32[2]{0:T(128)S(1)}, f32[2]{0:T(128)}, u32[]{:S(2)}) copy-start(f32[2]{0:T(128)} %timestep.3) | copy-start | bytes 28
  3.9 21.0 %collective-permute-start = (f32[456,128]{1,0:T(8,128)}, f32[456,128]{1,0:T(8,128)S(1)}, u32[]{:S(2)}, u32[]{:S(2)}) collective-permute-start(f32[456,128]{1,0:T(8,128)} %get-tuple-element.33), channel_id=1, source_target_pairs={{0,64},{64,0},{128,192},{192,128},{1,65},{65,1},{129,193},{193,129... | collective-permute-start | bytes 700424 | tf_op jit(solution)/shard_map/ppermute | solution.py:646
  6.2 18.7 %collective-permute-start.1 = (f32[456,128]{1,0:T(8,128)}, f32[456,128]{1,0:T(8,128)S(1)}, u32[]{:S(2)}, u32[]{:S(2)}) collective-permute-start(f32[456,128]{1,0:T(8,128)} %get-tuple-element.34), channel_id=1, source_target_pairs={{0,128},{64,192},{128,0},{192,64},{1,129},{65,193},{129,1},{193,65... | collective-permute-start | bytes 700424 | tf_op jit(solution)/shard_map/ppermute | solution.py:646
  8.8 16.1 %collective-permute-start.2 = (f32[456,128]{1,0:T(8,128)}, f32[456,128]{1,0:T(8,128)S(1)}, u32[]{:S(2)}, u32[]{:S(2)}) collective-permute-start(f32[456,128]{1,0:T(8,128)} %get-tuple-element.35), channel_id=1, source_target_pairs={{0,192},{64,128},{128,64},{192,0},{1,193},{65,129},{129,65},{193,1... | collective-permute-start | bytes 700424 | tf_op jit(solution)/shard_map/ppermute | solution.py:646
  8.8 5.3 %collective-permute-start.3 = (f32[4,16,128]{2,1,0:T(8,128)}, f32[4,16,128]{2,1,0:T(8,128)S(1)}, u32[]{:S(2)}, u32[]{:S(2)}) collective-permute-start(f32[4,16,128]{2,1,0:T(8,128)} %get-tuple-element.37), channel_id=1, source_target_pairs={{0,1},{1,2},{2,3},{3,4},{4,5},{5,6},{6,7},{7,0},{8,9},{9,10},{10,1... | collective-permute-start | bytes 98312 | tf_op jit(solution)/shard_map/ppermute | solution.py:640
  10.0 4.1 %collective-permute-start.4 = (f32[4,16,128]{2,1,0:T(8,128)}, f32[4,16,128]{2,1,0:T(8,128)S(1)}, u32[]{:S(2)}, u32[]{:S(2)}) collective-permute-start(f32[4,16,128]{2,1,0:T(8,128)} %get-tuple-element.38), channel_id=1, source_target_pairs={{1,0},{2,1},{3,2},{4,3},{5,4},{6,5},{7,6},{0,7},{9,8},{10,9},{11,1... | collective-permute-start | bytes 98312 | tf_op jit(solution)/shard_map/ppermute | solution.py:641
  14.1 1.0 copy-start
  15.1 3.9 %collective-permute-start.5 = (f32[2,4,16,128]{3,2,1,0:T(8,128)S(1)}, f32[2,4,16,128]{3,2,1,0:T(8,128)S(1)}, u32[]{:S(2)}, u32[]{:S(2)}) collective-permute-start(f32[2,4,16,128]{3,2,1,0:T(8,128)S(1)} %get-tuple-element.40), channel_id=1, source_target_pairs={{0,64},{64,0},{128,192},{192,128},{1,65},{65,1},{129,193},{193,129... | collective-permute-start | bytes 196616 | tf_op jit(solution)/shard_map/ppermute | solution.py:646
  15.2 6.2 %collective-permute-start.6 = (f32[2,4,16,128]{3,2,1,0:T(8,128)S(1)}, f32[2,4,16,128]{3,2,1,0:T(8,128)S(1)}, u32[]{:S(2)}, u32[]{:S(2)}) collective-permute-start(f32[2,4,16,128]{3,2,1,0:T(8,128)S(1)} %get-tuple-element.41), channel_id=1, source_target_pairs={{0,128},{64,192},{128,0},{192,64},{1,129},{65,193},{129,1},{193,65... | collective-permute-start | bytes 196616 | tf_op jit(solution)/shard_map/ppermute | solution.py:646
  19.1 5.8 %collective-permute-start.7 = (f32[2,4,16,128]{3,2,1,0:T(8,128)S(1)}, f32[2,4,16,128]{3,2,1,0:T(8,128)S(1)}, u32[]{:S(2)}, u32[]{:S(2)}) collective-permute-start(f32[2,4,16,128]{3,2,1,0:T(8,128)S(1)} %get-tuple-element.42), channel_id=1, source_target_pairs={{0,192},{64,128},{128,64},{192,0},{1,193},{65,129},{129,65},{193,1... | collective-permute-start | bytes 196616 | tf_op jit(solution)/shard_map/ppermute | solution.py:646
  24.9 0.9 copy-start.1
  26.2 27.7 %collective-permute-start.8 = (f32[72,8,128]{2,1,0:T(8,128)S(1)}, f32[72,8,128]{2,1,0:T(8,128)S(1)}, u32[]{:S(2)}, u32[]{:S(2)}) collective-permute-start(f32[72,8,128]{2,1,0:T(8,128)S(1)} %get-tuple-element.46), channel_id=1, source_target_pairs={{0,8},{8,16},{16,24},{24,32},{32,40},{40,48},{48,56},{56,0},{1,9},... | collective-permute-start | bytes 884744 | tf_op jit(solution)/shard_map/ppermute | solution.py:640
  31.8 22.1 %collective-permute-start.9 = (f32[72,8,128]{2,1,0:T(8,128)S(1)}, f32[72,8,128]{2,1,0:T(8,128)S(1)}, u32[]{:S(2)}, u32[]{:S(2)}) collective-permute-start(f32[72,8,128]{2,1,0:T(8,128)S(1)} %get-tuple-element.47), channel_id=1, source_target_pairs={{8,0},{16,8},{24,16},{32,24},{40,32},{48,40},{56,48},{0,56},{9,1},... | collective-permute-start | bytes 884744 | tf_op jit(solution)/shard_map/ppermute | solution.py:641
  63.7 23.0 %collective-permute-start.10 = (f32[13,8,8,128]{3,2,1,0:T(8,128)S(1)}, f32[13,8,8,128]{3,2,1,0:T(8,128)S(1)}, u32[]{:S(2)}, u32[]{:S(2)}) collective-permute-start(f32[13,8,8,128]{3,2,1,0:T(8,128)S(1)} %get-tuple-element.52), channel_id=1, source_target_pairs={{0,8},{8,16},{16,24},{24,32},{32,40},{40,48},{48,56},{56,0},{1,9},... | collective-permute-start | bytes 1277960 | tf_op jit(solution)/shard_map/ppermute | solution.py:640
  65.1 21.6 %collective-permute-start.11 = (f32[13,8,8,128]{3,2,1,0:T(8,128)S(1)}, f32[13,8,8,128]{3,2,1,0:T(8,128)S(1)}, u32[]{:S(2)}, u32[]{:S(2)}) collective-permute-start(f32[13,8,8,128]{3,2,1,0:T(8,128)S(1)} %get-tuple-element.53), channel_id=1, source_target_pairs={{8,0},{16,8},{24,16},{32,24},{40,32},{48,40},{56,48},{0,56},{9,1},... | collective-permute-start | bytes 1277960 | tf_op jit(solution)/shard_map/ppermute | solution.py:641
  95.4 5.8 %collective-permute-start.12 = (f32[13,2,16,128]{3,2,1,0:T(8,128)S(1)}, f32[13,2,16,128]{3,2,1,0:T(8,128)S(1)}, u32[]{:S(2)}, u32[]{:S(2)}) collective-permute-start(f32[13,2,16,128]{3,2,1,0:T(8,128)S(1)} %get-tuple-element.55), channel_id=1, source_target_pairs={{0,64},{64,0},{128,192},{192,128},{1,65},{65,1},{129,193},{193,129... | collective-permute-start | bytes 638984 | tf_op jit(solution)/shard_map/ppermute | solution.py:646
  95.5 10.6 %collective-permute-start.13 = (f32[13,2,16,128]{3,2,1,0:T(8,128)S(1)}, f32[13,2,16,128]{3,2,1,0:T(8,128)S(1)}, u32[]{:S(2)}, u32[]{:S(2)}) collective-permute-start(f32[13,2,16,128]{3,2,1,0:T(8,128)S(1)} %get-tuple-element.56), channel_id=1, source_target_pairs={{0,128},{64,192},{128,0},{192,64},{1,129},{65,193},{129,1},{193,65... | collective-permute-start | bytes 638984 | tf_op jit(solution)/shard_map/ppermute | solution.py:646
  97.3 11.8 %collective-permute-start.14 = (f32[13,2,16,128]{3,2,1,0:T(8,128)S(1)}, f32[13,2,16,128]{3,2,1,0:T(8,128)S(1)}, u32[]{:S(2)}, u32[]{:S(2)}) collective-permute-start(f32[13,2,16,128]{3,2,1,0:T(8,128)S(1)} %get-tuple-element.57), channel_id=1, source_target_pairs={{0,192},{64,128},{128,64},{192,0},{1,193},{65,129},{129,65},{193,1... | collective-permute-start | bytes 638984 | tf_op jit(solution)/shard_map/ppermute | solution.py:646

commit v6 on v4

--- a/solution.py
+++ b/solution.py
@@ -48,8 +48,7 @@
 
 
 def inverse(value):
-    guess = pl.reciprocal(value, approx=True)
-    return guess * (2.0 - value * guess)
+    return pltpu.reciprocal(value, approx=True)
 
 
 def pick(first, second, table):
@@ -84,14 +83,14 @@
         pltpu.make_async_copy(source, buffer, arrived.at[i])
         for i, (source, buffer) in enumerate(zip(sources, buffers))
     ]
-    for copy in copies:
-        copy.start()
-    for copy in copies:
-        copy.wait()
+    for i in (2, 6, 0, 1, 3, 4, 5):
+        copies[i].start()
     dens, ener, vel, plas, dama, devi, mat = buffers
     me = position()[0]
     refs = [dens, ener] + [vel.at[i] for i in range(3)] + [plas, dama]
     refs = refs + [devi.at[i] for i in range(6)] + [mat]
+    copies[2].wait()
+    copies[6].wait()
     peak = None
     for x in range(4):
         for t in range(2):
@@ -102,14 +101,16 @@
             speed = speed + pick(kind == 0, kind == 1, sound_table)
             peak = speed if peak is None else jnp.maximum(peak, speed)
     peak = jnp.full((8, LANES), jnp.max(peak), jnp.float32)
+    for out in (own, to1, to2, to3):
+        out[PART_ROWS:] = peak
     left = iota((OWN, LANES), 1) < HALF
-    for k, out in enumerate((own, to1, to2, to3)):
-        out[PART_ROWS:] = peak
-        target = me ^ k
-        cols = pl.ds(pl.multiple_of((target >> 1) * LANES, LANES), LANES)
-        odd = target & 1
-        side = left == (odd == 0)
-        for f in range(FIELDS + 1):
+
+    def pack(f):
+        for k, out in enumerate((own, to1, to2, to3)):
+            target = me ^ k
+            cols = pl.ds(pl.multiple_of((target >> 1) * LANES, LANES), LANES)
+            odd = target & 1
+            side = left == (odd == 0)
             for j in range(2):
                 even_plane = refs[f][2 * j, :, cols].astype(jnp.float32)
                 odd_plane = refs[f][2 * j + 1, :, cols].astype(jnp.float32)
@@ -117,6 +118,13 @@
                 turns = jnp.where(odd == 1, even_plane, odd_plane)
                 out[part_rows(f, j)] = jnp.where(side, stays, roll(turns, HALF, 1))
 
+    for f in (2, 3, 4, 13):
+        pack(f)
+    for copy, fields in ((0, (0,)), (1, (1,)), (3, (5,)), (4, (6,)), (5, range(7, 13))):
+        copies[copy].wait()
+        for f in fields:
+            pack(f)
+
     group = iota((OWN, LANES), 1) >> 3
 
     def plane(x, carry):
@@ -124,13 +132,17 @@
         below, above = [zero] * 5, [zero] * 5
         for f in range(FIELDS + 1):
             in_below, in_above = group == (f + 7) % 16, group == f
+            far_below, far_above = group == (f + 15) % 16, group == (f + 8) % 16
             for t in range(2):
                 tile = refs[f][x, :, t * LANES : (t + 1) * LANES].astype(jnp.float32)
-                near, far = roll(tile, 8 * f, 1), roll(tile, 8 * f - HALF, 1)
-                below[2 * t + 1] = jnp.where(in_below, near, below[2 * t + 1])
-                below[2 * t + 2] = jnp.where(in_below, far, below[2 * t + 2])
-                above[2 * t] = jnp.where(in_above, near, above[2 * t])
-                above[2 * t + 1] = jnp.where(in_above, far, above[2 * t + 1])
+                tile = roll(tile, 8 * f, 1)
+                below[2 * t + 1] = jnp.where(in_below, tile, below[2 * t + 1])
+                below[2 * t + 2] = jnp.where(far_below, tile, below[2 * t + 2])
+                above[2 * t] = jnp.where(in_above, tile, above[2 * t])
+                above[2 * t + 1] = jnp.where(far_above, tile, above[2 * t + 1])
+        for t in range(2):
+            below[2 * t + 2] = roll(below[2 * t + 2], HALF, 1)
+            above[2 * t + 1] = roll(above[2 * t + 1], HALF, 1)
         for g in range(4):
             edges[g, 0, x] = below[g]
             edges[g, 1, x] = above[g + 1]
@@ -398,6 +410,12 @@
     return jnp.concatenate([value[: HALF + 8], value[LANES - 8 :]], axis=0)
 
 
+def turn_twice(value, put, f, group):
+    value = jnp.concatenate([value[:HALF], value[:HALF]], axis=0).T
+    for i in range(GROUP):
+        put(f, GROUP * group + i, value[OWN * i : OWN * (i + 1)])
+
+
 def turn_back(value, put, f, group):
     gap = jnp.zeros((LANES - DEPTH, LANES), jnp.float32)
     value = jnp.concatenate([value[: HALF + 8], gap, value[HALF + 8 :]], axis=0).T
@@ -412,7 +430,7 @@
 ORDER = tuple((LEAD_AT + REST_AT).index(f) for f in range(FIELDS))
 
 
-def sweep_lead(dt, lead, moved, mids, courants, scales, inside, face_y, face_z, put):
+def sweep_lead(dt, lead, moved, mids, courants, scales, inside, face_y, face_z, put, back):
     along_x, along_y, along_z = courants
     first_courants(dt, lead, along_x, inside)
     for f in range(LEAD):
@@ -439,10 +457,10 @@
         value = rolled_change(density, positive, courant, weight)
         scale = jnp.where(ok, inverse(jnp.where(ok, value, 1.0)), 0.0)
         scales[group] = scale
-        turn_back(jnp.where(ok, value, 0.0), put, 0, group)
+        back(jnp.where(ok, value, 0.0), put, 0, group)
         for f in range(1, LEAD):
             value = turned(mids.at[group, f]) if f < 3 else momentum
-            turn_back(rolled_change(value, positive, courant, weight) * scale, put, f, group)
+            back(rolled_change(value, positive, courant, weight) * scale, put, f, group)
 
     second(0)
     second(1)
@@ -450,7 +468,7 @@
     third(1)
 
 
-def sweep_rest(rest, moved, mids, courants, scales, put):
+def sweep_rest(rest, moved, mids, courants, scales, put, back):
     along_x, along_y, along_z = courants
     last = REST - 1
 
@@ -461,7 +479,7 @@
         for group in range(2):
             courant = along_z[group]
             value = rolled_change(turned(mids.at[group]), courant > 0.0, courant, weigh(courant))
-            turn_back(value * scales[group], put, f, group)
+            back(value * scales[group], put, f, group)
             second(jnp.minimum(f + 1, last), group)
         return carry
 
@@ -482,7 +500,7 @@
             state[f, p] = zero
 
 
-def lead_kernel(
+def lead_part(
     timestep, tops, own, sides, low, high, out, rest, along_x, along_y, along_z, scales, kinds, top,
     state, stress, lead, moved, mids, inside, face_y, face_z,
 ):
@@ -516,7 +534,7 @@
         out[f, p] = value
 
     sweep_lead(
-        dt, lead, moved, mids, (along_x, along_y, along_z), scales, inside, face_y, face_z, put
+        dt, lead, moved, mids, (along_x, along_y, along_z), scales, inside, face_y, face_z, put, turn_back
     )
 
     def peaks(p, peak):
@@ -531,11 +549,11 @@
     top[...] = jnp.full(top.shape, jnp.max(peak), jnp.float32)
 
 
-def rest_kernel(lead, rest, along_x, along_y, along_z, scales, out, up, down, moved, mids):
+def rest_part(lead, rest, along_x, along_y, along_z, scales, out, up, down, moved, mids):
     def put(f, p, value):
         out[f, p] = value
 
-    sweep_rest(rest, moved, mids, (along_x, along_y, along_z), scales, put)
+    sweep_rest(rest, moved, mids, (along_x, along_y, along_z), scales, put, turn_back)
 
     def messages(i, carry):
         for f in range(FIELDS):
@@ -576,8 +594,8 @@
     def put_rest(f, p, value):
         out[LEAD + f, p] = value
 
-    sweep_lead(dt, lead, moved, mids, courants, scales, inside, face_y, face_z, put_lead)
-    sweep_rest(rest, rest_moved, rest_mids, courants, scales, put_rest)
+    sweep_lead(dt, lead, moved, mids, courants, scales, inside, face_y, face_z, put_lead, turn_twice)
+    sweep_rest(rest, rest_moved, rest_mids, courants, scales, put_rest, turn_twice)
     me = position()[0]
     for k, part in enumerate((mine, to1, to2, to3)):
         pack_block(out, me ^ k, part)
@@ -589,7 +607,7 @@
     for f in range(FIELDS):
         for j in range(2):
             even, odd = out[ORDER[f], first + 2 * j], out[ORDER[f], first + 2 * j + 1]
-            part[f, j] = jnp.where(left, even, roll(odd, HALF, 1))
+            part[f, j] = jnp.where(left, even, odd)
 
 
 def unpack_kernel(mine, from1, from2, from3, dens, ener, vel, plas, dama, devi, held):
@@ -640,7 +658,7 @@
 
 
 def shards(density, energy, velocity, plastic_strain, damage, deviator, materials, timestep):
-    size_y, size_z = lax.axis_size("gy"), lax.axis_size("gz")
+    size_x, size_y, size_z = lax.axis_size("gx"), lax.axis_size("gy"), lax.axis_size("gz")
     all_fields = FIELDS + 1
     part = (PART_ROWS + 8, LANES)
     inputs = (density, energy, velocity, plastic_strain, damage, deviator, materials)
@@ -694,9 +712,9 @@
     ]
     rest_scratch = [(REST, PLANES) + full, (2, LANES, LANES)]
     lead, *rest, kinds, top = call(
-        lead_kernel,
+        lead_part,
         1,
-        [(LEAD, PLANES, OWN, LANES)] + left_over + [(PLANES,) + full, (8, LANES)],
+        [(LEAD, PLANES, OWN, LANES)] + left_over + [(PLANES,) + full, (size_x * size_y * size_z, LANES)],
         scratch,
         timestep,
         tops,
@@ -705,20 +723,18 @@
         low,
         high,
     )
-    others = swap_blocks([top] * 3)
+    tops = lax.all_to_all(top, ("gx", "gy", "gz"), 0, 0)
     rest, up, down = call(
-        rest_kernel,
+        rest_part,
         0,
         [(REST, PLANES, OWN, LANES)] + [(FIELDS, PLANES // 2, 8, LANES)] * 2,
         rest_scratch,
         lead,
         *rest,
-        micros=5,
-    )
+        micros=20,
+    )
+    tops, up, down = lax.optimization_barrier((tops, up, down))
     low, high = ring_pair(up, down, "gy", list(range(size_y)))
-    for other in others:
-        top = jnp.maximum(top, other)
-    tops = lax.all_to_all(jnp.broadcast_to(top[:1], (size_y * size_z, LANES)), ("gy", "gz"), 0, 0)
     mine, *parts = call(
         second_kernel,
         1,

time: 112 us -> 123 us (1.098)
  blocking collectives: 38.3 us -> 22.1 us
  waiting for transfers between devices: 16.8 us -> 31.8 us
  local copies, waits for them, and re-layouts: 1.91 us -> 10.4 us
  starting transfers between devices: 29.8 us -> 33.9 us
    all_to_all x1 -> x0, blocking collectives: 16.2 us -> none  [shards(): lax.all_to_all(jnp.broadcast_to(top[:1], (size_y * size_z, LANES)), ('gy'...]
    unnamed x6 -> x28, local copies, waits for them, and re-layouts: 1.89 us -> 10.4 us
    all_to_all x0 -> x1, starting transfers between devices: none -> 7.64 us  [shards(): tops = lax.all_to_all(top, ('gx', 'gy', 'gz'), 0, 0)]
    ppermute x3, waiting for transfers between devices: 1.51 us -> 9.1 us  [ring_pair(): low = lax.ppermute(to_next, axes, list(zip(order, after)))]
    ppermute x3, waiting for transfers between devices: 0.01 us -> 5.74 us  [ring_pair(): high = lax.ppermute(to_last, axes, list(zip(after, order)))]
    all_to_all x0 -> x1, waiting for transfers between devices: none -> 3.87 us  [shards(): tops = lax.all_to_all(top, ('gx', 'gy', 'gz'), 0, 0)]
    ppermute x12 -> x9, starting transfers between devices: 18.4 us -> 14.9 us  [swap_block(): lax.ppermute(part, 'gx', [(i, i ^ k) for i in range(lax.axis_size('gx'))])]
    ppermute x12 -> x9, waiting for transfers between devices: 15.2 us -> 13.1 us  [swap_block(): lax.ppermute(part, 'gx', [(i, i ^ k) for i in range(lax.axis_size('gx'))])]
  transfers between devices with their start and end apart: 18 -> 16, of which waited for: 6 -> 9; matrix products, arithmetic and copies ran while one was open for 0% -> 0% of each run, Pallas kernels for 4% -> 3%
where the time goes in v6:
time: 123 us
  starting transfers between devices  33.9 us (28%)
  waiting for transfers between devices  31.8 us (26%)
  Pallas kernels  24.1 us (20%)
  blocking collectives  22.1 us (18%)
  local copies, waits for them, and re-layouts  10.4 us (8%)
    all_to_all x1, blocking collectives, shards(): tops = lax.all_to_all(top, ('gy', 'gz'), 0, 0)  22.1 us
    pallas_call x6, Pallas kernels, call(): pl.pallas_call(kernel, out_shape=[jax.ShapeDtypeStruct(shape, jnp.float32...  20.8 us
    ppermute x9, starting transfers between devices, swap_block(): lax.ppermute(part, 'gx', [(i, i ^ k) for i in range(lax.axis_size('gx'))])  14.9 us
    ppermute x9, waiting for transfers between devices, swap_block(): lax.ppermute(part, 'gx', [(i, i ^ k) for i in range(lax.axis_size('gx'))])  13.1 us
    unnamed x28, local copies, waits for them, and re-layouts  10.4 us
    ppermute x3, waiting for transfers between devices, ring_pair(): low = lax.ppermute(to_next, axes, list(zip(order, after)))  9.1 us
    ppermute x3, starting transfers between devices, ring_pair(): low = lax.ppermute(to_next, axes, list(zip(order, after)))  8.71 us
    all_to_all x1, starting transfers between devices, shards(): tops = lax.all_to_all(top, ('gx', 'gy', 'gz'), 0, 0)  7.64 us
  transfers between devices with their start and end apart: 16, of which 9 were waited for; matrix products, arithmetic and copies ran while one was open for 0% of the time, Pallas kernels for 3%

profile of v6, /device:TPU:1, one launch (start us, length us, event | category | flops | bytes accessed | tf_op | source)
XLA Modules:
  0.0 123.1 jit_solution(6942107569840764391)
XLA Ops:
  0.6 3.3 %shard_map.127 = (f32[456,128]{1,0:T(8,128)}, f32[456,128]{1,0:T(8,128)}, f32[456,128]{1,0:T(8,128)}, f32[456,128]{1,0:T(8,128)}, f32[4,2,4,16,128]{4,3,2,1,0:T(...) custom-call(f32[4,16,256]{2,1,0:T(8,128)} %args_0_.4, f32[4,16,256]{2,1,0:T(8,128)} %args_1_.4, ...), custom_call_target="tpu_custom_call" | custom-call | tf_op jit(solution)/shard_map/pallas_call | solution.py:666
  4.0 2.2 %collective-permute-start = (f32[456,128]{1,0:T(8,128)}, f32[456,128]{1,0:T(8,128)S(1)}, u32[]{:S(2)}, u32[]{:S(2)}) collective-permute-start(f32[456,128]{1,0:T(8,128)} %get-tuple-element.41), channel_id=1, source_target_pairs={{0,64},{64,0},{128,192},{192,128},{1,65},{65,1},{129,193},{193,129... | collective-permute-start | bytes 700424 | tf_op jit(solution)/shard_map/ppermute | solution.py:653
  6.2 2.6 %collective-permute-start.1 = (f32[456,128]{1,0:T(8,128)}, f32[456,128]{1,0:T(8,128)S(1)}, u32[]{:S(2)}, u32[]{:S(2)}) collective-permute-start(f32[456,128]{1,0:T(8,128)} %get-tuple-element.42), channel_id=1, source_target_pairs={{0,128},{64,192},{128,0},{192,64},{1,129},{65,193},{129,1},{193,65... | collective-permute-start | bytes 700424 | tf_op jit(solution)/shard_map/ppermute | solution.py:653
  8.8 1.2 collective-permute-start.3
  10.0 2.6 %collective-permute-start.4 = (f32[4,16,128]{2,1,0:T(8,128)}, f32[4,16,128]{2,1,0:T(8,128)S(1)}, u32[]{:S(2)}, u32[]{:S(2)}) collective-permute-start(f32[4,16,128]{2,1,0:T(8,128)} %get-tuple-element.46), channel_id=1, source_target_pairs={{1,0},{2,1},{3,2},{4,3},{5,4},{6,5},{7,6},{0,7},{9,8},{10,9},{11,1... | collective-permute-start | bytes 98312 | tf_op jit(solution)/shard_map/ppermute | solution.py:648
  12.6 1.5 %collective-permute-done.3.from_below = f32[4,16,128]{2,1,0:T(8,128)S(1)} collective-permute-done((f32[4,16,128]{2,1,0:T(8,128)}, f32[4,16,128]{2,1,0:T(8,128)S(1)}, u32[]{:S(2)}, u32[]{:S(2)}) %collective-permute-start.3) | collective-permute-done | bytes 32800 | tf_op jit(solution)/shard_map/ppermute | solution.py:647
  14.2 0.9 copy-done
  15.3 3.8 %collective-permute-start.6 = (f32[2,4,16,128]{3,2,1,0:T(8,128)S(1)}, f32[2,4,16,128]{3,2,1,0:T(8,128)S(1)}, u32[]{:S(2)}, u32[]{:S(2)}) collective-permute-start(f32[2,4,16,128]{3,2,1,0:T(8,128)S(1)} %get-tuple-element.49), channel_id=1, source_target_pairs={{0,128},{64,192},{128,0},{192,64},{1,129},{65,193},{129,1},{193,65... | collective-permute-start | bytes 196616 | tf_op jit(solution)/shard_map/ppermute | solution.py:653
  19.1 2.2 %collective-permute-start.7 = (f32[2,4,16,128]{3,2,1,0:T(8,128)S(1)}, f32[2,4,16,128]{3,2,1,0:T(8,128)S(1)}, u32[]{:S(2)}, u32[]{:S(2)}) collective-permute-start(f32[2,4,16,128]{3,2,1,0:T(8,128)S(1)} %get-tuple-element.50), channel_id=1, source_target_pairs={{0,192},{64,128},{128,64},{192,0},{1,193},{65,129},{129,65},{193,1... | collective-permute-start | bytes 196616 | tf_op jit(solution)/shard_map/ppermute | solution.py:653
  21.5 3.4 %collective-permute-done.7.z3 = f32[2,4,16,128]{3,2,1,0:T(8,128)S(1)} collective-permute-done((f32[2,4,16,128]{3,2,1,0:T(8,128)S(1)}, f32[2,4,16,128]{3,2,1,0:T(8,128)S(1)}, u32[]{:S(2)}, u32[]{:S(2)}) %collective-permute-start.7) | collective-permute-done | bytes 65568 | tf_op jit(solution)/shard_map/ppermute | solution.py:653
  24.9 0.9 copy-done.1
  26.2 5.6 %collective-permute-start.8 = (f32[72,8,128]{2,1,0:T(8,128)S(1)}, f32[72,8,128]{2,1,0:T(8,128)S(1)}, u32[]{:S(2)}, u32[]{:S(2)}) collective-permute-start(f32[72,8,128]{2,1,0:T(8,128)S(1)} %get-tuple-element.54), channel_id=1, source_target_pairs={{0,8},{8,16},{16,24},{24,32},{32,40},{40,48},{48,56},{56,0},{1,9},... | collective-permute-start | bytes 884744 | tf_op jit(solution)/shard_map/ppermute | solution.py:647
  31.8 22.1 %all_to_all.23 = f32[64,1,128]{2,1,0:T(1,128)S(1)} all-to-all(f32[64,1,128]{2,1,0:T(1,128)S(1)} %bitcast.9), channel_id=1, replica_groups=mesh['gx'=4,'gy'=8,'gz'=8] {'gy','gz'}, dimensions={0} | all-to-all | bytes 65536 | tf_op jit(solution)/shard_map/all_to_all | solution.py:694
  53.9 6.2 %shard_map.130 = (f32[4,16,16,128]{3,2,1,0:T(8,128)S(1)}, f32[9,16,24,128]{3,2,1,0:T(8,128)S(1)}, f32[15,24,128]{2,1,0:T(8,128)S(1)}, f32[16,24,128]{2,1,0:T(8,1...) custom-call(f32[2]{0:T(128)S(1)} %copy-done.10, ...), custom_call_target="tpu_custom_call" | custom-call | bytes 3600000 | tf_op jit(solution)/shard_map/pallas_call | solution.py:634
  62.8 7.6 %all-to-all-start.1 = ((f32[256,1,128]{2,1,0:T(1,128)}), f32[256,1,128]{2,1,0:T(1,128)}, u32[]{:S(2)}, u32[]{:S(2)}) async-start(f32[256,1,128]{2,1,0:T(1,128)} %bitcast.4), calls=%async_computation.1 | async-start | bytes 262144 | tf_op jit(solution)/shard_map/all_to_all | solution.py:726
  70.5 0.9 copy-done.5
  71.4 0.9 copy-done.7
  72.3 0.9 copy-done.9
  73.2 4.2 %shard_map.131 = (f32[9,16,16,128]{3,2,1,0:T(8,128)S(1)}, f32[13,8,8,128]{3,2,1,0:T(8,128)S(1)}, f32[13,8,8,128]{3,2,1,0:T(8,128)S(1)}) custom-call(f32[4,16,16,128]{3,2,1,0:T(8,128)S(1)} %get-tuple-element.57.lead.own_lead, f32[9,16,24,128]{3,2,1,0:T(8,128)S(1)} %get-tuple-element.58.rest, f32[15,24,128]{2,1,0:T(8,128)S(1)} %copy-done.7, ...), custom_call_target="tpu_custom_call" | custom-call | bytes 72000000 | tf_op jit(solution)/shard_map/pallas_call | solution.py:634
  78.1 0.8 copy-done.13
  78.9 3.9 %all-to-all-done.1 = f32[256,1,128]{2,1,0:T(1,128)} async-done(((f32[256,1,128]{2,1,0:T(1,128)}), f32[256,1,128]{2,1,0:T(1,128)}, u32[]{:S(2)}, u32[]{:S(2)}) %all-to-all-start.1) | async-done | bytes 131104 | tf_op jit(solution)/shard_map/all_to_all | solution.py:726
  82.8 1.9 %collective-permute-start.10 = (f32[13,8,8,128]{3,2,1,0:T(8,128)}, f32[13,8,8,128]{3,2,1,0:T(8,128)S(1)}, u32[]{:S(2)}, u32[]{:S(2)}) collective-permute-start(f32[13,8,8,128]{3,2,1,0:T(8,128)} %copy-done.13), channel_id=1, source_target_pairs={{0,8},{8,16},{16,24},{24,32},{32,40},{40,48},{48,56},{56,0},{1,9},... | collective-permute-start | bytes 1277960 | tf_op jit(solution)/shard_map/ppermute | solution.py:647
  84.7 7.6 %collective-permute-done.10.low = f32[13,8,8,128]{3,2,1,0:T(8,128)S(1)} collective-permute-done((f32[13,8,8,128]{3,2,1,0:T(8,128)}, f32[13,8,8,128]{3,2,1,0:T(8,128)S(1)}, u32[]{:S(2)}, u32[]{:S(2)}) %collective-permute-start.10) | collective-permute-done | bytes 426016 | tf_op jit(solution)/shard_map/ppermute | solution.py:647
  92.3 5.7 %collective-permute-done.11.high = f32[13,8,8,128]{3,2,1,0:T(8,128)S(1)} collective-permute-done((f32[13,8,8,128]{3,2,1,0:T(8,128)}, f32[13,8,8,128]{3,2,1,0:T(8,128)S(1)}, u32[]{:S(2)}, u32[]{:S(2)}) %collective-permute-start.11) | collective-permute-done | bytes 426016 | tf_op jit(solution)/shard_map/ppermute | solution.py:648
  98.1 0.9 copy-done.3
  99.6 8.9 %shard_map.132 = (f32[13,2,16,128]{3,2,1,0:T(8,128)S(1)}, f32[13,2,16,128]{3,2,1,0:T(8,128)S(1)}, f32[13,2,16,128]{3,2,1,0:T(8,128)S(1)}, f32[13,2,16,128]{3,2,1,0:T(8,128)S(1)}) custom-call(f32[2]{0:T(128)S(1)} %copy-done.11, f32[256,128]{1,0:T(8,128)} %bitcast.5.tops, f32[4,16,16,128]{3,2,1,0:T(8,128)S(1)} %get-tuple-element.57.lead.own_lead, ...), custom_call_target="tpu_custom_call" | custom-call | bytes 3600000 | tf_op jit(solution)/shard_map/pallas_call | solution.py:634
  108.7 1.5 %collective-permute-start.13 = (f32[13,2,16,128]{3,2,1,0:T(8,128)S(1)}, f32[13,2,16,128]{3,2,1,0:T(8,128)S(1)}, u32[]{:S(2)}, u32[]{:S(2)}) collective-permute-start(f32[13,2,16,128]{3,2,1,0:T(8,128)S(1)} %get-tuple-element.72), channel_id=1, source_target_pairs={{0,128},{64,192},{128,0},{192,64},{1,129},{65,193},{129,1},{193,65... | collective-permute-start | bytes 638984 | tf_op jit(solution)/shard_map/ppermute | solution.py:653
  110.2 2.3 %collective-permute-start.14 = (f32[13,2,16,128]{3,2,1,0:T(8,128)S(1)}, f32[13,2,16,128]{3,2,1,0:T(8,128)S(1)}, u32[]{:S(2)}, u32[]{:S(2)}) collective-permute-start(f32[13,2,16,128]{3,2,1,0:T(8,128)S(1)} %get-tuple-element.73), channel_id=1, source_target_pairs={{0,192},{64,128},{128,64},{192,0},{1,193},{65,129},{129,65},{193,1... | collective-permute-start | bytes 638984 | tf_op jit(solution)/shard_map/ppermute | solution.py:653
  112.5 3.2 %collective-permute-done.12.from1 = f32[13,2,16,128]{3,2,1,0:T(8,128)S(1)} collective-permute-done((f32[13,2,16,128]{3,2,1,0:T(8,128)S(1)}, f32[13,2,16,128]{3,2,1,0:T(8,128)S(1)}, u32[]{:S(2)}, u32[]{:S(2)}) %collective-permute-start.12) | collective-permute-done | bytes 213024 | tf_op jit(solution)/shard_map/ppermute | solution.py:653
  115.7 4.0 %collective-permute-done.13.from2 = f32[13,2,16,128]{3,2,1,0:T(8,128)S(1)} collective-permute-done((f32[13,2,16,128]{3,2,1,0:T(8,128)S(1)}, f32[13,2,16,128]{3,2,1,0:T(8,128)S(1)}, u32[]{:S(2)}, u32[]{:S(2)}) %collective-permute-start.13) | collective-permute-done | bytes 213024 | tf_op jit(solution)/shard_map/ppermute | solution.py:653
  119.7 2.3 %collective-permute-done.14.from3 = f32[13,2,16,128]{3,2,1,0:T(8,128)S(1)} collective-permute-done((f32[13,2,16,128]{3,2,1,0:T(8,128)S(1)}, f32[13,2,16,128]{3,2,1,0:T(8,128)S(1)}, u32[]{:S(2)}, u32[]{:S(2)}) %collective-permute-start.14) | collective-permute-done | bytes 213024 | tf_op jit(solution)/shard_map/ppermute | solution.py:653
  122.0 1.1 shard_map.133
  (36 shorter events, 4.9 us)
Async XLA Ops:
  0.6 53.3 %copy-start.10 = (f32[2]{0:T(128)S(1)}, f32[2]{0:T(128)}, u32[]{:S(2)}) copy-start(f32[2]{0:T(128)} %timestep.3) | copy-start | bytes 28
  4.0 20.9 %collective-permute-start = (f32[456,128]{1,0:T(8,128)}, f32[456,128]{1,0:T(8,128)S(1)}, u32[]{:S(2)}, u32[]{:S(2)}) collective-permute-start(f32[456,128]{1,0:T(8,128)} %get-tuple-element.41), channel_id=1, source_target_pairs={{0,64},{64,0},{128,192},{192,128},{1,65},{65,1},{129,193},{193,129... | collective-permute-start | bytes 700424 | tf_op jit(solution)/shard_map/ppermute | solution.py:653
  6.2 18.7 %collective-permute-start.1 = (f32[456,128]{1,0:T(8,128)}, f32[456,128]{1,0:T(8,128)S(1)}, u32[]{:S(2)}, u32[]{:S(2)}) collective-permute-start(f32[456,128]{1,0:T(8,128)} %get-tuple-element.42), channel_id=1, source_target_pairs={{0,128},{64,192},{128,0},{192,64},{1,129},{65,193},{129,1},{193,65... | collective-permute-start | bytes 700424 | tf_op jit(solution)/shard_map/ppermute | solution.py:653
  8.8 16.1 %collective-permute-start.2 = (f32[456,128]{1,0:T(8,128)}, f32[456,128]{1,0:T(8,128)S(1)}, u32[]{:S(2)}, u32[]{:S(2)}) collective-permute-start(f32[456,128]{1,0:T(8,128)} %get-tuple-element.43), channel_id=1, source_target_pairs={{0,192},{64,128},{128,64},{192,0},{1,193},{65,129},{129,65},{193,1... | collective-permute-start | bytes 700424 | tf_op jit(solution)/shard_map/ppermute | solution.py:653
  8.8 5.3 %collective-permute-start.3 = (f32[4,16,128]{2,1,0:T(8,128)}, f32[4,16,128]{2,1,0:T(8,128)S(1)}, u32[]{:S(2)}, u32[]{:S(2)}) collective-permute-start(f32[4,16,128]{2,1,0:T(8,128)} %get-tuple-element.45), channel_id=1, source_target_pairs={{0,1},{1,2},{2,3},{3,4},{4,5},{5,6},{6,7},{7,0},{8,9},{9,10},{10,1... | collective-permute-start | bytes 98312 | tf_op jit(solution)/shard_map/ppermute | solution.py:647
  10.0 4.1 %collective-permute-start.4 = (f32[4,16,128]{2,1,0:T(8,128)}, f32[4,16,128]{2,1,0:T(8,128)S(1)}, u32[]{:S(2)}, u32[]{:S(2)}) collective-permute-start(f32[4,16,128]{2,1,0:T(8,128)} %get-tuple-element.46), channel_id=1, source_target_pairs={{1,0},{2,1},{3,2},{4,3},{5,4},{6,5},{7,6},{0,7},{9,8},{10,9},{11,1... | collective-permute-start | bytes 98312 | tf_op jit(solution)/shard_map/ppermute | solution.py:648
  14.2 1.0 copy-start
  15.1 3.9 %collective-permute-start.5 = (f32[2,4,16,128]{3,2,1,0:T(8,128)S(1)}, f32[2,4,16,128]{3,2,1,0:T(8,128)S(1)}, u32[]{:S(2)}, u32[]{:S(2)}) collective-permute-start(f32[2,4,16,128]{3,2,1,0:T(8,128)S(1)} %get-tuple-element.48), channel_id=1, source_target_pairs={{0,64},{64,0},{128,192},{192,128},{1,65},{65,1},{129,193},{193,129... | collective-permute-start | bytes 196616 | tf_op jit(solution)/shard_map/ppermute | solution.py:653
  15.3 6.2 %collective-permute-start.6 = (f32[2,4,16,128]{3,2,1,0:T(8,128)S(1)}, f32[2,4,16,128]{3,2,1,0:T(8,128)S(1)}, u32[]{:S(2)}, u32[]{:S(2)}) collective-permute-start(f32[2,4,16,128]{3,2,1,0:T(8,128)S(1)} %get-tuple-element.49), channel_id=1, source_target_pairs={{0,128},{64,192},{128,0},{192,64},{1,129},{65,193},{129,1},{193,65... | collective-permute-start | bytes 196616 | tf_op jit(solution)/shard_map/ppermute | solution.py:653
  19.1 5.8 %collective-permute-start.7 = (f32[2,4,16,128]{3,2,1,0:T(8,128)S(1)}, f32[2,4,16,128]{3,2,1,0:T(8,128)S(1)}, u32[]{:S(2)}, u32[]{:S(2)}) collective-permute-start(f32[2,4,16,128]{3,2,1,0:T(8,128)S(1)} %get-tuple-element.50), channel_id=1, source_target_pairs={{0,192},{64,128},{128,64},{192,0},{1,193},{65,129},{129,65},{193,1... | collective-permute-start | bytes 196616 | tf_op jit(solution)/shard_map/ppermute | solution.py:653
  24.9 0.9 copy-start.1
  26.2 27.7 %collective-permute-start.8 = (f32[72,8,128]{2,1,0:T(8,128)S(1)}, f32[72,8,128]{2,1,0:T(8,128)S(1)}, u32[]{:S(2)}, u32[]{:S(2)}) collective-permute-start(f32[72,8,128]{2,1,0:T(8,128)S(1)} %get-tuple-element.54), channel_id=1, source_target_pairs={{0,8},{8,16},{16,24},{24,32},{32,40},{40,48},{48,56},{56,0},{1,9},... | collective-permute-start | bytes 884744 | tf_op jit(solution)/shard_map/ppermute | solution.py:647
  31.8 22.1 %collective-permute-start.9 = (f32[72,8,128]{2,1,0:T(8,128)S(1)}, f32[72,8,128]{2,1,0:T(8,128)S(1)}, u32[]{:S(2)}, u32[]{:S(2)}) collective-permute-start(f32[72,8,128]{2,1,0:T(8,128)S(1)} %get-tuple-element.55), channel_id=1, source_target_pairs={{8,0},{16,8},{24,16},{32,24},{40,32},{48,40},{56,48},{0,56},{9,1},... | collective-permute-start | bytes 884744 | tf_op jit(solution)/shard_map/ppermute | solution.py:648
  60.1 0.7 copy-start.2
  60.8 0.7 copy-start.4
  61.5 0.7 copy-start.6
  62.2 0.6 copy-start.8
  62.8 20.0 %all-to-all-start.1 = ((f32[256,1,128]{2,1,0:T(1,128)}), f32[256,1,128]{2,1,0:T(1,128)}, u32[]{:S(2)}, u32[]{:S(2)}) async-start(f32[256,1,128]{2,1,0:T(1,128)} %bitcast.4), calls=%async_computation.1 | async-start | bytes 262144 | tf_op jit(solution)/shard_map/all_to_all | solution.py:726
  70.5 0.9 copy-start.5
  71.4 0.9 copy-start.7
  72.3 0.9 copy-start.9
  77.4 0.8 copy-start.12
  78.1 0.8 copy-start.13
  82.8 9.5 %collective-permute-start.10 = (f32[13,8,8,128]{3,2,1,0:T(8,128)}, f32[13,8,8,128]{3,2,1,0:T(8,128)S(1)}, u32[]{:S(2)}, u32[]{:S(2)}) collective-permute-start(f32[13,8,8,128]{3,2,1,0:T(8,128)} %copy-done.13), channel_id=1, source_target_pairs={{0,8},{8,16},{16,24},{24,32},{32,40},{40,48},{48,56},{56,0},{1,9},... | collective-permute-start | bytes 1277960 | tf_op jit(solution)/shard_map/ppermute | solution.py:647
  84.7 13.3 %collective-permute-start.11 = (f32[13,8,8,128]{3,2,1,0:T(8,128)}, f32[13,8,8,128]{3,2,1,0:T(8,128)S(1)}, u32[]{:S(2)}, u32[]{:S(2)}) collective-permute-start(f32[13,8,8,128]{3,2,1,0:T(8,128)} %copy-done.12), channel_id=1, source_target_pairs={{8,0},{16,8},{24,16},{32,24},{40,32},{48,40},{56,48},{0,56},{9,1},... | collective-permute-start | bytes 1277960 | tf_op jit(solution)/shard_map/ppermute | solution.py:648
  98.1 0.9 copy-start.3
  99.0 0.7 copy-start.11
  108.6 7.1 %collective-permute-start.12 = (f32[13,2,16,128]{3,2,1,0:T(8,128)S(1)}, f32[13,2,16,128]{3,2,1,0:T(8,128)S(1)}, u32[]{:S(2)}, u32[]{:S(2)}) collective-permute-start(f32[13,2,16,128]{3,2,1,0:T(8,128)S(1)} %get-tuple-element.71), channel_id=1, source_target_pairs={{0,64},{64,0},{128,192},{192,128},{1,65},{65,1},{129,193},{193,129... | collective-permute-start | bytes 638984 | tf_op jit(solution)/shard_map/ppermute | solution.py:653
  108.7 11.0 %collective-permute-start.13 = (f32[13,2,16,128]{3,2,1,0:T(8,128)S(1)}, f32[13,2,16,128]{3,2,1,0:T(8,128)S(1)}, u32[]{:S(2)}, u32[]{:S(2)}) collective-permute-start(f32[13,2,16,128]{3,2,1,0:T(8,128)S(1)} %get-tuple-element.72), channel_id=1, source_target_pairs={{0,128},{64,192},{128,0},{192,64},{1,129},{65,193},{129,1},{193,65... | collective-permute-start | bytes 638984 | tf_op jit(solution)/shard_map/ppermute | solution.py:653
  110.2 11.8 %collective-permute-start.14 = (f32[13,2,16,128]{3,2,1,0:T(8,128)S(1)}, f32[13,2,16,128]{3,2,1,0:T(8,128)S(1)}, u32[]{:S(2)}, u32[]{:S(2)}) collective-permute-start(f32[13,2,16,128]{3,2,1,0:T(8,128)S(1)} %get-tuple-element.73), channel_id=1, source_target_pairs={{0,192},{64,128},{128,64},{192,0},{1,193},{65,129},{129,65},{193,1... | collective-permute-start | bytes 638984 | tf_op jit(solution)/shard_map/ppermute | solution.py:653
